TPU v7x, 256 devices: a whole 4x4x8 slice. The times are simulated.
256 devices in a mesh: tgt: 8 (over z_lo, core), sup: 32 (over z_hi, x, y).
Axes of the slice: x: 4, y: 4, z: 8 (z_hi: 2, z_lo: 4; z = z_hi * 4 + z_lo), core: 2. Of those that a mesh axis runs over, the one named last changes fastest.
Arguments:
- image_pool: bfloat16 [16384, 3072], P(('tgt', 'sup')), may hold values from -1 to 2
- target_index: int32 [256], replicated, may hold values from 0 to 16383, as said below
- labels: int32 [256], P('tgt'), may hold values from 0 to 1023
- support: float32 [128, 3, 1024], P('sup'), may hold values from -1 to 2
- ridge_coef: float32 [128, 1024], P('sup'), may hold values from -1 to 1
Outputs:
- residual: float32 [256, 1024], P('tgt', 'sup')
- support_grad: float32 [128, 3, 1024], P('sup')
Inputs may be any that keep to these rules, and one draw needn't show every extreme that they name: `target_index`: any row of the pool; the first of each group's 32 targets lies in the pool rows of the devices half the tgt axis away.
All inputs are finite; a program needn't handle non-finite values.
Results may differ from a plain program's by a relative error of at most 0.0003.
Values may be sent and summed in bfloat16 or wider, within the bound.
No kernel may reach another device: no remote copies, remote signals or barrier semaphores. Data moves between devices by JAX's collectives and lax.ppermute only.
A program may use at most 64 MiB of HBM per device.

v0:
```python
import math

import jax
import jax.numpy as jnp
from jax import lax
from jax.sharding import PartitionSpec as P

SIDE = 32
CHAN = 3
LAYERS = 4


WEIGHT_VAR = 2.0
BIAS_VAR = 0.1


def cut_along(x, dim, devices):
    lengths = x.shape
    parts = x.reshape(*lengths[:dim], devices, lengths[dim] // devices, *lengths[dim + 1 :])
    return jnp.moveaxis(parts, dim, 0)


def sent_and_summed(x, axis, dim):
    parts = cut_along(x, dim, lax.axis_size(axis))
    arrived = lax.all_to_all(parts, axis, split_axis=0, concat_axis=0, tiled=True)
    return arrived.sum(axis=0)


def sent_to_all(x, axis):
    devices = lax.axis_size(axis)
    return lax.all_to_all(jnp.broadcast_to(x[None], (devices, *x.shape)), axis, 0, 0, tiled=True)


def laid_out(parts, dim):
    parts = jnp.moveaxis(parts, 0, dim)
    lengths = parts.shape
    return parts.reshape(*lengths[:dim], lengths[dim] * lengths[dim + 1], *lengths[dim + 2 :])


def gather_directly(x, axis, dim):
    parts = sent_to_all(x, axis)
    return laid_out(parts, dim)


def over_copies(x, axis):
    everything = sent_to_all(x, axis)
    return jnp.sum(everything, axis=0)


def box_sum(values_map):
    column = jnp.arange(SIDE * SIDE) % SIDE
    zero_col = jnp.zeros(values_map.shape[:-1] + (1,), values_map.dtype)
    from_left = jnp.concatenate([zero_col, values_map[..., :-1]], -1)
    from_right = jnp.concatenate([values_map[..., 1:], zero_col], -1)
    row_sum = (
        values_map
        + jnp.where(column > 0, from_left, 0.0)
        + jnp.where(column < SIDE - 1, from_right, 0.0)
    )
    zero_row = jnp.zeros(values_map.shape[:-1] + (SIDE,), values_map.dtype)
    from_above = jnp.concatenate([zero_row, row_sum[..., :-SIDE]], -1)
    from_below = jnp.concatenate([row_sum[..., SIDE:], zero_row], -1)
    return (row_sum + from_above + from_below) / 9.0


def self_maps(pixels):
    current = jnp.sum(pixels * pixels, axis=1) / 3.0
    variances = []
    for depth in range(LAYERS):
        variance = WEIGHT_VAR * box_sum(current) + BIAS_VAR
        variances.append(variance)
        current = 2.0 / math.pi * jnp.arcsin(2.0 * variance / (1.0 + 2.0 * variance))
    return variances


def cross_layer(current, target_var, support_var):
    covariance = WEIGHT_VAR * box_sum(current) + BIAS_VAR
    denominator = jnp.sqrt(
        (1.0 + 2.0 * target_var)[:, None, :] * (1.0 + 2.0 * support_var)[None, :, :]
    )
    return 2.0 / math.pi * jnp.arcsin(2.0 * covariance / denominator)


def kernel_rows(targets, support, layer_step):
    target_vars = self_maps(targets)
    support_vars = self_maps(support)
    current = jnp.einsum("icp,jcp->ijp", targets, support, precision=lax.Precision.HIGHEST) / 3.0
    for depth in range(LAYERS):
        current = layer_step(current, target_vars[depth], support_vars[depth])
    return jnp.mean(current, axis=-1)


def local(image_pool, target_index, labels, support, ridge_coef):
    pool_rows = image_pool.shape[0]
    tgt_dev = labels.shape[0]
    flat_rank = lax.axis_index("tgt") * lax.axis_size("sup") + lax.axis_index("sup")
    owned_ids = flat_rank * pool_rows + jnp.arange(pool_rows, dtype=jnp.int32)
    selector = (target_index[:, None] == owned_ids[None, :]).astype(jnp.bfloat16)
    picked = jnp.dot(selector, image_pool, preferred_element_type=jnp.float32)
    every_target = lax.psum(picked, ("tgt", "sup"))
    group_pixels = lax.dynamic_slice_in_dim(
        every_target, lax.axis_index("tgt") * tgt_dev, tgt_dev, 0
    )
    targets = group_pixels.reshape(tgt_dev, CHAN, -1)
    layer_step = jax.checkpoint(cross_layer)
    kernel_block, pullback = jax.vjp(
        lambda points: kernel_rows(targets, points, layer_step), support
    )
    partial_value = jnp.dot(
        kernel_block,
        ridge_coef,
        precision=lax.Precision.HIGHEST,
        preferred_element_type=jnp.float32,
    )
    n_classes = ridge_coef.shape[1]
    per_owner = n_classes // lax.axis_size("sup")
    mine_pred = sent_and_summed(partial_value, "sup", 1)
    class_start = lax.axis_index("sup") * per_owner
    target_hot = (
        labels[:, None] == class_start + jnp.arange(per_owner, dtype=jnp.int32)[None, :]
    ).astype(jnp.float32)
    residual = mine_pred - target_hot
    full_residual = gather_directly(residual, "sup", 1)
    loss_scale = float(SIDE * SIDE) / tgt_dev
    kernel_grad = loss_scale * jnp.dot(
        full_residual,
        ridge_coef.T,
        precision=lax.Precision.HIGHEST,
        preferred_element_type=jnp.float32,
    )
    local_grad = pullback(kernel_grad)[0]
    support_grad = over_copies(local_grad, "tgt")
    return (residual, support_grad)


def solution(mesh):
    in_specs = (P(("tgt", "sup"), None), P(), P("tgt"), P("sup", None, None), P("sup", None))
    out_specs = (P("tgt", "sup"), P("sup", None, None))
    return jax.shard_map(local, mesh=mesh, in_specs=in_specs, out_specs=out_specs, check_vma=False)
```

profile of v0, /device:TPU:2, one launch (start us, length us, event | category | flops | bytes accessed | tf_op | source)
XLA Modules:
  0.0 403.1 jit_solution(7968444701514444447)
XLA Ops:
  7.2 0.9 copy-done
  8.2 2.9 fusion
  11.9 1.8 copy.74
  17.8 263.1 %all-reduce.98.cloned.1.call-done = f32[256,3072]{1,0:T(8,128)} async-done(((f32[256,3072]{1,0:T(8,128)}), f32[256,3072]{1,0:T(8,128)}) %all-reduce.98.cloned.1.call-update) | async-done | bytes 3145744 | tf_op jit(solution)/shard_map/psum | solution.py:100
  280.9 1.0 constant_dynamic-slice_fusion
  283.5 9.8 %fusion.56 = f32[1024,32,4]{1,2,0:T(4,128)} fusion(f32[32,3,1024]{0,1,2:T(4,128)S(1)} %copy.73, f32[4,3,1024]{1,0,2:T(4,128)} %copy.74), kind=kOutput, calls=%fused_computation.182 | convolution fusion | flops 4718592 | bytes 966656 | tf_op jit(solution)/shard_map/jvp(icp,jcp->ijp)/dot_general | solution.py:87
  293.3 2.0 copy.75
  297.2 1.2 add_multiply_fusion.6
  300.0 1.2 add_multiply_fusion.5
  302.8 1.2 add_multiply_fusion.4
  305.5 1.3 multiply_reduce_fusion.4
  308.6 9.9 %all-to-all-start = ((f32[32,1,1024]{2,1,0:T(1,128)}), f32[32,1,1024]{2,1,0:T(1,128)S(1)}, u32[]{:S(2)}, u32[]{:S(2)}) async-start(f32[32,1,1024]{2,1,0:T(1,128)} %reshape.84), calls=%async_computation | async-start | bytes 262144 | tf_op jit(solution)/shard_map/all_to_all | solution.py:25
  318.6 11.2 %all-to-all-done = f32[32,1,1024]{2,1,0:T(1,128)S(1)} async-done(((f32[32,1,1024]{2,1,0:T(1,128)}), f32[32,1,1024]{2,1,0:T(1,128)S(1)}, u32[]{:S(2)}, u32[]{:S(2)}) %all-to-all-start) | async-done | bytes 131104 | tf_op jit(solution)/shard_map/all_to_all | solution.py:25
  330.3 0.9 reduce
  332.5 6.6 %all-to-all-start.1 = ((f32[32,1,1024]{2,1,0:T(1,128)}), f32[32,1,1024]{2,1,0:T(1,128)S(1)}, u32[]{:S(2)}, u32[]{:S(2)}) async-start(f32[32,1,1024]{2,1,0:T(1,128)} %reshape.86), calls=%async_computation.1 | async-start | bytes 262144 | tf_op jit(solution)/shard_map/all_to_all | solution.py:31
  339.2 11.2 %all-to-all-done.1 = f32[32,1,1024]{2,1,0:T(1,128)S(1)} async-done(((f32[32,1,1024]{2,1,0:T(1,128)}), f32[32,1,1024]{2,1,0:T(1,128)S(1)}, u32[]{:S(2)}, u32[]{:S(2)}) %all-to-all-start.1) | async-done | bytes 131104 | tf_op jit(solution)/shard_map/all_to_all | solution.py:31
  350.4 1.0 reduce.1
  355.4 1.3 multiply_reduce_fusion
  358.4 1.3 multiply_reduce_fusion.1
  361.4 1.3 multiply_reduce_fusion.2
  366.0 1.8 copy.79
  367.8 9.5 %fusion.57 = f32[1024,4,3]{1,2,0:T(4,128)} fusion(f32[1024,4,32]{2,1,0:T(4,128)} %copy.79, f32[32,3,1024]{0,1,2:T(4,128)S(1)} %copy-done.3), kind=kOutput, calls=%fused_computation.183 | convolution fusion | flops 4718592 | bytes 966656 | tf_op jit(solution)/shard_map/transpose(jvp(icp,jcp->ijp))/dot_general | solution.py:87
  377.3 1.9 copy.81
  380.7 14.9 %all_to_all.15 = f32[8,4,3,1024]{3,1,2,0:T(4,128)S(1)} all-to-all(f32[8,4,3,1024]{3,1,2,0:T(4,128)S(1)} %broadcast_in_dim.242), channel_id=1, replica_groups=mesh['tgt'=8,'sup'=32] {'tgt'}, dimensions={0} | all-to-all | bytes 786432 | tf_op jit(solution)/shard_map/all_to_all | solution.py:31
  (179 shorter events, 29.1 us)
Async XLA Ops:
  7.2 1.0 copy-start
  7.2 273.7 %all-reduce.98.cloned.1.call-start = ((), (), s32[]{:S(2)}) async-start(), calls=%async_computation.3 | async-start | bytes 6291456 | tf_op jit(solution)/shard_map/psum | solution.py:100
  11.1 0.8 copy-start.4
  14.2 266.7 %copy-start.6 = (f32[4,1024]{1,0:T(4,128)}, f32[4,1024]{1,0:T(4,128)S(1)}, u32[]{:S(2)}) copy-start(f32[4,1024]{1,0:T(4,128)S(1)} %get-tuple-element.33) | copy-start | bytes 49156
  15.2 265.7 %copy-start.8 = (f32[4,1024]{1,0:T(4,128)}, f32[4,1024]{1,0:T(4,128)S(1)}, u32[]{:S(2)}) copy-start(f32[4,1024]{1,0:T(4,128)S(1)} %get-tuple-element.29) | copy-start | bytes 49156
  16.2 264.7 %copy-start.11 = (f32[4,1024]{1,0:T(4,128)}, f32[4,1024]{1,0:T(4,128)S(1)}, u32[]{:S(2)}) copy-start(f32[4,1024]{1,0:T(4,128)S(1)} %get-tuple-element.25) | copy-start | bytes 49156
  283.1 10.2 %copy-start.2 = (f32[32,3,1024]{0,1,2:T(4,128)}, f32[32,3,1024]{0,1,2:T(4,128)S(1)}, u32[]{:S(2)}) copy-start(f32[32,3,1024]{0,1,2:T(4,128)S(1)} %copy.73) | copy-start | bytes 1179652
  296.0 1.2 copy-start.18
  298.8 1.1 copy-start.17
  301.6 1.1 copy-start.16
  304.4 1.1 copy-start.15
  304.4 2.4 copy-start.21
  306.9 24.6 %copy-start.23 = (s32[32]{0:T(128)S(1)}, s32[32]{0:T(128)}, u32[]{:S(2)}) copy-start(s32[32]{0:T(128)} %param.7) | copy-start | bytes 388
  308.6 21.2 %all-to-all-start = ((f32[32,1,1024]{2,1,0:T(1,128)}), f32[32,1,1024]{2,1,0:T(1,128)S(1)}, u32[]{:S(2)}, u32[]{:S(2)}) async-start(f32[32,1,1024]{2,1,0:T(1,128)} %reshape.84), calls=%async_computation | async-start | bytes 262144 | tf_op jit(solution)/shard_map/all_to_all | solution.py:25
  331.6 7.6 %copy-start.22 = (f32[32,32]{1,0:T(8,128)}, f32[32,32]{1,0:T(8,128)S(1)}, u32[]{:S(2)}) copy-start(f32[32,32]{1,0:T(8,128)S(1)} %convert_subtract_fusion) | copy-start | bytes 12292
  332.5 17.8 %all-to-all-start.1 = ((f32[32,1,1024]{2,1,0:T(1,128)}), f32[32,1,1024]{2,1,0:T(1,128)S(1)}, u32[]{:S(2)}, u32[]{:S(2)}) async-start(f32[32,1,1024]{2,1,0:T(1,128)} %reshape.86), calls=%async_computation.1 | async-start | bytes 262144 | tf_op jit(solution)/shard_map/all_to_all | solution.py:31
  365.8 2.0 copy-start.3
  367.8 28.5 %copy-start.1 = (bf16[64,3072]{1,0:T(8,128)(2,1)S(1)}, bf16[64,3072]{1,0:T(8,128)(2,1)}, u32[]{:S(2)}) copy-start(bf16[64,3072]{1,0:T(8,128)(2,1)} %param.5) | copy-start | bytes 1179652
  377.3 1.9 copy-start.14
  377.3 2.2 copy-start.13
  377.3 2.2 copy-start.19
  377.3 2.5 copy-start.10
  377.3 2.5 copy-start.20
  377.3 3.3 copy-start.5
  (3 other events, 2.2 us)
Sparse Core Ops, SparseCore 0:
  13.4 267.4 all-reduce.97
where the time goes:
time: 406 us; the launch traced here: 403 us
  waiting for transfers between devices  286 us (70%)
  other arithmetic  25.9 us (6%)
  matrix products  23.6 us (6%)
  local copies, waits for them, and re-layouts  21.9 us (5%)
  starting transfers between devices  16.6 us (4%)
  blocking collectives  14.9 us (4%)
  between operations  14.7 us (4%)
    psum x1, waiting for transfers between devices, local(): every_target = lax.psum(picked, ('tgt', 'sup'))  263 us
    dot_general x2, matrix products, kernel_rows(): jnp.einsum('icp,jcp->ijp', targets, support, precision=lax.Precision.HIGH...  19.4 us
    all_to_all x1, blocking collectives, sent_to_all(): lax.all_to_all(jnp.broadcast_to(x[None], (devices, *x.shape)), axis, 0, 0...  14.9 us
    all_to_all x1, waiting for transfers between devices, sent_and_summed(): lax.all_to_all(parts, axis, split_axis=0, concat_axis=0, tiled=True)  11.2 us
    all_to_all x1, waiting for transfers between devices, sent_to_all(): lax.all_to_all(jnp.broadcast_to(x[None], (devices, *x.shape)), axis, 0, 0...  11.2 us
    all_to_all x1, starting transfers between devices, sent_and_summed(): lax.all_to_all(parts, axis, split_axis=0, concat_axis=0, tiled=True)  9.94 us
  transfers between devices with their start and end apart: 3, of which 3 were waited for; matrix products, arithmetic and copies ran while one was open for 1% of the time, Pallas kernels for 0%

commit v1 on v0

v1 whole, which is shorter than its diff:
```python
import functools
import math

import jax
import jax.numpy as jnp
from jax import lax
from jax.experimental import pallas as pl
from jax.experimental.pallas import tpu as pltpu
from jax.sharding import Mesh, PartitionSpec as P

SIDE = 32
CHAN = 3
LAYERS = 4
PIX = SIDE * SIDE
PLANES = 4
SUB = 8
LANES = 128
STEP_COLS = 4

WEIGHT_VAR = 2.0
BIAS_VAR = 0.1
BOX_SCALE = WEIGHT_VAR / 9.0

F32 = jnp.float32
BF16 = jnp.bfloat16
VMEM = pl.BlockSpec(memory_space=pltpu.VMEM)
SMEM = pl.BlockSpec(memory_space=pltpu.SMEM)

ASIN_Q = [
    c * 2.0 / math.pi
    for c in (
        1.5707963050,
        -0.2145988016,
        0.0889789874,
        -0.0501743046,
        0.0308918810,
        -0.0170881256,
        0.0066700901,
        -0.0012624911,
    )
]


def call(body, outs, n_in, scratch=(), smem=(), flops=0, name=None, vmem=32):
    specs = [SMEM if k in smem else VMEM for k in range(n_in)]
    many = isinstance(outs, (list, tuple))
    return pl.pallas_call(
        body,
        out_shape=outs,
        in_specs=specs,
        out_specs=[VMEM] * len(outs) if many else VMEM,
        scratch_shapes=list(scratch),
        compiler_params=pltpu.CompilerParams(vmem_limit_bytes=vmem * 2**20),
        cost_estimate=pl.CostEstimate(flops=flops, bytes_accessed=1 << 20, transcendentals=0),
        name=name,
    )


def three_parts(x):
    high = x.astype(BF16)
    rest = x - high.astype(F32)
    mid = rest.astype(BF16)
    low = (rest - mid.astype(F32)).astype(BF16)
    return high, mid, low


def dot_f32(a, b, dims):
    return lax.dot_general(a, b, (dims, ((), ())), preferred_element_type=F32, precision=lax.Precision.HIGHEST)


def dot_bf16(a, b, dims):
    return lax.dot_general(a, b, (dims, ((), ())), preferred_element_type=F32)


def pack_body(pool_ref, ridge_ref, out_ref, parts_ref):
    rows = pool_ref.shape[0]
    n_sup = ridge_ref.shape[0]
    parts_ref[...] = jnp.zeros_like(parts_ref)
    for k, part in enumerate(three_parts(ridge_ref[...])):
        parts_ref[k * n_sup : (k + 1) * n_sup, :] = part.astype(F32)
    for tile in range(PIX // LANES):
        at = tile * LANES
        pieces = [pool_ref[:, c * PIX + at : c * PIX + at + LANES] for c in range(CHAN)]
        pieces.append(parts_ref[:, at : at + LANES].astype(BF16))
        for r in range(LANES // SIDE):
            cut = [p[:, r * SIDE : (r + 1) * SIDE] for p in pieces]
            out_ref[tile * (LANES // SIDE) + r, :, :] = jnp.concatenate(cut, axis=1)


def select_body(base_ref, index_ref, rows_ref, out_ref):
    n_src, rows, _ = rows_ref.shape
    total = n_src * rows
    data = rows_ref[...].reshape(total, LANES)
    wanted = index_ref[...] - base_ref[0]
    ids = lax.broadcasted_iota(jnp.int32, (wanted.shape[0], total), 1)
    pick = jnp.where(ids == wanted, 1.0, 0.0).astype(BF16)
    got = dot_bf16(pick, data, ((1,), (0,)))
    out_ref[...] = got.astype(BF16).reshape(out_ref.shape)


def merge_body(parts_ref, out_ref):
    total = parts_ref[0].astype(F32)
    for k in range(1, parts_ref.shape[0]):
        total = total + parts_ref[k].astype(F32)
    total = total.astype(BF16)
    for k in range(out_ref.shape[0]):
        out_ref[k] = total


def steps(fn):
    def one(b, carry):
        for plane in range(PLANES):
            fn(plane, b * STEP_COLS)
        return carry

    lax.fori_loop(0, SIDE // STEP_COLS, one, 0)


def box(ref, plane, col):
    wide = pl.ds(col, STEP_COLS + 2)
    tall = ref[plane, wide] + ref[plane + 1, wide] + ref[plane + 2, wide]
    return tall[0:STEP_COLS] + tall[1 : STEP_COLS + 1] + tall[2 : STEP_COLS + 2]


def put(ref, plane, col, x):
    at = pl.ds(col + 1, STEP_COLS)
    ref[plane + 1, at] = x
    if plane == 0 or plane == PLANES - 1:
        sub = lax.broadcasted_iota(jnp.int32, x.shape, 1)
        if plane == 0:
            ref[PLANES + 1, at] = jnp.where(sub < SUB - 1, pltpu.roll(x, SUB - 1, 1), 0.0)
        else:
            ref[0, at] = jnp.where(sub > 0, pltpu.roll(x, 1, 1), 0.0)


def q_poly(a):
    acc = ASIN_Q[-1] * a + ASIN_Q[-2]
    for c in ASIN_Q[-3::-1]:
        acc = acc * a + c
    return acc


def act_of(x):
    a = jnp.abs(x)
    left = 1.0 - a
    inv = lax.rsqrt(left)
    value = 1.0 - left * inv * q_poly(a)
    return jnp.where(x < 0.0, -value, value), a, inv


def self_step(ref, plane, col):
    var = BOX_SCALE * box(ref, plane, col) + BIAS_VAR
    w = 1.0 + 2.0 * var
    inv = lax.rsqrt(w)
    return var, w, inv


def self_act(var, inv):
    x = 2.0 * var * inv * inv
    left = 1.0 - x
    return 1.0 - left * lax.rsqrt(left) * q_poly(x)


def spread(pix_ref, ones, nat_ref):
    def one(d, carry):
        nat_ref[pl.ds(d * LANES, LANES), :] = dot_bf16(pix_ref[d], ones, ((0,), (0,)))
        return carry

    lax.fori_loop(0, SIDE, one, 0, unroll=4)


def target_at(nat_ref, c, plane, col):
    cols = []
    for k in range(STEP_COLS):
        start = plane * LANES + c * SIDE + col + k
        cols.append(nat_ref[pl.ds(start, SUB, stride=PLANES * LANES), :])
    return jnp.stack(cols, axis=0)


def copies_matrix(n_tgt):
    row = lax.broadcasted_iota(jnp.int32, (n_tgt, LANES), 0)
    lane = lax.broadcasted_iota(jnp.int32, (n_tgt, LANES), 1)
    return jnp.where(lane % n_tgt == row, 1.0, 0.0).astype(BF16)


def first_maps(pix_ref, s_ref, nat_ref, self_ref, pair_ref):
    n_tgt = pix_ref.shape[1]
    spread(pix_ref, copies_matrix(n_tgt), nat_ref)

    def one(plane, col):
        own = jnp.zeros((STEP_COLS, SUB, LANES), F32)
        pair = own
        for c in range(CHAN):
            t = target_at(nat_ref, c, plane, col)
            own = own + t * t
            pair = pair + t * s_ref[c, plane, pl.ds(col, STEP_COLS)]
        put(self_ref, plane, col, own * (1.0 / CHAN))
        put(pair_ref, plane, col, pair * (1.0 / CHAN))

    steps(one)


def side_body(
    sup_ref, ridge_ref, labels_ref, rows_ref, s_ref, inv_ref, dself_ref, mine_ref, gram_ref, picked_ref, nat_ref, buf_ref, parts_ref
):
    n_sup = sup_ref.shape[0]
    n_tgt = labels_ref.shape[0]
    n_src = rows_ref.shape[0]
    for j in range(n_sup):
        total = jnp.zeros((n_src, LANES), F32)
        for k in range(3):
            total = total + rows_ref[:, k * n_sup + j, :].astype(F32)
        mine_ref[j * n_src : (j + 1) * n_src, :] = total
    lane = lax.broadcasted_iota(jnp.int32, mine_ref.shape, 1)
    mine = jnp.where(lane >= CHAN * SIDE, mine_ref[...], 0.0)
    mine_ref[...] = mine
    gram_ref[...] = dot_f32(mine, mine, ((1,), (1,)))
    hot = labels_ref[...] == lax.broadcasted_iota(jnp.int32, (n_tgt, ridge_ref.shape[1]), 1)
    hot = jnp.where(hot, 1.0, 0.0)
    hot = jnp.concatenate([hot] * n_sup, axis=0)
    picked_ref[...] = jnp.zeros_like(picked_ref)
    picked_ref[0:n_sup, :] = dot_f32(ridge_ref[...], hot, ((1,), (1,)))
    rows = parts_ref.shape[0]
    row = lax.broadcasted_iota(jnp.int32, (rows, LANES), 0)
    lane = lax.broadcasted_iota(jnp.int32, (rows, LANES), 1)
    ones = jnp.where((row < 3 * n_sup) & (row % n_sup == lane // n_tgt), 1.0, 0.0).astype(BF16)
    buf_ref[...] = jnp.zeros_like(buf_ref)
    for c in range(CHAN):
        parts_ref[...] = jnp.zeros_like(parts_ref)
        for k, part in enumerate(three_parts(sup_ref[:, c, :])):
            parts_ref[k * n_sup : (k + 1) * n_sup, :] = part.astype(F32)
        nat_ref[c * PIX : (c + 1) * PIX, :] = dot_bf16(parts_ref[...].astype(BF16), ones, ((0,), (0,)))

    def start(plane, col):
        own = jnp.zeros((STEP_COLS, SUB, LANES), F32)
        for c in range(CHAN):
            cols = []
            for k in range(STEP_COLS):
                at = c * PIX + plane * SIDE + col + k
                cols.append(nat_ref[pl.ds(at, SUB, stride=PLANES * SIDE), :])
            s = jnp.stack(cols, axis=0)
            s_ref[c, plane, pl.ds(col, STEP_COLS)] = s
            own = own + s * s
        put(buf_ref.at[0], plane, col, own * (1.0 / CHAN))

    steps(start)

    def layer(depth, carry):
        now, later = buf_ref.at[depth % 2], buf_ref.at[(depth + 1) % 2]

        def one(plane, col):
            at = pl.ds(col, STEP_COLS)
            var, w, inv = self_step(now, plane, col)
            inv_ref[depth, plane, at] = inv
            dself_ref[depth, plane, at] = (4.0 / math.pi) * inv * inv * lax.rsqrt(2.0 * w - 1.0)
            put(later, plane, col, self_act(var, inv))

        steps(one)
        return carry

    lax.fori_loop(0, LAYERS, layer, 0)


def forward_body(pix_ref, s_ref, inv_ref, gram_ref, out_ref, nat_ref, self_ref, pair_ref, acc_ref):
    self_ref[...] = jnp.zeros_like(self_ref)
    pair_ref[...] = jnp.zeros_like(pair_ref)
    first_maps(pix_ref, s_ref, nat_ref, self_ref.at[0], pair_ref.at[0])

    def layer(depth, carry):
        now, later = depth % 2, (depth + 1) % 2

        def one(plane, col):
            var, _, inv = self_step(self_ref.at[now], plane, col)
            put(self_ref.at[later], plane, col, self_act(var, inv))
            twice = (2.0 * BOX_SCALE) * box(pair_ref.at[now], plane, col) + 2.0 * BIAS_VAR
            x = twice * (inv * inv_ref[depth, plane, pl.ds(col, STEP_COLS)])
            put(pair_ref.at[later], plane, col, act_of(x)[0])

        steps(one)
        return carry

    lax.fori_loop(0, LAYERS - 1, layer, 0)
    last = LAYERS - 1
    acc_ref[...] = jnp.zeros_like(acc_ref)

    def one(plane, col):
        _, _, inv = self_step(self_ref.at[last % 2], plane, col)
        twice = (2.0 * BOX_SCALE) * box(pair_ref.at[last % 2], plane, col) + 2.0 * BIAS_VAR
        x = twice * (inv * inv_ref[last, plane, pl.ds(col, STEP_COLS)])
        acc_ref[...] += jnp.sum(act_of(x)[0], axis=0)

    steps(one)
    value = jnp.sum(acc_ref[...], axis=0, keepdims=True) * (1.0 / PIX)
    n_dst = out_ref.shape[0]
    n_sup = gram_ref.shape[0] // n_dst
    for j in range(n_sup):
        out_ref[:, j, :] = gram_ref[j * n_dst : (j + 1) * n_dst, :]
    for k in range(n_sup, out_ref.shape[1]):
        out_ref[:, k, :] = jnp.broadcast_to(value, (n_dst, LANES))


def backward_body(
    pix_ref, s_ref, inv_ref, dself_ref, high_ref, low_ref, nat_ref, self_ref, pair_ref, dcov_ref, dvar_ref, out_ref
):
    self_ref[...] = jnp.zeros_like(self_ref)
    pair_ref[...] = jnp.zeros_like(pair_ref)
    first_maps(pix_ref, s_ref, nat_ref, self_ref.at[0], pair_ref.at[0])

    def layer(depth, carry):
        now, later = depth % 2, (depth + 1) % 2

        def one(plane, col):
            at = pl.ds(col, STEP_COLS)
            var, _, inv = self_step(self_ref.at[now], plane, col)
            put(self_ref.at[later], plane, col, self_act(var, inv))
            twice = (2.0 * BOX_SCALE) * box(pair_ref.at[now], plane, col) + 2.0 * BIAS_VAR
            s_inv = inv_ref[depth, plane, at]
            both = inv * s_inv
            x = twice * both
            value, a, left = act_of(x)
            put(pair_ref.at[later], plane, col, value)
            slope = (2.0 / math.pi) * left * lax.rsqrt(1.0 + a)
            dcov_ref[depth, plane, at] = 2.0 * both * slope
            dvar_ref[depth, plane, at] = -(slope * x) * (s_inv * s_inv)

        steps(one)
        return carry

    lax.fori_loop(0, LAYERS, layer, 0)
    last = LAYERS - 1

    def seed(plane, col):
        at = pl.ds(col, STEP_COLS)
        put(pair_ref.at[last % 2], plane, col, dcov_ref[last, plane, at] * (1.0 / PIX))
        put(self_ref.at[last % 2], plane, col, dvar_ref[last, plane, at] * (1.0 / PIX))

    steps(seed)

    def back(k, carry):
        depth = last - 1 - k
        now, later = (depth + 1) % 2, depth % 2

        def one(plane, col):
            at = pl.ds(col, STEP_COLS)
            g_pair = BOX_SCALE * box(pair_ref.at[now], plane, col)
            g_self = BOX_SCALE * box(self_ref.at[now], plane, col)
            put(pair_ref.at[later], plane, col, g_pair * dcov_ref[depth, plane, at])
            g_var = g_self * dself_ref[depth, plane, at] + g_pair * dvar_ref[depth, plane, at]
            put(self_ref.at[later], plane, col, g_var)

        steps(one)
        return carry

    lax.fori_loop(0, LAYERS - 1, back, 0)

    def finish(plane, col):
        g_pair = (BOX_SCALE / CHAN) * box(pair_ref.at[0], plane, col)
        g_self = BOX_SCALE * box(self_ref.at[0], plane, col)
        for c in range(CHAN + 1):
            g = g_pair * target_at(nat_ref, c, plane, col) if c < CHAN else g_self
            for k in range(STEP_COLS):
                at = c * PIX + plane * SIDE + col + k
                out_ref[pl.ds(at, SUB, stride=PLANES * SIDE), :] = g[k]

    steps(finish)

    def split(k, carry):
        at = pl.ds(pl.multiple_of(k * 64, 64), 64)
        g = out_ref[at, :]
        high = g.astype(BF16)
        high_ref[at, :] = high
        low_ref[at, :] = (g - high.astype(F32)).astype(BF16)
        return carry

    lax.fori_loop(0, out_ref.shape[0] // 64, split, 0)


def weigh_body(scale, n_tgt, got_ref, high_ref, low_ref, picked_ref, sup_ref, out_ref):
    n_src = got_ref.shape[0]
    n_sup = sup_ref.shape[0]
    rows = got_ref.shape[1]
    gram = jnp.sum(got_ref[...], axis=0)
    values = got_ref[:, n_sup, :]
    lane = lax.broadcasted_iota(jnp.int32, (n_src, LANES), 1)
    big = jnp.concatenate([jnp.where(lane // n_tgt == j, values, 0.0) for j in range(n_sup)], axis=0)
    part = dot_f32(gram, big, ((1,), (0,)))
    part = part + pltpu.roll(part, 64, 1)
    part = part + pltpu.roll(part, 32, 1)
    row = lax.broadcasted_iota(jnp.int32, (rows, LANES), 0)
    lane = lax.broadcasted_iota(jnp.int32, (rows, LANES), 1)
    weight = jnp.where(lane // n_tgt == row, scale * (part - picked_ref[...]), 0.0)
    w_high = weight.astype(BF16)
    w_low = (weight - w_high.astype(F32)).astype(BF16)
    zero = jnp.zeros_like(w_high)
    first = jnp.concatenate([w_high, w_low], axis=0)
    second = jnp.concatenate([w_high, zero], axis=0)
    sums = []
    for c in range(CHAN + 1):
        at = slice(c * PIX, (c + 1) * PIX)
        one = dot_bf16(first, high_ref[at, :], ((1,), (1,)))
        two = dot_bf16(second, low_ref[at, :], ((1,), (1,)))
        sums.append((one[:rows] + one[rows:] + two[:rows])[:n_sup])
    per = PIX // LANES
    for c in range(CHAN):
        grad = sums[c] + (2.0 / CHAN) * sup_ref[:, c, :] * sums[CHAN]
        for k in range(per):
            out_ref[pl.ds(c * per + k, n_sup, stride=CHAN * per), :] = grad[:, k * LANES : (k + 1) * LANES]


def residual_body(n_sup, start_ref, got_ref, mine_ref, labels_ref, out_ref):
    n_src = got_ref.shape[0]
    n_tgt, classes = out_ref.shape
    values = got_ref[:, n_sup, :]
    total = jnp.zeros((n_tgt, LANES), F32)
    for j in range(n_sup):
        one = dot_f32(values, mine_ref[j * n_src : (j + 1) * n_src, :], ((0,), (0,)))
        total = total + one[j * n_tgt : (j + 1) * n_tgt, :]
    predicted = total[:, CHAN * SIDE :]
    ids = start_ref[0] + lax.broadcasted_iota(jnp.int32, (n_tgt, classes), 1)
    out_ref[...] = predicted - jnp.where(labels_ref[...] == ids, 1.0, 0.0)


def pair_sum_body(a_ref, b_ref, out_ref):
    total = a_ref[...] + b_ref[...]
    for k in range(out_ref.shape[0]):
        out_ref[k] = total


def last_sum_body(parts_ref, out_ref):
    total = parts_ref[0]
    for k in range(1, parts_ref.shape[0]):
        total = total + parts_ref[k]
    n_sup = out_ref.shape[0]
    per = PIX // LANES
    for j in range(n_sup):
        for c in range(CHAN):
            for k in range(per):
                row = (j * CHAN + c) * per + k
                out_ref[j, c : c + 1, k * LANES : (k + 1) * LANES] = total[row : row + 1, :]


def maps(*lead):
    return pltpu.VMEM((*lead, PLANES + 2, SIDE + 2, SUB, LANES), F32)


def local(image_pool, target_index, labels, support, ridge_coef):
    n_chip, n_core, n_sup_dev = lax.axis_size("chip"), lax.axis_size("core"), lax.axis_size("sup")
    n_grp = n_chip * n_core
    pool_rows = image_pool.shape[0]
    n_sup = support.shape[0]
    n_tgt = labels.shape[0]
    classes = ridge_coef.shape[1] // n_sup_dev
    group = lax.axis_index("chip") * n_core + lax.axis_index("core")
    base = (group * (n_sup_dev * pool_rows))[None].astype(jnp.int32)
    start = (lax.axis_index("sup") * classes)[None].astype(jnp.int32)
    label_col = labels[:, None]
    index_col = target_index[:, None]

    packed = call(
        pack_body,
        jax.ShapeDtypeStruct((n_sup_dev, pool_rows, LANES), BF16),
        2,
        scratch=[pltpu.VMEM((pool_rows, PIX), F32)],
        name="pack_pool",
    )(image_pool, ridge_coef)
    rows = lax.all_to_all(packed, "sup", 0, 0, tiled=True)
    chosen = call(
        select_body, jax.ShapeDtypeStruct((n_grp, n_tgt, LANES), BF16), 3, smem=(0,), name="select_targets"
    )(base, index_col, rows)
    got = lax.all_to_all(chosen, ("chip", "core"), 0, 0, tiled=True)
    side_maps = (PLANES, SIDE, SUB, LANES)
    s_maps, s_inv, dself, mine, gram, picked = call(
        side_body,
        [
            jax.ShapeDtypeStruct((CHAN, *side_maps), F32),
            jax.ShapeDtypeStruct((LAYERS, *side_maps), F32),
            jax.ShapeDtypeStruct((LAYERS, *side_maps), F32),
            jax.ShapeDtypeStruct((n_sup * n_sup_dev, LANES), F32),
            jax.ShapeDtypeStruct((n_sup * n_sup_dev, n_sup * n_sup_dev), F32),
            jax.ShapeDtypeStruct((SUB, LANES), F32),
        ],
        4,
        scratch=[pltpu.VMEM((CHAN * PIX, LANES), F32), maps(2), pltpu.VMEM((16, PIX), F32)],
        flops=10**8,
        name="support_maps",
    )(support, ridge_coef, label_col, rows)
    merged = call(
        merge_body, jax.ShapeDtypeStruct((n_sup_dev, n_tgt, LANES), BF16), 1, name="merge_targets"
    )(got)
    pixels = lax.all_to_all(merged, "sup", 0, 0, tiled=True)
    nat = pltpu.VMEM((SIDE * LANES, LANES), F32)
    sent = call(
        forward_body,
        jax.ShapeDtypeStruct((n_sup_dev, SUB, LANES), F32),
        4,
        scratch=[nat, maps(2), maps(2), pltpu.VMEM((SUB, LANES), F32)],
        flops=10**8,
        name="forward_maps",
    )(pixels, s_maps, s_inv, gram)
    arrived = lax.all_to_all(sent, "sup", 0, 0, tiled=True)
    layer_maps = pltpu.VMEM((LAYERS, *side_maps), F32)
    flat = (CHAN + 1) * PIX
    high, low = call(
        backward_body,
        [jax.ShapeDtypeStruct((flat, LANES), BF16)] * 2,
        4,
        scratch=[nat, maps(2), maps(2), layer_maps, layer_maps, pltpu.VMEM((flat, LANES), F32)],
        flops=10**10,
        name="backward_maps",
    )(pixels, s_maps, s_inv, dself)
    loss_scale = float(PIX) / n_tgt
    wide = n_sup * CHAN * PIX // LANES
    grad = call(
        functools.partial(weigh_body, loss_scale, n_tgt),
        jax.ShapeDtypeStruct((wide, LANES), F32),
        5,
        name="weigh_gradient",
    )(arrived, high, low, picked, support)
    other = lax.ppermute(grad, "core", [(k, (k + 1) % n_core) for k in range(n_core)])
    summed = call(pair_sum_body, jax.ShapeDtypeStruct((n_chip, wide, LANES), F32), 2, name="sum_cores")(grad, other)
    shares = lax.all_to_all(summed, "chip", 0, 0, tiled=True)
    residual = call(
        functools.partial(residual_body, n_sup),
        jax.ShapeDtypeStruct((n_tgt, classes), F32),
        4,
        smem=(0,),
        flops=10**7,
        name="residual",
    )(start, arrived, mine, label_col)
    support_grad = call(last_sum_body, jax.ShapeDtypeStruct(support.shape, F32), 1, name="sum_chips")(shares)
    return (residual, support_grad)


def solution(mesh):
    n_tgt, n_sup = mesh.devices.shape
    parts = Mesh(mesh.devices.reshape(n_tgt // 2, 2, n_sup), ("chip", "core", "sup"))
    tgt = ("chip", "core")
    in_specs = (P((*tgt, "sup"), None), P(), P(tgt), P("sup", None, None), P("sup", None))
    out_specs = (P(tgt, "sup"), P("sup", None, None))
    return jax.shard_map(local, mesh=parts, in_specs=in_specs, out_specs=out_specs, check_vma=False)
```

time: 406 us -> 121 us (0.30)
  waiting for transfers between devices: 286 us -> 24.9 us
  Pallas kernels: 0 us -> 34.1 us
  other arithmetic: 25.9 us -> 0 us
  matrix products: 23.6 us -> 0 us
  starting transfers between devices: 16.6 us -> 33.1 us
  between operations: 14.7 us -> 0.79 us
  local copies, waits for them, and re-layouts: 21.9 us -> 14.6 us
    psum x1 -> x0, waiting for transfers between devices: 263 us -> none  [local(): every_target = lax.psum(picked, ('tgt', 'sup'))]
    pallas_call x0 -> x10, Pallas kernels: none -> 34.1 us  [the longest x1 13.1 us: local(): call(backward_body, [jax.ShapeDtypeStruct((flat, LANES), BF16)] * 2, 4, s...]
    dot_general x5 -> x0, matrix products: 23.6 us -> none  [the longest x2 19.4 us: kernel_rows(): jnp.einsum('icp,jcp->ijp', targets, support, precision=lax.Precision.HIGH...]
    all_to_all x2 -> x4, starting transfers between devices: 16.5 us -> 33 us  [the longest x1 14.2 us: local(): rows = lax.all_to_all(packed, 'sup', 0, 0, tiled=True)]
    add x31 -> x0, other arithmetic: 8.12 us -> none  [the longest x8 3.28 us: cross_layer(): 1.0 + 2.0 * support_var]
    unnamed x53 -> x30, local copies, waits for them, and re-layouts: 6.52 us -> 13.7 us
    reduce_sum x9 -> x0, other arithmetic: 6.86 us -> none  [the longest x4 4.42 us: cross_layer(): (1.0 + 2.0 * target_var)[:, None, :] * (1.0 + 2.0 * support_var)[None, :, :]]
    mul x9 -> x0, other arithmetic: 5.35 us -> none  [the longest x3 3.66 us: cross_layer(): return 2.0 / math.pi * jnp.arcsin(2.0 * covariance / denominator)]
  transfers between devices with their start and end apart: 3 -> 5, of which waited for: 3 -> 4; matrix products, arithmetic and copies ran while one was open for 1% -> 1% of each run, Pallas kernels for 0% -> 18%
where the time goes in v1:
time: 121 us; the launch traced here: 120 us
  Pallas kernels  34.1 us (28%)
  starting transfers between devices  33.1 us (27%)
  waiting for transfers between devices  24.9 us (21%)
  local copies, waits for them, and re-layouts  14.6 us (12%)
  blocking collectives  12.9 us (11%)
    all_to_all x1, waiting for transfers between devices, local(): rows = lax.all_to_all(packed, 'sup', 0, 0, tiled=True)  14.6 us
    all_to_all x1, starting transfers between devices, local(): rows = lax.all_to_all(packed, 'sup', 0, 0, tiled=True)  14.2 us
    unnamed x30, local copies, waits for them, and re-layouts  13.7 us
    pallas_call x1, Pallas kernels, local(): call(backward_body, [jax.ShapeDtypeStruct((flat, LANES), BF16)] * 2, 4, s...  13.1 us
    all_to_all x1, blocking collectives, local(): got = lax.all_to_all(chosen, ('chip', 'core'), 0, 0, tiled=True)  12.9 us
    all_to_all x1, starting transfers between devices, local(): arrived = lax.all_to_all(sent, 'sup', 0, 0, tiled=True)  10.1 us
    pallas_call x1, Pallas kernels, local(): call(forward_body, jax.ShapeDtypeStruct((n_sup_dev, SUB, LANES), F32), 4,...  8.65 us
    pallas_call x1, Pallas kernels, local(): call(side_body, [jax.ShapeDtypeStruct((CHAN, *side_maps), F32), jax.Shape...  7 us
  transfers between devices with their start and end apart: 5, of which 4 were waited for; matrix products, arithmetic and copies ran while one was open for 1% of the time, Pallas kernels for 18%

profile of v1, /device:TPU:2, one launch (start us, length us, event | category | flops | bytes accessed | tf_op | source)
XLA Modules:
  0.0 120.3 jit_solution(825860971132283901)
XLA Ops:
  0.6 1.0 copy-done.7
  2.4 1.3 %pack_pool.1 = bf16[32,64,128]{2,1,0:T(8,128)(2,1)} custom-call(bf16[64,3072]{1,0:T(8,128)(2,1)S(1)} %copy-done.7, f32[4,1024]{1,0:T(4,128)S(1)} %copy-done.8), custom_call_target="tpu_custom_call" | custom-call | bytes 1048576 | tf_op jit(solution)/shard_map/pack_pool/pallas_call | solution.py:459
  3.6 14.2 %all-to-all-start = ((bf16[32,64,128]{2,1,0:T(8,128)(2,1)}), bf16[32,64,128]{2,1,0:T(8,128)(2,1)S(1)}, u32[]{:S(2)}, u32[]{:S(2)}) async-start(bf16[32,64,128]{2,1,0:T(8,128)(2,1)} %pack_pool.1), calls=%async_computation | async-start | bytes 1048576 | tf_op jit(solution)/shard_map/all_to_all | solution.py:466
  18.7 14.6 %all-to-all-done.rows_ref = bf16[32,64,128]{2,1,0:T(8,128)(2,1)S(1)} async-done(((bf16[32,64,128]{2,1,0:T(8,128)(2,1)}), bf16[32,64,128]{2,1,0:T(8,128)(2,1)S(1)}, u32[]{:S(2)}, u32[]{:S(2)}) %all-to-all-start) | async-done | bytes 524320 | tf_op jit(solution)/shard_map/all_to_all | solution.py:466
  33.8 12.9 %all_to_all.25.parts_ref = bf16[8,32,128]{2,1,0:T(8,128)(2,1)S(1)} all-to-all(bf16[8,32,128]{2,1,0:T(8,128)(2,1)S(1)} %select_targets.1), channel_id=1, replica_groups=mesh['chip'=4,'core'=2,'sup'=32] {'chip','core'}, dimensions={0} | all-to-all | bytes 131072 | tf_op jit(solution)/shard_map/all_to_all | solution.py:470
  47.4 5.3 %all-to-all-start.2 = ((bf16[32,32,128]{2,1,0:T(8,128)(2,1)}), bf16[32,32,128]{2,1,0:T(8,128)(2,1)S(1)}, u32[]{:S(2)}, u32[]{:S(2)}) async-start(bf16[32,32,128]{2,1,0:T(8,128)(2,1)} %merge_targets.1), calls=%async_computation.2 | async-start | bytes 524288 | tf_op jit(solution)/shard_map/all_to_all | solution.py:490
  52.9 7.0 %support_maps.1 = (f32[3,4,32,8,128]{4,3,2,1,0:T(8,128)S(1)}, f32[4,4,32,8,128]{4,3,2,1,0:T(8,128)S(1)}, f32[4,4,32,8,128]{4,3,2,1,0:T(8,128)S(1)}, f32[128,128]...) custom-call(f32[4,3,1024]{2,1,0:T(4,128)S(1)} %copy.13.sup_ref, f32[4,1024]{1,0:T(4,128)S(1)} %copy-done.9, ...), custom_call_target="tpu_custom_call" | custom-call | flops 100000000 | bytes 1048576 | tf_op jit(solution)/shard_map/support_maps/pallas_call | solution.py:472
  59.9 1.1 copy-done
  61.0 1.3 %copy-done.10 = f32[4,4,32,8,128]{4,3,2,1,0:T(8,128)} copy-done((f32[4,4,32,8,128]{4,3,2,1,0:T(8,128)}, f32[4,4,32,8,128]{4,3,2,1,0:T(8,128)S(1)}, u32[]{:S(2)}) %copy-start.10) | copy-done | bytes 2097176
  62.4 2.1 %all-to-all-done.2.pix_ref = bf16[32,32,128]{2,1,0:T(8,128)(2,1)S(1)} async-done(((bf16[32,32,128]{2,1,0:T(8,128)(2,1)}), bf16[32,32,128]{2,1,0:T(8,128)(2,1)S(1)}, u32[]{:S(2)}, u32[]{:S(2)}) %all-to-all-start.2) | async-done | bytes 262176 | tf_op jit(solution)/shard_map/all_to_all | solution.py:490
  64.5 1.4 %copy-done.1 = f32[3,4,32,8,128]{4,3,2,1,0:T(8,128)S(1)} copy-done((f32[3,4,32,8,128]{4,3,2,1,0:T(8,128)S(1)}, f32[3,4,32,8,128]{4,3,2,1,0:T(8,128)}, u32[]{:S(2)}) %copy-start.1) | copy-done | bytes 1572888
  65.9 8.6 %forward_maps.1 = f32[32,8,128]{2,1,0:T(8,128)} custom-call(bf16[32,32,128]{2,1,0:T(8,128)(2,1)S(1)} %all-to-all-done.2.pix_ref, f32[3,4,32,8,128]{4,3,2,1,0:T(8,128)S(1)} %copy-done.1, f32[4,4,32,8,128]{4,3,2,1,0:T(8,128)S(1)} %get-tuple-element.11.inv_ref, f32[128,128]{1,0:T(8,128)S(1)} %get-tuple-element.12.gram_ref), custom_call_target="tpu_custom_call" | custom-call | flops 100000000 | bytes 1048576 | tf_op jit(solution)/shard_map/forward_maps/pallas_call | solution.py:492
  74.5 10.1 %all-to-all-start.3 = ((f32[32,8,128]{2,1,0:T(8,128)}), f32[32,8,128]{2,1,0:T(8,128)S(1)}, u32[]{:S(2)}, u32[]{:S(2)}) async-start(f32[32,8,128]{2,1,0:T(8,128)} %forward_maps.1), calls=%async_computation.3 | async-start | bytes 262144 | tf_op jit(solution)/shard_map/all_to_all | solution.py:500
  84.7 1.4 %copy-done.2 = f32[3,4,32,8,128]{4,3,2,1,0:T(8,128)S(1)} copy-done((f32[3,4,32,8,128]{4,3,2,1,0:T(8,128)S(1)}, f32[3,4,32,8,128]{4,3,2,1,0:T(8,128)}, u32[]{:S(2)}) %copy-start.2) | copy-done | bytes 1572888
  86.1 1.6 %copy-done.11 = f32[4,4,32,8,128]{4,3,2,1,0:T(8,128)S(1)} copy-done((f32[4,4,32,8,128]{4,3,2,1,0:T(8,128)S(1)}, f32[4,4,32,8,128]{4,3,2,1,0:T(8,128)}, u32[]{:S(2)}) %copy-start.11) | copy-done | bytes 2097176
  87.7 13.1 %backward_maps.1 = (bf16[4096,128]{1,0:T(8,128)(2,1)S(1)}, bf16[4096,128]{1,0:T(8,128)(2,1)S(1)}) custom-call(bf16[32,32,128]{2,1,0:T(8,128)(2,1)S(1)} %all-to-all-done.2.pix_ref, f32[3,4,32,8,128]{4,3,2,1,0:T(8,128)S(1)} %copy-done.2, f32[4,4,32,8,128]{4,3,2,1,0:T(8,128)S(1)} %get-tuple-element.11.inv_ref, f32[4,4,32,8,128]{4,3,2,1,0:T(8,128)S(1)} %copy-done.11), custom_call_target="tpu_custom_call" | custom-call | flops 10000000000 | bytes 1048576 | tf_op jit(solution)/shard_map/backward_maps/pallas_call | solution.py:503
  100.8 1.0 copy-done.3
  102.7 1.2 %copy-done.4 = bf16[4096,128]{1,0:T(8,128)(2,1)S(1)} copy-done((bf16[4096,128]{1,0:T(8,128)(2,1)S(1)}, bf16[4096,128]{1,0:T(8,128)(2,1)}, u32[]{:S(2)}) %copy-start.4) | copy-done | bytes 1048600
  104.0 1.2 %copy-done.6 = bf16[4096,128]{1,0:T(8,128)(2,1)S(1)} copy-done((bf16[4096,128]{1,0:T(8,128)(2,1)S(1)}, bf16[4096,128]{1,0:T(8,128)(2,1)}, u32[]{:S(2)}) %copy-start.6) | copy-done | bytes 1048600
  105.2 1.0 weigh_gradient.1.a_ref
  106.3 1.2 %collective-permute-done.b_ref = f32[96,128]{1,0:T(8,128)S(1)} collective-permute-done((f32[96,128]{1,0:T(8,128)S(1)}, f32[96,128]{1,0:T(8,128)S(1)}, u32[]{:S(2)}, u32[]{:S(2)}) %collective-permute-start) | collective-permute-done | bytes 49184 | tf_op jit(solution)/shard_map/ppermute | solution.py:519
  108.2 3.4 %all-to-all-start.4 = ((f32[4,96,128]{2,1,0:T(8,128)}), f32[4,96,128]{2,1,0:T(8,128)S(1)}, u32[]{:S(2)}, u32[]{:S(2)}) async-start(f32[4,96,128]{2,1,0:T(8,128)} %sum_cores.1), calls=%async_computation.4 | async-start | bytes 393216 | tf_op jit(solution)/shard_map/all_to_all | solution.py:521
  111.6 1.1 residual.1
  112.7 6.9 %all-to-all-done.4.parts_ref = f32[4,96,128]{2,1,0:T(8,128)S(1)} async-done(((f32[4,96,128]{2,1,0:T(8,128)}), f32[4,96,128]{2,1,0:T(8,128)S(1)}, u32[]{:S(2)}, u32[]{:S(2)}) %all-to-all-start.4) | async-done | bytes 196640 | tf_op jit(solution)/shard_map/all_to_all | solution.py:521
  (29 shorter events, 5.3 us)
Async XLA Ops:
  0.6 1.0 copy-start.7
  1.6 0.7 copy-start.8
  2.3 50.4 %copy-start.12 = (f32[4,3,1024]{2,0,1:T(4,128)S(1)}, f32[4,3,1024]{2,0,1:T(4,128)}, u32[]{:S(2)}) copy-start(f32[4,3,1024]{2,0,1:T(4,128)} %param.8) | copy-start | bytes 147460
  2.3 50.4 %copy-start.13 = (s32[32]{0:T(128)S(1)}, s32[32]{0:T(128)}, u32[]{:S(2)}) copy-start(s32[32]{0:T(128)} %param.7) | copy-start | bytes 388
  2.3 50.5 %copy-start.9 = (f32[4,1024]{1,0:T(4,128)S(1)}, f32[4,1024]{1,0:T(4,128)}, u32[]{:S(2)}) copy-start(f32[4,1024]{1,0:T(4,128)} %ridge_ref.3) | copy-start | bytes 49156
  3.6 29.7 %all-to-all-start = ((bf16[32,64,128]{2,1,0:T(8,128)(2,1)}), bf16[32,64,128]{2,1,0:T(8,128)(2,1)S(1)}, u32[]{:S(2)}, u32[]{:S(2)}) async-start(bf16[32,64,128]{2,1,0:T(8,128)(2,1)} %pack_pool.1), calls=%async_computation | async-start | bytes 1048576 | tf_op jit(solution)/shard_map/all_to_all | solution.py:466
  47.4 17.1 %all-to-all-start.2 = ((bf16[32,32,128]{2,1,0:T(8,128)(2,1)}), bf16[32,32,128]{2,1,0:T(8,128)(2,1)S(1)}, u32[]{:S(2)}, u32[]{:S(2)}) async-start(bf16[32,32,128]{2,1,0:T(8,128)(2,1)} %merge_targets.1), calls=%async_computation.2 | async-start | bytes 524288 | tf_op jit(solution)/shard_map/all_to_all | solution.py:490
  59.9 1.1 copy-start
  61.0 1.3 %copy-start.10 = (f32[4,4,32,8,128]{4,3,2,1,0:T(8,128)}, f32[4,4,32,8,128]{4,3,2,1,0:T(8,128)S(1)}, u32[]{:S(2)}) copy-start(f32[4,4,32,8,128]{4,3,2,1,0:T(8,128)S(1)} %get-tuple-element.14.dself_ref) | copy-start | bytes 6291460
  64.5 1.4 %copy-start.1 = (f32[3,4,32,8,128]{4,3,2,1,0:T(8,128)S(1)}, f32[3,4,32,8,128]{4,3,2,1,0:T(8,128)}, u32[]{:S(2)}) copy-start(f32[3,4,32,8,128]{4,3,2,1,0:T(8,128)} %copy-done) | copy-start | bytes 4718596
  74.5 28.2 %all-to-all-start.3 = ((f32[32,8,128]{2,1,0:T(8,128)}), f32[32,8,128]{2,1,0:T(8,128)S(1)}, u32[]{:S(2)}, u32[]{:S(2)}) async-start(f32[32,8,128]{2,1,0:T(8,128)} %forward_maps.1), calls=%async_computation.3 | async-start | bytes 262144 | tf_op jit(solution)/shard_map/all_to_all | solution.py:500
  84.7 1.4 %copy-start.2 = (f32[3,4,32,8,128]{4,3,2,1,0:T(8,128)S(1)}, f32[3,4,32,8,128]{4,3,2,1,0:T(8,128)}, u32[]{:S(2)}) copy-start(f32[3,4,32,8,128]{4,3,2,1,0:T(8,128)} %copy-done) | copy-start | bytes 4718596
  86.1 1.6 %copy-start.11 = (f32[4,4,32,8,128]{4,3,2,1,0:T(8,128)S(1)}, f32[4,4,32,8,128]{4,3,2,1,0:T(8,128)}, u32[]{:S(2)}) copy-start(f32[4,4,32,8,128]{4,3,2,1,0:T(8,128)} %copy-done.10) | copy-start | bytes 6291460
  100.8 1.0 copy-start.3
  101.8 1.0 copy-start.5
  102.7 1.2 %copy-start.4 = (bf16[4096,128]{1,0:T(8,128)(2,1)S(1)}, bf16[4096,128]{1,0:T(8,128)(2,1)}, u32[]{:S(2)}) copy-start(bf16[4096,128]{1,0:T(8,128)(2,1)} %copy-done.3) | copy-start | bytes 3145732
  104.0 1.2 %copy-start.6 = (bf16[4096,128]{1,0:T(8,128)(2,1)S(1)}, bf16[4096,128]{1,0:T(8,128)(2,1)}, u32[]{:S(2)}) copy-start(bf16[4096,128]{1,0:T(8,128)(2,1)} %copy-done.5) | copy-start | bytes 3145732
  106.2 1.3 %collective-permute-start = (f32[96,128]{1,0:T(8,128)S(1)}, f32[96,128]{1,0:T(8,128)S(1)}, u32[]{:S(2)}, u32[]{:S(2)}) collective-permute-start(f32[96,128]{1,0:T(8,128)S(1)} %weigh_gradient.1.a_ref), channel_id=1, source_target_pairs={{0,32},{32,0},{1,33},{33,1},{2,34},{34,2},{3,35},{35,3},{4,36},{36... | collective-permute-start | bytes 147464 | tf_op jit(solution)/shard_map/ppermute | solution.py:519
  108.2 11.4 %all-to-all-start.4 = ((f32[4,96,128]{2,1,0:T(8,128)}), f32[4,96,128]{2,1,0:T(8,128)S(1)}, u32[]{:S(2)}, u32[]{:S(2)}) async-start(f32[4,96,128]{2,1,0:T(8,128)} %sum_cores.1), calls=%async_computation.4 | async-start | bytes 393216 | tf_op jit(solution)/shard_map/all_to_all | solution.py:521

commit v2 on v1

v2 whole, which is shorter than its diff:
```python
import functools
import math

import jax
import jax.numpy as jnp
from jax import lax
from jax.experimental import pallas as pl
from jax.experimental.pallas import tpu as pltpu
from jax.sharding import Mesh, PartitionSpec as P

SIDE = 32
CHAN = 3
LAYERS = 4
PIX = SIDE * SIDE
PLANES = 4
SUB = 8
LANES = 128
STEP_COLS = 4

WEIGHT_VAR = 2.0
BIAS_VAR = 0.1
BOX_SCALE = WEIGHT_VAR / 9.0

F32 = jnp.float32
BF16 = jnp.bfloat16
VMEM = pl.BlockSpec(memory_space=pltpu.VMEM)
SMEM = pl.BlockSpec(memory_space=pltpu.SMEM)

ASIN_Q = [
    c * 2.0 / math.pi
    for c in (
        1.5707963050,
        -0.2145988016,
        0.0889789874,
        -0.0501743046,
        0.0308918810,
        -0.0170881256,
        0.0066700901,
        -0.0012624911,
    )
]


def call(body, outs, n_in, scratch=(), smem=(), flops=0, name=None, vmem=4):
    specs = [SMEM if k in smem else VMEM for k in range(n_in)]
    many = isinstance(outs, (list, tuple))
    return pl.pallas_call(
        body,
        out_shape=outs,
        in_specs=specs,
        out_specs=[VMEM] * len(outs) if many else VMEM,
        scratch_shapes=list(scratch),
        compiler_params=pltpu.CompilerParams(vmem_limit_bytes=vmem * 2**20),
        cost_estimate=pl.CostEstimate(flops=flops, bytes_accessed=1 << 20, transcendentals=0),
        name=name,
    )


def three_parts(x):
    high = x.astype(BF16)
    rest = x - high.astype(F32)
    mid = rest.astype(BF16)
    low = (rest - mid.astype(F32)).astype(BF16)
    return high, mid, low


def dot_f32(a, b, dims):
    return lax.dot_general(a, b, (dims, ((), ())), preferred_element_type=F32, precision=lax.Precision.HIGHEST)


def dot_bf16(a, b, dims):
    return lax.dot_general(a, b, (dims, ((), ())), preferred_element_type=F32)


def pack_body(pool_ref, ridge_ref, out_ref, parts_ref):
    rows = pool_ref.shape[0]
    n_sup = ridge_ref.shape[0]
    parts_ref[...] = jnp.zeros_like(parts_ref)
    for k, part in enumerate(three_parts(ridge_ref[...])):
        parts_ref[k * n_sup : (k + 1) * n_sup, :] = part.astype(F32)
    for tile in range(PIX // LANES):
        at = tile * LANES
        pieces = [pool_ref[:, c * PIX + at : c * PIX + at + LANES] for c in range(CHAN)]
        pieces.append(parts_ref[:, at : at + LANES].astype(BF16))
        for r in range(LANES // SIDE):
            cut = [p[:, r * SIDE : (r + 1) * SIDE] for p in pieces]
            out_ref[tile * (LANES // SIDE) + r, :, :] = jnp.concatenate(cut, axis=1)


def select_body(base_ref, index_ref, rows_ref, out_ref):
    n_src, rows, _ = rows_ref.shape
    total = n_src * rows
    data = rows_ref[...].reshape(total, LANES)
    wanted = index_ref[...] - base_ref[0]
    ids = lax.broadcasted_iota(jnp.int32, (wanted.shape[0], total), 1)
    pick = jnp.where(ids == wanted, 1.0, 0.0).astype(BF16)
    got = dot_bf16(pick, data, ((1,), (0,)))
    out_ref[...] = got.astype(BF16).reshape(out_ref.shape)


def merge_body(parts_ref, out_ref):
    total = parts_ref[0].astype(F32)
    for k in range(1, parts_ref.shape[0]):
        total = total + parts_ref[k].astype(F32)
    total = total.astype(BF16)
    for k in range(out_ref.shape[0]):
        out_ref[k] = total


def steps(fn):
    def one(b, carry):
        fn(b * STEP_COLS)
        return carry

    lax.fori_loop(0, SIDE // STEP_COLS, one, 0)


def box(ref, col):
    x = ref[:, pl.ds(col, STEP_COLS + 2)]
    x = x[:, 0:STEP_COLS] + x[:, 1 : STEP_COLS + 1] + x[:, 2 : STEP_COLS + 2]
    return x[0:PLANES] + x[1 : PLANES + 1] + x[2 : PLANES + 2]


def put(ref, col, x):
    at = pl.ds(col + 1, STEP_COLS)
    ref[1 : PLANES + 1, at] = x
    sub = lax.broadcasted_iota(jnp.int32, x.shape[1:], 1)
    ref[PLANES + 1, at] = jnp.where(sub < SUB - 1, pltpu.roll(x[0], SUB - 1, 1), 0.0)
    ref[0, at] = jnp.where(sub > 0, pltpu.roll(x[PLANES - 1], 1, 1), 0.0)


def take(ref, start, step, col):
    planes = []
    for plane in range(PLANES):
        at = start + step * plane + col
        cols = [ref[pl.ds(at + k, SUB, stride=PLANES * step), :] for k in range(STEP_COLS)]
        planes.append(jnp.stack(cols, axis=0))
    return jnp.stack(planes, axis=0)


def q_poly(a):
    acc = ASIN_Q[-1] * a + ASIN_Q[-2]
    for c in ASIN_Q[-3::-1]:
        acc = acc * a + c
    return acc


def act_of(x):
    a = jnp.abs(x)
    left = 1.0 - a
    inv = lax.rsqrt(left)
    value = 1.0 - left * inv * q_poly(a)
    return jnp.where(x < 0.0, -value, value), a, inv


def self_act(var, inv):
    x = 2.0 * var * inv * inv
    left = 1.0 - x
    return 1.0 - left * lax.rsqrt(left) * q_poly(x)


def self_step(ref, col):
    var = BOX_SCALE * box(ref, col) + BIAS_VAR
    return var, lax.rsqrt(1.0 + 2.0 * var)


def spread(pix_ref, nat_ref):
    n_tgt = pix_ref.shape[1]
    row = lax.broadcasted_iota(jnp.int32, (n_tgt, LANES), 0)
    lane = lax.broadcasted_iota(jnp.int32, (n_tgt, LANES), 1)
    ones = jnp.where(lane % n_tgt == row, 1.0, 0.0).astype(BF16)

    def one(d, carry):
        nat_ref[pl.ds(d * LANES, LANES), :] = dot_bf16(pix_ref[d], ones, ((0,), (0,)))
        return carry

    lax.fori_loop(0, SIDE, one, 0, unroll=4)


def spread_support(maps_ref, n_tgt, n_sup, nat_ref):
    rows = maps_ref.shape[1]
    row = lax.broadcasted_iota(jnp.int32, (rows, LANES), 0)
    lane = lax.broadcasted_iota(jnp.int32, (rows, LANES), 1)
    ones = jnp.where((row < 3 * n_sup) & (row % n_sup == lane // n_tgt), 1.0, 0.0).astype(BF16)
    for k in range(nat_ref.shape[0] // PIX):
        nat_ref[k * PIX : (k + 1) * PIX, :] = dot_bf16(maps_ref[k], ones, ((0,), (0,)))


def take_target(nat_ref, c, col):
    return take(nat_ref, c * SIDE, LANES, col)


def take_support(nat_ref, k, col):
    return take(nat_ref, k * PIX, SIDE, col)


def first_maps(tgt_ref, sup_ref, self_ref, pair_ref):
    def one(col):
        own = pair = 0.0
        for c in range(CHAN):
            t = take_target(tgt_ref, c, col)
            own = own + t * t
            pair = pair + t * take_support(sup_ref, c, col)
        put(self_ref, col, own * (1.0 / CHAN))
        put(pair_ref, col, pair * (1.0 / CHAN))

    steps(one)


def flat_box(x):
    at = lax.broadcasted_iota(jnp.int32, x.shape, 1)
    col = at % SIDE
    left = jnp.where(col > 0, pltpu.roll(x, 1, 1), 0.0)
    right = jnp.where(col < SIDE - 1, pltpu.roll(x, PIX - 1, 1), 0.0)
    x = x + left + right
    above = jnp.where(at >= SIDE, pltpu.roll(x, SIDE, 1), 0.0)
    below = jnp.where(at < PIX - SIDE, pltpu.roll(x, PIX - SIDE, 1), 0.0)
    return x + above + below


def side_body(sup_ref, ridge_ref, labels_ref, rows_ref, maps_ref, mine_ref, gram_ref, picked_ref, parts_ref):
    n_sup = sup_ref.shape[1]
    n_tgt = labels_ref.shape[0]
    n_src = rows_ref.shape[0]
    for j in range(n_sup):
        total = jnp.zeros((n_src, LANES), F32)
        for k in range(3):
            total = total + rows_ref[:, k * n_sup + j, :].astype(F32)
        mine_ref[j * n_src : (j + 1) * n_src, :] = total
    lane = lax.broadcasted_iota(jnp.int32, mine_ref.shape, 1)
    mine = jnp.where(lane >= CHAN * SIDE, mine_ref[...], 0.0)
    mine_ref[...] = mine
    gram_ref[...] = dot_f32(mine, mine, ((1,), (1,)))
    hot = labels_ref[...] == lax.broadcasted_iota(jnp.int32, (n_tgt, ridge_ref.shape[1]), 1)
    hot = jnp.where(hot, 1.0, 0.0)
    hot = jnp.concatenate([hot] * n_sup, axis=0)
    picked_ref[...] = jnp.zeros_like(picked_ref)
    picked_ref[0:n_sup, :] = dot_f32(ridge_ref[...], hot, ((1,), (1,)))
    parts_ref[...] = jnp.zeros_like(parts_ref)

    def keep(k, x):
        for i, part in enumerate(three_parts(x)):
            parts_ref[i * n_sup : (i + 1) * n_sup, :] = part.astype(F32)
        maps_ref[k] = parts_ref[...].astype(BF16)

    current = 0.0
    for c in range(CHAN):
        s = sup_ref[c]
        keep(c, s)
        current = current + s * s
    current = current * (1.0 / CHAN)
    for depth in range(LAYERS):
        var = BOX_SCALE * flat_box(current) + BIAS_VAR
        inv = lax.rsqrt(1.0 + 2.0 * var)
        keep(CHAN + depth, inv)
        if depth < LAYERS - 1:
            keep(CHAN + LAYERS + depth, (4.0 / math.pi) * inv * inv * lax.rsqrt(1.0 + 4.0 * var))
            current = self_act(var, inv)


def forward_body(n_sup, pix_ref, maps_ref, gram_ref, out_ref, tgt_ref, sup_ref, self_a, self_b, pair_a, pair_b, acc_ref):
    for ref in (self_a, self_b, pair_a, pair_b):
        ref[...] = jnp.zeros_like(ref)
    spread(pix_ref, tgt_ref)
    spread_support(maps_ref, pix_ref.shape[1], n_sup, sup_ref)
    first_maps(tgt_ref, sup_ref, self_a, pair_a)
    acc_ref[...] = jnp.zeros_like(acc_ref)
    for depth in range(LAYERS):
        self_now, self_later = (self_a, self_b) if depth % 2 == 0 else (self_b, self_a)
        pair_now, pair_later = (pair_a, pair_b) if depth % 2 == 0 else (pair_b, pair_a)

        def one(col, depth=depth, self_now=self_now, self_later=self_later, pair_now=pair_now, pair_later=pair_later):
            var, inv = self_step(self_now, col)
            twice = (2.0 * BOX_SCALE) * box(pair_now, col) + 2.0 * BIAS_VAR
            x = twice * (inv * take_support(sup_ref, CHAN + depth, col))
            value = act_of(x)[0]
            if depth < LAYERS - 1:
                put(self_later, col, self_act(var, inv))
                put(pair_later, col, value)
            else:
                acc_ref[...] += jnp.sum(value, axis=(0, 1))

        steps(one)
    value = jnp.sum(acc_ref[...], axis=0, keepdims=True) * (1.0 / PIX)
    n_dst = out_ref.shape[0]
    for j in range(n_sup):
        out_ref[:, j, :] = gram_ref[j * n_dst : (j + 1) * n_dst, :]
    for k in range(n_sup, out_ref.shape[1]):
        out_ref[:, k, :] = jnp.broadcast_to(value, (n_dst, LANES))


def backward_body(
    n_sup,
    pix_ref,
    maps_ref,
    high_ref,
    low_ref,
    tgt_ref,
    sup_ref,
    self_a,
    self_b,
    pair_a,
    pair_b,
    dcov_ref,
    dvar_ref,
    out_ref,
):
    for ref in (self_a, self_b, pair_a, pair_b):
        ref[...] = jnp.zeros_like(ref)
    spread(pix_ref, tgt_ref)
    spread_support(maps_ref, pix_ref.shape[1], n_sup, sup_ref)
    first_maps(tgt_ref, sup_ref, self_a, pair_a)
    last = LAYERS - 1
    for depth in range(LAYERS):
        self_now, self_later = (self_a, self_b) if depth % 2 == 0 else (self_b, self_a)
        pair_now, pair_later = (pair_a, pair_b) if depth % 2 == 0 else (pair_b, pair_a)

        def one(col, depth=depth, self_now=self_now, self_later=self_later, pair_now=pair_now, pair_later=pair_later):
            at = pl.ds(col, STEP_COLS)
            var, inv = self_step(self_now, col)
            twice = (2.0 * BOX_SCALE) * box(pair_now, col) + 2.0 * BIAS_VAR
            s_inv = take_support(sup_ref, CHAN + depth, col)
            both = inv * s_inv
            x = twice * both
            value, a, left = act_of(x)
            slope = (2.0 / math.pi) * left * lax.rsqrt(1.0 + a)
            d_cov = 2.0 * both * slope
            d_var = -(slope * x) * (s_inv * s_inv)
            if depth < last:
                put(self_later, col, self_act(var, inv))
                put(pair_later, col, value)
                dcov_ref[depth, :, at] = d_cov
                dvar_ref[depth, :, at] = d_var
            else:
                put(pair_later, col, d_cov * (1.0 / PIX))
                put(self_later, col, d_var * (1.0 / PIX))

        steps(one)
    for depth in range(last - 1, -1, -1):
        self_now, self_later = (self_a, self_b) if depth % 2 == 0 else (self_b, self_a)
        pair_now, pair_later = (pair_a, pair_b) if depth % 2 == 0 else (pair_b, pair_a)

        def one(col, depth=depth, self_now=self_now, self_later=self_later, pair_now=pair_now, pair_later=pair_later):
            at = pl.ds(col, STEP_COLS)
            g_pair = BOX_SCALE * box(pair_now, col)
            g_self = BOX_SCALE * box(self_now, col)
            slope = take_support(sup_ref, CHAN + LAYERS + depth, col)
            put(pair_later, col, g_pair * dcov_ref[depth, :, at])
            put(self_later, col, g_self * slope + g_pair * dvar_ref[depth, :, at])

        steps(one)

    def finish(col):
        g_pair = (BOX_SCALE / CHAN) * box(pair_b, col)
        g_self = BOX_SCALE * box(self_b, col)
        for c in range(CHAN + 1):
            g = g_pair * take_target(tgt_ref, c, col) if c < CHAN else g_self
            for plane in range(PLANES):
                for k in range(STEP_COLS):
                    at = c * PIX + plane * SIDE + col + k
                    out_ref[pl.ds(at, SUB, stride=PLANES * SIDE), :] = g[plane, k]

    steps(finish)

    def split(k, carry):
        at = pl.ds(pl.multiple_of(k * 128, 128), 128)
        g = out_ref[at, :]
        high = g.astype(BF16)
        high_ref[at, :] = high
        low_ref[at, :] = (g - high.astype(F32)).astype(BF16)
        return carry

    lax.fori_loop(0, out_ref.shape[0] // 128, split, 0)


def weigh_body(scale, n_tgt, got_ref, high_ref, low_ref, picked_ref, sup_ref, out_ref):
    n_src = got_ref.shape[0]
    n_sup = sup_ref.shape[1]
    rows = got_ref.shape[1]
    gram = jnp.sum(got_ref[...], axis=0)
    values = got_ref[:, n_sup, :]
    lane = lax.broadcasted_iota(jnp.int32, (n_src, LANES), 1)
    big = jnp.concatenate([jnp.where(lane // n_tgt == j, values, 0.0) for j in range(n_sup)], axis=0)
    part = dot_f32(gram, big, ((1,), (0,)))
    part = part + pltpu.roll(part, 64, 1)
    part = part + pltpu.roll(part, 32, 1)
    row = lax.broadcasted_iota(jnp.int32, (rows, LANES), 0)
    lane = lax.broadcasted_iota(jnp.int32, (rows, LANES), 1)
    weight = jnp.where(lane // n_tgt == row, scale * (part - picked_ref[...]), 0.0)
    w_high = weight.astype(BF16)
    w_low = (weight - w_high.astype(F32)).astype(BF16)
    zero = jnp.zeros_like(w_high)
    first = jnp.concatenate([w_high, w_low], axis=0)
    second = jnp.concatenate([w_high, zero], axis=0)
    sums = []
    for c in range(CHAN + 1):
        at = slice(c * PIX, (c + 1) * PIX)
        one = dot_bf16(first, high_ref[at, :], ((1,), (1,)))
        two = dot_bf16(second, low_ref[at, :], ((1,), (1,)))
        sums.append((one[:rows] + one[rows:] + two[:rows])[:n_sup])
    per = PIX // LANES
    for c in range(CHAN):
        grad = sums[c] + (2.0 / CHAN) * sup_ref[c] * sums[CHAN]
        for k in range(per):
            out_ref[pl.ds(c * per + k, n_sup, stride=CHAN * per), :] = grad[:, k * LANES : (k + 1) * LANES]


def residual_body(n_sup, start_ref, got_ref, mine_ref, labels_ref, out_ref):
    n_src = got_ref.shape[0]
    n_tgt, classes = out_ref.shape
    values = got_ref[:, n_sup, :]
    total = jnp.zeros((n_tgt, LANES), F32)
    for j in range(n_sup):
        one = dot_f32(values, mine_ref[j * n_src : (j + 1) * n_src, :], ((0,), (0,)))
        total = total + one[j * n_tgt : (j + 1) * n_tgt, :]
    predicted = total[:, CHAN * SIDE :]
    ids = start_ref[0] + lax.broadcasted_iota(jnp.int32, (n_tgt, classes), 1)
    out_ref[...] = predicted - jnp.where(labels_ref[...] == ids, 1.0, 0.0)


def pair_sum_body(a_ref, b_ref, out_ref):
    total = a_ref[...] + b_ref[...]
    for k in range(out_ref.shape[0]):
        out_ref[k] = total


def last_sum_body(parts_ref, out_ref):
    total = parts_ref[0]
    for k in range(1, parts_ref.shape[0]):
        total = total + parts_ref[k]
    n_sup = out_ref.shape[1]
    per = PIX // LANES
    for j in range(n_sup):
        for c in range(CHAN):
            for k in range(per):
                row = (j * CHAN + c) * per + k
                out_ref[c, j : j + 1, k * LANES : (k + 1) * LANES] = total[row : row + 1, :]


def maps(*lead):
    return pltpu.VMEM((*lead, PLANES + 2, SIDE + 2, SUB, LANES), F32)


def local(image_pool, target_index, labels, support, ridge_coef):
    n_chip, n_core, n_sup_dev = lax.axis_size("chip"), lax.axis_size("core"), lax.axis_size("sup")
    n_grp = n_chip * n_core
    pool_rows = image_pool.shape[0]
    n_sup = support.shape[0]
    n_tgt = labels.shape[0]
    classes = ridge_coef.shape[1] // n_sup_dev
    group = lax.axis_index("chip") * n_core + lax.axis_index("core")
    base = (group * (n_sup_dev * pool_rows))[None].astype(jnp.int32)
    start = (lax.axis_index("sup") * classes)[None].astype(jnp.int32)
    label_col = labels[:, None]
    index_col = target_index[:, None]

    packed = call(
        pack_body,
        jax.ShapeDtypeStruct((n_sup_dev, pool_rows, LANES), BF16),
        2,
        scratch=[pltpu.VMEM((pool_rows, PIX), F32)],
        name="pack_pool",
    )(image_pool, ridge_coef)
    packed, index_col = lax.optimization_barrier((packed, index_col))
    rows = lax.all_to_all(packed, "sup", 0, 0, tiled=True)
    chosen = call(
        select_body, jax.ShapeDtypeStruct((n_grp, n_tgt, LANES), BF16), 3, smem=(0,), name="select_targets"
    )(base, index_col, rows)
    got = lax.all_to_all(chosen, ("chip", "core"), 0, 0, tiled=True)
    by_channel = jnp.swapaxes(support, 0, 1)
    n_maps = CHAN + 2 * LAYERS - 1
    s_maps, mine, gram, picked = call(
        side_body,
        [
            jax.ShapeDtypeStruct((n_maps, 16, PIX), BF16),
            jax.ShapeDtypeStruct((n_sup * n_sup_dev, LANES), F32),
            jax.ShapeDtypeStruct((n_sup * n_sup_dev, n_sup * n_sup_dev), F32),
            jax.ShapeDtypeStruct((SUB, LANES), F32),
        ],
        4,
        scratch=[pltpu.VMEM((16, PIX), F32)],
        flops=10**8,
        name="support_maps",
    )(by_channel, ridge_coef, label_col, rows)
    merged = call(
        merge_body, jax.ShapeDtypeStruct((n_sup_dev, n_tgt, LANES), BF16), 1, name="merge_targets"
    )(got)
    pixels = lax.all_to_all(merged, "sup", 0, 0, tiled=True)
    tgt_nat = pltpu.VMEM((SIDE * LANES, LANES), F32)
    sent = call(
        functools.partial(forward_body, n_sup),
        jax.ShapeDtypeStruct((n_sup_dev, SUB, LANES), F32),
        3,
        scratch=[tgt_nat, pltpu.VMEM(((CHAN + LAYERS) * PIX, LANES), F32), *[maps()] * 4, pltpu.VMEM((SUB, LANES), F32)],
        flops=10**8,
        name="forward_maps",
        vmem=12,
    )(pixels, s_maps, gram)
    arrived = lax.all_to_all(sent, "sup", 0, 0, tiled=True)
    layer_maps = pltpu.VMEM((LAYERS - 1, PLANES, SIDE, SUB, LANES), F32)
    flat = (CHAN + 1) * PIX
    high, low = call(
        functools.partial(backward_body, n_sup),
        [jax.ShapeDtypeStruct((flat, LANES), BF16)] * 2,
        2,
        scratch=[
            tgt_nat,
            pltpu.VMEM((n_maps * PIX, LANES), F32),
            *[maps()] * 4,
            layer_maps,
            layer_maps,
            pltpu.VMEM((flat, LANES), F32),
        ],
        flops=10**10,
        name="backward_maps",
        vmem=20,
    )(pixels, s_maps)
    loss_scale = float(PIX) / n_tgt
    wide = n_sup * CHAN * PIX // LANES
    grad = call(
        functools.partial(weigh_body, loss_scale, n_tgt),
        jax.ShapeDtypeStruct((wide, LANES), F32),
        5,
        name="weigh_gradient",
        vmem=8,
    )(arrived, high, low, picked, by_channel)
    other = lax.ppermute(grad, "core", [(k, (k + 1) % n_core) for k in range(n_core)])
    summed = call(pair_sum_body, jax.ShapeDtypeStruct((n_chip, wide, LANES), F32), 2, name="sum_cores")(grad, other)
    shares = lax.all_to_all(summed, "chip", 0, 0, tiled=True)
    residual = call(
        functools.partial(residual_body, n_sup),
        jax.ShapeDtypeStruct((n_tgt, classes), F32),
        4,
        smem=(0,),
        flops=10**7,
        name="residual",
    )(start, arrived, mine, label_col)
    total = call(last_sum_body, jax.ShapeDtypeStruct(by_channel.shape, F32), 1, name="sum_chips")(shares)
    return (residual, jnp.swapaxes(total, 0, 1))


def solution(mesh):
    n_tgt, n_sup = mesh.devices.shape
    parts = Mesh(mesh.devices.reshape(n_tgt // 2, 2, n_sup), ("chip", "core", "sup"))
    tgt = ("chip", "core")
    in_specs = (P((*tgt, "sup"), None), P(), P(tgt), P("sup", None, None), P("sup", None))
    out_specs = (P(tgt, "sup"), P("sup", None, None))
    return jax.shard_map(local, mesh=parts, in_specs=in_specs, out_specs=out_specs, check_vma=False)
```

time: 121 us -> 111 us (0.917)
  local copies, waits for them, and re-layouts: 14.6 us -> 3.22 us
  waiting for transfers between devices: 24.9 us -> 32.6 us
  starting transfers between devices: 33.1 us -> 29.6 us
  Pallas kernels: 34.1 us -> 31.5 us
    unnamed x30 -> x12, local copies, waits for them, and re-layouts: 13.7 us -> 3 us
    all_to_all x1, waiting for transfers between devices: 2.12 us -> 10 us  [local(): pixels = lax.all_to_all(merged, 'sup', 0, 0, tiled=True)]
    all_to_all x1, starting transfers between devices: 10.1 us -> 5.13 us  [local(): arrived = lax.all_to_all(sent, 'sup', 0, 0, tiled=True)]
    pallas_call x4, Pallas kernels: 28.8 us -> 26.2 us  [the longest x1 14.2 us: local(): call(functools.partial(backward_body, n_sup), [jax.ShapeDtypeStruct((flat...]
    all_to_all x1, starting transfers between devices: 3.36 us -> 4.67 us  [local(): shares = lax.all_to_all(summed, 'chip', 0, 0, tiled=True)]
  transfers between devices with their start and end apart: 5 -> 5, of which waited for: 4 -> 4; matrix products, arithmetic and copies ran while one was open for 1% -> 0% of each run, Pallas kernels for 18% -> 15%
where the time goes in v2:
time: 111 us
  waiting for transfers between devices  32.6 us (29%)
  Pallas kernels  31.5 us (28%)
  starting transfers between devices  29.6 us (27%)
  blocking collectives  12.9 us (12%)
  local copies, waits for them, and re-layouts  3.22 us (3%)
    all_to_all x1, waiting for transfers between devices, local(): rows = lax.all_to_all(packed, 'sup', 0, 0, tiled=True)  14.6 us
    all_to_all x1, starting transfers between devices, local(): rows = lax.all_to_all(packed, 'sup', 0, 0, tiled=True)  14.2 us
    pallas_call x1, Pallas kernels, local(): call(functools.partial(backward_body, n_sup), [jax.ShapeDtypeStruct((flat...  14.2 us
    all_to_all x1, blocking collectives, local(): got = lax.all_to_all(chosen, ('chip', 'core'), 0, 0, tiled=True)  12.9 us
    pallas_call x1, Pallas kernels, local(): call(functools.partial(forward_body, n_sup), jax.ShapeDtypeStruct((n_sup_...  10.4 us
    all_to_all x1, waiting for transfers between devices, local(): pixels = lax.all_to_all(merged, 'sup', 0, 0, tiled=True)  10 us
    all_to_all x1, waiting for transfers between devices, local(): shares = lax.all_to_all(summed, 'chip', 0, 0, tiled=True)  6.74 us
    all_to_all x1, starting transfers between devices, local(): pixels = lax.all_to_all(merged, 'sup', 0, 0, tiled=True)  5.45 us
  transfers between devices with their start and end apart: 5, of which 4 were waited for; matrix products, arithmetic and copies ran while one was open for 0% of the time, Pallas kernels for 15%

profile of v2, /device:TPU:2, one launch (start us, length us, event | category | flops | bytes accessed | tf_op | source)
XLA Modules:
  0.0 110.5 jit_solution(11521420319440054569)
XLA Ops:
  0.6 1.0 copy-done
  1.6 0.7 copy-done.2
  2.3 1.3 %pack_pool.1 = bf16[32,64,128]{2,1,0:T(8,128)(2,1)} custom-call(bf16[64,3072]{1,0:T(8,128)(2,1)S(1)} %copy-done, f32[4,1024]{1,0:T(4,128)S(1)} %copy-done.2), custom_call_target="tpu_custom_call" | custom-call | bytes 1048576 | tf_op jit(solution)/shard_map/pack_pool/pallas_call | solution.py:457
  3.6 14.2 %all-to-all-start = ((bf16[32,64,128]{2,1,0:T(8,128)(2,1)}), bf16[32,64,128]{2,1,0:T(8,128)(2,1)S(1)}, u32[]{:S(2)}, u32[]{:S(2)}) async-start(bf16[32,64,128]{2,1,0:T(8,128)(2,1)} %pack_pool.1), calls=%async_computation | async-start | bytes 1048576 | tf_op jit(solution)/shard_map/all_to_all | solution.py:465
  17.9 0.7 copy-done.4
  18.6 0.1 copy.9.index_ref
  18.7 14.6 %all-to-all-done.rows_ref = bf16[32,64,128]{2,1,0:T(8,128)(2,1)S(1)} async-done(((bf16[32,64,128]{2,1,0:T(8,128)(2,1)}), bf16[32,64,128]{2,1,0:T(8,128)(2,1)S(1)}, u32[]{:S(2)}, u32[]{:S(2)}) %all-to-all-start) | async-done | bytes 524320 | tf_op jit(solution)/shard_map/all_to_all | solution.py:465
  33.3 0.5 select_targets.1
  33.8 12.9 %all_to_all.25.parts_ref = bf16[8,32,128]{2,1,0:T(8,128)(2,1)S(1)} all-to-all(bf16[8,32,128]{2,1,0:T(8,128)(2,1)S(1)} %select_targets.1), channel_id=1, replica_groups=mesh['chip'=4,'core'=2,'sup'=32] {'chip','core'}, dimensions={0} | all-to-all | bytes 131072 | tf_op jit(solution)/shard_map/all_to_all | solution.py:469
  46.7 0.7 merge_targets.1
  47.4 5.4 %all-to-all-start.2 = ((bf16[32,32,128]{2,1,0:T(8,128)(2,1)}), bf16[32,32,128]{2,1,0:T(8,128)(2,1)S(1)}, u32[]{:S(2)}, u32[]{:S(2)}) async-start(bf16[32,32,128]{2,1,0:T(8,128)(2,1)} %merge_targets.1), calls=%async_computation.2 | async-start | bytes 524288 | tf_op jit(solution)/shard_map/all_to_all | solution.py:488
  52.9 0.6 copy-done.3
  53.6 1.0 support_maps.1
  54.6 10.0 %all-to-all-done.2.pix_ref = bf16[32,32,128]{2,1,0:T(8,128)(2,1)S(1)} async-done(((bf16[32,32,128]{2,1,0:T(8,128)(2,1)}), bf16[32,32,128]{2,1,0:T(8,128)(2,1)S(1)}, u32[]{:S(2)}, u32[]{:S(2)}) %all-to-all-start.2) | async-done | bytes 262176 | tf_op jit(solution)/shard_map/all_to_all | solution.py:488
  64.6 10.4 %forward_maps.1 = f32[32,8,128]{2,1,0:T(8,128)} custom-call(bf16[32,32,128]{2,1,0:T(8,128)(2,1)S(1)} %all-to-all-done.2.pix_ref, bf16[10,16,1024]{2,1,0:T(8,128)(2,1)S(1)} %get-tuple-element.12.maps_ref, f32[128,128]{1,0:T(8,128)S(1)} %get-tuple-element.13.gram_ref), custom_call_target="tpu_custom_call" | custom-call | flops 100000000 | bytes 1048576 | tf_op jit(solution)/shard_map/forward_maps/pallas_call | solution.py:490
  75.0 5.1 %all-to-all-start.3 = ((f32[32,8,128]{2,1,0:T(8,128)}), f32[32,8,128]{2,1,0:T(8,128)S(1)}, u32[]{:S(2)}, u32[]{:S(2)}) async-start(f32[32,8,128]{2,1,0:T(8,128)} %forward_maps.1), calls=%async_computation.3 | async-start | bytes 262144 | tf_op jit(solution)/shard_map/all_to_all | solution.py:499
  80.1 14.2 %backward_maps.1 = (bf16[4096,128]{1,0:T(8,128)(2,1)S(1)}, bf16[4096,128]{1,0:T(8,128)(2,1)S(1)}) custom-call(bf16[32,32,128]{2,1,0:T(8,128)(2,1)S(1)} %all-to-all-done.2.pix_ref, bf16[10,16,1024]{2,1,0:T(8,128)(2,1)S(1)} %get-tuple-element.12.maps_ref), custom_call_target="tpu_custom_call" | custom-call | flops 10000000000 | bytes 1048576 | tf_op jit(solution)/shard_map/backward_maps/pallas_call | solution.py:502
  94.3 1.0 weigh_gradient.1.a_ref
  95.4 1.2 %collective-permute-done.b_ref = f32[96,128]{1,0:T(8,128)S(1)} collective-permute-done((f32[96,128]{1,0:T(8,128)S(1)}, f32[96,128]{1,0:T(8,128)S(1)}, u32[]{:S(2)}, u32[]{:S(2)}) %collective-permute-start) | collective-permute-done | bytes 49184 | tf_op jit(solution)/shard_map/ppermute | solution.py:527
  96.7 0.7 sum_cores.1
  97.3 4.7 %all-to-all-start.4 = ((f32[4,96,128]{2,1,0:T(8,128)}), f32[4,96,128]{2,1,0:T(8,128)S(1)}, u32[]{:S(2)}, u32[]{:S(2)}) async-start(f32[4,96,128]{2,1,0:T(8,128)} %sum_cores.1), calls=%async_computation.4 | async-start | bytes 393216 | tf_op jit(solution)/shard_map/all_to_all | solution.py:529
  102.0 1.1 residual.1
  103.1 6.7 %all-to-all-done.4.parts_ref = f32[4,96,128]{2,1,0:T(8,128)S(1)} async-done(((f32[4,96,128]{2,1,0:T(8,128)}), f32[4,96,128]{2,1,0:T(8,128)S(1)}, u32[]{:S(2)}, u32[]{:S(2)}) %all-to-all-start.4) | async-done | bytes 196640 | tf_op jit(solution)/shard_map/all_to_all | solution.py:529
  109.9 0.7 sum_chips.1
  (11 shorter events, 0.2 us)
Async XLA Ops:
  0.6 1.0 copy-start
  1.6 0.7 copy-start.2
  3.6 29.7 %all-to-all-start = ((bf16[32,64,128]{2,1,0:T(8,128)(2,1)}), bf16[32,64,128]{2,1,0:T(8,128)(2,1)S(1)}, u32[]{:S(2)}, u32[]{:S(2)}) async-start(bf16[32,64,128]{2,1,0:T(8,128)(2,1)} %pack_pool.1), calls=%async_computation | async-start | bytes 1048576 | tf_op jit(solution)/shard_map/all_to_all | solution.py:465
  17.9 0.7 copy-start.4
  47.4 5.5 %copy-start.5 = (s32[32]{0:T(128)S(1)}, s32[32]{0:T(128)}, u32[]{:S(2)}) copy-start(s32[32]{0:T(128)} %param.7) | copy-start | bytes 388
  47.4 5.6 %copy-start.1 = (f32[4,3,1024]{2,0,1:T(4,128)S(1)}, f32[4,3,1024]{2,0,1:T(4,128)}, u32[]{:S(2)}) copy-start(f32[4,3,1024]{2,0,1:T(4,128)} %param.8) | copy-start | bytes 147460
  47.4 17.2 %all-to-all-start.2 = ((bf16[32,32,128]{2,1,0:T(8,128)(2,1)}), bf16[32,32,128]{2,1,0:T(8,128)(2,1)S(1)}, u32[]{:S(2)}, u32[]{:S(2)}) async-start(bf16[32,32,128]{2,1,0:T(8,128)(2,1)} %merge_targets.1), calls=%async_computation.2 | async-start | bytes 524288 | tf_op jit(solution)/shard_map/all_to_all | solution.py:488
  52.8 0.7 copy-start.3
  75.0 19.3 %all-to-all-start.3 = ((f32[32,8,128]{2,1,0:T(8,128)}), f32[32,8,128]{2,1,0:T(8,128)S(1)}, u32[]{:S(2)}, u32[]{:S(2)}) async-start(f32[32,8,128]{2,1,0:T(8,128)} %forward_maps.1), calls=%async_computation.3 | async-start | bytes 262144 | tf_op jit(solution)/shard_map/all_to_all | solution.py:499
  95.3 1.3 %collective-permute-start = (f32[96,128]{1,0:T(8,128)S(1)}, f32[96,128]{1,0:T(8,128)S(1)}, u32[]{:S(2)}, u32[]{:S(2)}) collective-permute-start(f32[96,128]{1,0:T(8,128)S(1)} %weigh_gradient.1.a_ref), channel_id=1, source_target_pairs={{0,32},{32,0},{1,33},{33,1},{2,34},{34,2},{3,35},{35,3},{4,36},{36... | collective-permute-start | bytes 147464 | tf_op jit(solution)/shard_map/ppermute | solution.py:527
  97.3 12.5 %all-to-all-start.4 = ((f32[4,96,128]{2,1,0:T(8,128)}), f32[4,96,128]{2,1,0:T(8,128)S(1)}, u32[]{:S(2)}, u32[]{:S(2)}) async-start(f32[4,96,128]{2,1,0:T(8,128)} %sum_cores.1), calls=%async_computation.4 | async-start | bytes 393216 | tf_op jit(solution)/shard_map/all_to_all | solution.py:529

commit v3 on v2

--- a/solution.py
+++ b/solution.py
@@ -12,10 +12,12 @@
 CHAN = 3
 LAYERS = 4
 PIX = SIDE * SIDE
-PLANES = 4
 SUB = 8
 LANES = 128
-STEP_COLS = 4
+TILES = SIDE // SUB
+STEP_ROWS = 8
+STEP_PIX = STEP_ROWS * SIDE
+PARTS = 3
 
 WEIGHT_VAR = 2.0
 BIAS_VAR = 0.1
@@ -102,40 +104,50 @@
     total = parts_ref[0].astype(F32)
     for k in range(1, parts_ref.shape[0]):
         total = total + parts_ref[k].astype(F32)
-    total = total.astype(BF16)
+    turned = total.T
+    n_tgt = turned.shape[1]
+    cut = [turned[c * SIDE : (c + 1) * SIDE, :] for c in range(CHAN)]
+    cut.append(jnp.zeros((SIDE, LANES - CHAN * n_tgt), F32))
+    message = jnp.concatenate(cut, axis=1).astype(BF16)
     for k in range(out_ref.shape[0]):
-        out_ref[k] = total
+        out_ref[k] = message
 
 
 def steps(fn):
-    def one(b, carry):
-        fn(b * STEP_COLS)
-        return carry
-
-    lax.fori_loop(0, SIDE // STEP_COLS, one, 0)
-
-
-def box(ref, col):
-    x = ref[:, pl.ds(col, STEP_COLS + 2)]
-    x = x[:, 0:STEP_COLS] + x[:, 1 : STEP_COLS + 1] + x[:, 2 : STEP_COLS + 2]
-    return x[0:PLANES] + x[1 : PLANES + 1] + x[2 : PLANES + 2]
-
-
-def put(ref, col, x):
-    at = pl.ds(col + 1, STEP_COLS)
-    ref[1 : PLANES + 1, at] = x
-    sub = lax.broadcasted_iota(jnp.int32, x.shape[1:], 1)
-    ref[PLANES + 1, at] = jnp.where(sub < SUB - 1, pltpu.roll(x[0], SUB - 1, 1), 0.0)
-    ref[0, at] = jnp.where(sub > 0, pltpu.roll(x[PLANES - 1], 1, 1), 0.0)
-
-
-def take(ref, start, step, col):
-    planes = []
-    for plane in range(PLANES):
-        at = start + step * plane + col
-        cols = [ref[pl.ds(at + k, SUB, stride=PLANES * step), :] for k in range(STEP_COLS)]
-        planes.append(jnp.stack(cols, axis=0))
-    return jnp.stack(planes, axis=0)
+    for b in range(SIDE // STEP_ROWS):
+        fn(b)
+
+
+def rows_of(b):
+    return pl.ds(b * STEP_ROWS, STEP_ROWS)
+
+
+def pixels_of(b):
+    return pl.ds(b * STEP_PIX, STEP_PIX)
+
+
+def as_map(x):
+    return x.reshape(x.shape[0] // SIDE, TILES, SUB, LANES)
+
+
+def box(ref, row, n):
+    x = ref[pl.ds(row, n + 2)]
+    x = x[0:n] + x[1 : n + 1] + x[2 : n + 2]
+    sub = lax.broadcasted_iota(jnp.int32, x.shape, 2)
+    zero = jnp.zeros_like(x[:, 0:1])
+    left = pltpu.roll(x, 1, 2)
+    right = pltpu.roll(x, SUB - 1, 2)
+    left = jnp.where(sub == 0, jnp.concatenate([zero, left[:, : TILES - 1]], axis=1), left)
+    right = jnp.where(sub == SUB - 1, jnp.concatenate([right[:, 1:], zero], axis=1), right)
+    return x + left + right
+
+
+def step_box(ref, b):
+    return box(ref, b * STEP_ROWS, STEP_ROWS)
+
+
+def put(ref, b, x):
+    ref[pl.ds(b * STEP_ROWS + 1, STEP_ROWS)] = x
 
 
 def q_poly(a):
@@ -157,54 +169,6 @@
     x = 2.0 * var * inv * inv
     left = 1.0 - x
     return 1.0 - left * lax.rsqrt(left) * q_poly(x)
-
-
-def self_step(ref, col):
-    var = BOX_SCALE * box(ref, col) + BIAS_VAR
-    return var, lax.rsqrt(1.0 + 2.0 * var)
-
-
-def spread(pix_ref, nat_ref):
-    n_tgt = pix_ref.shape[1]
-    row = lax.broadcasted_iota(jnp.int32, (n_tgt, LANES), 0)
-    lane = lax.broadcasted_iota(jnp.int32, (n_tgt, LANES), 1)
-    ones = jnp.where(lane % n_tgt == row, 1.0, 0.0).astype(BF16)
-
-    def one(d, carry):
-        nat_ref[pl.ds(d * LANES, LANES), :] = dot_bf16(pix_ref[d], ones, ((0,), (0,)))
-        return carry
-
-    lax.fori_loop(0, SIDE, one, 0, unroll=4)
-
-
-def spread_support(maps_ref, n_tgt, n_sup, nat_ref):
-    rows = maps_ref.shape[1]
-    row = lax.broadcasted_iota(jnp.int32, (rows, LANES), 0)
-    lane = lax.broadcasted_iota(jnp.int32, (rows, LANES), 1)
-    ones = jnp.where((row < 3 * n_sup) & (row % n_sup == lane // n_tgt), 1.0, 0.0).astype(BF16)
-    for k in range(nat_ref.shape[0] // PIX):
-        nat_ref[k * PIX : (k + 1) * PIX, :] = dot_bf16(maps_ref[k], ones, ((0,), (0,)))
-
-
-def take_target(nat_ref, c, col):
-    return take(nat_ref, c * SIDE, LANES, col)
-
-
-def take_support(nat_ref, k, col):
-    return take(nat_ref, k * PIX, SIDE, col)
-
-
-def first_maps(tgt_ref, sup_ref, self_ref, pair_ref):
-    def one(col):
-        own = pair = 0.0
-        for c in range(CHAN):
-            t = take_target(tgt_ref, c, col)
-            own = own + t * t
-            pair = pair + t * take_support(sup_ref, c, col)
-        put(self_ref, col, own * (1.0 / CHAN))
-        put(pair_ref, col, pair * (1.0 / CHAN))
-
-    steps(one)
 
 
 def flat_box(x):
@@ -224,7 +188,7 @@
     n_src = rows_ref.shape[0]
     for j in range(n_sup):
         total = jnp.zeros((n_src, LANES), F32)
-        for k in range(3):
+        for k in range(PARTS):
             total = total + rows_ref[:, k * n_sup + j, :].astype(F32)
         mine_ref[j * n_src : (j + 1) * n_src, :] = total
     lane = lax.broadcasted_iota(jnp.int32, mine_ref.shape, 1)
@@ -240,8 +204,8 @@
 
     def keep(k, x):
         for i, part in enumerate(three_parts(x)):
-            parts_ref[i * n_sup : (i + 1) * n_sup, :] = part.astype(F32)
-        maps_ref[k] = parts_ref[...].astype(BF16)
+            at = (k * PARTS + i) * n_sup
+            parts_ref[at : at + n_sup, :] = part.astype(F32)
 
     current = 0.0
     for c in range(CHAN):
@@ -256,27 +220,99 @@
         if depth < LAYERS - 1:
             keep(CHAN + LAYERS + depth, (4.0 / math.pi) * inv * inv * lax.rsqrt(1.0 + 4.0 * var))
             current = self_act(var, inv)
-
-
-def forward_body(n_sup, pix_ref, maps_ref, gram_ref, out_ref, tgt_ref, sup_ref, self_a, self_b, pair_a, pair_b, acc_ref):
+    row = lax.broadcasted_iota(jnp.int32, (LANES, LANES), 0)
+    lane = lax.broadcasted_iota(jnp.int32, (LANES, LANES), 1)
+    same = jnp.where(row == lane, 1.0, 0.0).astype(BF16)
+    maps_ref[...] = dot_bf16(parts_ref[...].astype(BF16), same, ((0,), (0,))).astype(BF16)
+
+
+def fill_spreads(n_sup, n_tgt, tgt_ref, sup_ref):
+    row = lax.broadcasted_iota(jnp.int32, (LANES, LANES), 0)
+    lane = lax.broadcasted_iota(jnp.int32, (LANES, LANES), 1)
+    own = row % n_tgt == lane % n_tgt
+    for c in range(CHAN):
+        tgt_ref[c] = jnp.where((row // n_tgt == c) & own, 1.0, 0.0).astype(BF16)
+    own = row % n_sup == lane // n_tgt
+    for k in range(sup_ref.shape[0]):
+        sup_ref[k] = jnp.where((row // (PARTS * n_sup) == k) & own, 1.0, 0.0).astype(BF16)
+
+
+def target_map(pix_ref, tgt_ref, c, b):
+    pix = pix_ref[rows_of(b)].reshape(STEP_PIX, LANES)
+    return as_map(dot_bf16(pix, tgt_ref[c], ((1,), (0,))))
+
+
+def support_map(maps_ref, sup_ref, k, b):
+    return as_map(dot_bf16(maps_ref[pixels_of(b), :], sup_ref[k], ((1,), (0,))))
+
+
+QUARTERS = 4
+QUARTER_ROWS = SIDE // QUARTERS
+PER_QUARTER = QUARTER_ROWS // STEP_ROWS
+
+
+def lane_block(shape):
+    return lax.broadcasted_iota(jnp.int32, shape, len(shape) - 1) // (LANES // QUARTERS)
+
+
+def put_edges(ref, first, final):
+    width = LANES // QUARTERS
+    block = lane_block(first.shape)
+    ref[0] = jnp.where(block > 0, pltpu.roll(final, width, 2), 0.0)
+    ref[QUARTER_ROWS + 1] = jnp.where(block < QUARTERS - 1, pltpu.roll(first, LANES - width, 2), 0.0)
+
+
+def first_maps(pix_ref, maps_ref, tgt_ref, sup_ref, self_a, self_b, inv_ref, pair_ref):
+    def one(b):
+        own = pair = 0.0
+        for c in range(CHAN):
+            t = target_map(pix_ref, tgt_ref, c, b)
+            own = own + t * t
+            pair = pair + t * support_map(maps_ref, sup_ref, c, b)
+        put(pair_ref, b, pair * (1.0 / CHAN))
+        at = pl.ds((b % PER_QUARTER) * STEP_ROWS + 1, STEP_ROWS)
+        self_a[at] = jnp.where(lane_block(own.shape) == b // PER_QUARTER, own * (1.0 / CHAN), self_a[at])
+
+    steps(one)
+    put_edges(self_a, self_a[1], self_a[QUARTER_ROWS])
+    for depth in range(LAYERS):
+        now, later = (self_a, self_b) if depth % 2 == 0 else (self_b, self_a)
+        for part in range(PER_QUARTER):
+            var = BOX_SCALE * box(now, part * STEP_ROWS, STEP_ROWS) + BIAS_VAR
+            inv = lax.rsqrt(1.0 + 2.0 * var)
+            inv_ref[depth, part] = inv
+            if depth < LAYERS - 1:
+                value = self_act(var, inv)
+                later[part * STEP_ROWS + 1 : (part + 1) * STEP_ROWS + 1] = value
+        if depth < LAYERS - 1:
+            put_edges(later, later[1], later[QUARTER_ROWS])
+
+
+def target_inv(inv_ref, depth, b):
+    x = inv_ref[depth, b % PER_QUARTER]
+    x = jnp.where(lane_block(x.shape) == b // PER_QUARTER, x, 0.0)
+    x = x + pltpu.roll(x, LANES // 2, 3)
+    return x + pltpu.roll(x, LANES // 4, 3)
+
+
+def forward_body(
+    n_sup, pix_ref, maps_ref, gram_ref, out_ref, tgt_ref, sup_ref, self_a, self_b, inv_ref, pair_a, pair_b, acc_ref
+):
+    n_tgt = LANES // n_sup
     for ref in (self_a, self_b, pair_a, pair_b):
         ref[...] = jnp.zeros_like(ref)
-    spread(pix_ref, tgt_ref)
-    spread_support(maps_ref, pix_ref.shape[1], n_sup, sup_ref)
-    first_maps(tgt_ref, sup_ref, self_a, pair_a)
+    fill_spreads(n_sup, n_tgt, tgt_ref, sup_ref)
+    first_maps(pix_ref, maps_ref, tgt_ref, sup_ref, self_a, self_b, inv_ref, pair_a)
     acc_ref[...] = jnp.zeros_like(acc_ref)
     for depth in range(LAYERS):
-        self_now, self_later = (self_a, self_b) if depth % 2 == 0 else (self_b, self_a)
-        pair_now, pair_later = (pair_a, pair_b) if depth % 2 == 0 else (pair_b, pair_a)
-
-        def one(col, depth=depth, self_now=self_now, self_later=self_later, pair_now=pair_now, pair_later=pair_later):
-            var, inv = self_step(self_now, col)
-            twice = (2.0 * BOX_SCALE) * box(pair_now, col) + 2.0 * BIAS_VAR
-            x = twice * (inv * take_support(sup_ref, CHAN + depth, col))
-            value = act_of(x)[0]
+        now, later = (pair_a, pair_b) if depth % 2 == 0 else (pair_b, pair_a)
+
+        def one(b, depth=depth, now=now, later=later):
+            twice = (2.0 * BOX_SCALE) * step_box(now, b) + 2.0 * BIAS_VAR
+            both = target_inv(inv_ref, depth, b) * support_map(maps_ref, sup_ref, CHAN + depth, b)
+            value = act_of(twice * both)[0]
             if depth < LAYERS - 1:
-                put(self_later, col, self_act(var, inv))
-                put(pair_later, col, value)
+                put(later, b, value)
             else:
                 acc_ref[...] += jnp.sum(value, axis=(0, 1))
 
@@ -299,78 +335,69 @@
     sup_ref,
     self_a,
     self_b,
+    inv_ref,
     pair_a,
     pair_b,
+    grad_a,
+    grad_b,
     dcov_ref,
     dvar_ref,
-    out_ref,
 ):
-    for ref in (self_a, self_b, pair_a, pair_b):
+    n_tgt = LANES // n_sup
+    for ref in (self_a, self_b, pair_a, pair_b, grad_a, grad_b):
         ref[...] = jnp.zeros_like(ref)
-    spread(pix_ref, tgt_ref)
-    spread_support(maps_ref, pix_ref.shape[1], n_sup, sup_ref)
-    first_maps(tgt_ref, sup_ref, self_a, pair_a)
+    fill_spreads(n_sup, n_tgt, tgt_ref, sup_ref)
+    first_maps(pix_ref, maps_ref, tgt_ref, sup_ref, self_a, self_b, inv_ref, pair_a)
     last = LAYERS - 1
     for depth in range(LAYERS):
-        self_now, self_later = (self_a, self_b) if depth % 2 == 0 else (self_b, self_a)
-        pair_now, pair_later = (pair_a, pair_b) if depth % 2 == 0 else (pair_b, pair_a)
-
-        def one(col, depth=depth, self_now=self_now, self_later=self_later, pair_now=pair_now, pair_later=pair_later):
-            at = pl.ds(col, STEP_COLS)
-            var, inv = self_step(self_now, col)
-            twice = (2.0 * BOX_SCALE) * box(pair_now, col) + 2.0 * BIAS_VAR
-            s_inv = take_support(sup_ref, CHAN + depth, col)
-            both = inv * s_inv
+        now, later = (pair_a, pair_b) if depth % 2 == 0 else (pair_b, pair_a)
+
+        def one(b, depth=depth, now=now, later=later):
+            twice = (2.0 * BOX_SCALE) * step_box(now, b) + 2.0 * BIAS_VAR
+            s_inv = support_map(maps_ref, sup_ref, CHAN + depth, b)
+            both = target_inv(inv_ref, depth, b) * s_inv
             x = twice * both
-            value, a, left = act_of(x)
+            if depth < last:
+                value, a, left = act_of(x)
+                put(later, b, value)
+            else:
+                a = jnp.abs(x)
+                left = lax.rsqrt(1.0 - a)
             slope = (2.0 / math.pi) * left * lax.rsqrt(1.0 + a)
             d_cov = 2.0 * both * slope
             d_var = -(slope * x) * (s_inv * s_inv)
             if depth < last:
-                put(self_later, col, self_act(var, inv))
-                put(pair_later, col, value)
-                dcov_ref[depth, :, at] = d_cov
-                dvar_ref[depth, :, at] = d_var
+                dcov_ref[depth, rows_of(b)] = d_cov
+                dvar_ref[depth, rows_of(b)] = d_var
             else:
-                put(pair_later, col, d_cov * (1.0 / PIX))
-                put(self_later, col, d_var * (1.0 / PIX))
+                put(later, b, d_cov * (1.0 / PIX))
+                put(grad_a, b, d_var * (1.0 / PIX))
 
         steps(one)
     for depth in range(last - 1, -1, -1):
-        self_now, self_later = (self_a, self_b) if depth % 2 == 0 else (self_b, self_a)
-        pair_now, pair_later = (pair_a, pair_b) if depth % 2 == 0 else (pair_b, pair_a)
-
-        def one(col, depth=depth, self_now=self_now, self_later=self_later, pair_now=pair_now, pair_later=pair_later):
-            at = pl.ds(col, STEP_COLS)
-            g_pair = BOX_SCALE * box(pair_now, col)
-            g_self = BOX_SCALE * box(self_now, col)
-            slope = take_support(sup_ref, CHAN + LAYERS + depth, col)
-            put(pair_later, col, g_pair * dcov_ref[depth, :, at])
-            put(self_later, col, g_self * slope + g_pair * dvar_ref[depth, :, at])
+        now, later = (pair_a, pair_b) if depth % 2 == 0 else (pair_b, pair_a)
+        own_now, own_later = (grad_a, grad_b) if depth % 2 == 0 else (grad_b, grad_a)
+
+        def one(b, depth=depth, now=now, later=later, own_now=own_now, own_later=own_later):
+            g_pair = BOX_SCALE * step_box(now, b)
+            g_self = BOX_SCALE * step_box(own_now, b)
+            slope = support_map(maps_ref, sup_ref, CHAN + LAYERS + depth, b)
+            put(later, b, g_pair * dcov_ref[depth, rows_of(b)])
+            put(own_later, b, g_self * slope + g_pair * dvar_ref[depth, rows_of(b)])
 
         steps(one)
 
-    def finish(col):
-        g_pair = (BOX_SCALE / CHAN) * box(pair_b, col)
-        g_self = BOX_SCALE * box(self_b, col)
+    def finish(b):
+        g_pair = (BOX_SCALE / CHAN) * step_box(pair_b, b)
         for c in range(CHAN + 1):
-            g = g_pair * take_target(tgt_ref, c, col) if c < CHAN else g_self
-            for plane in range(PLANES):
-                for k in range(STEP_COLS):
-                    at = c * PIX + plane * SIDE + col + k
-                    out_ref[pl.ds(at, SUB, stride=PLANES * SIDE), :] = g[plane, k]
+            g = g_pair * target_map(pix_ref, tgt_ref, c, b) if c < CHAN else BOX_SCALE * step_box(grad_b, b)
+            g = g.reshape(STEP_PIX, LANES)
+            high = g.astype(BF16)
+            at = pl.ds(c * PIX + b * STEP_PIX, STEP_PIX)
+            high_ref[at, :] = high
+            low_ref[at, :] = (g - high.astype(F32)).astype(BF16)
 
     steps(finish)
-
-    def split(k, carry):
-        at = pl.ds(pl.multiple_of(k * 128, 128), 128)
-        g = out_ref[at, :]
-        high = g.astype(BF16)
-        high_ref[at, :] = high
-        low_ref[at, :] = (g - high.astype(F32)).astype(BF16)
-        return carry
-
-    lax.fori_loop(0, out_ref.shape[0] // 128, split, 0)
 
 
 def weigh_body(scale, n_tgt, got_ref, high_ref, low_ref, picked_ref, sup_ref, out_ref):
@@ -437,8 +464,20 @@
                 out_ref[c, j : j + 1, k * LANES : (k + 1) * LANES] = total[row : row + 1, :]
 
 
-def maps(*lead):
-    return pltpu.VMEM((*lead, PLANES + 2, SIDE + 2, SUB, LANES), F32)
+def maps(rows):
+    return pltpu.VMEM((rows, TILES, SUB, LANES), F32)
+
+
+def map_scratch(n_maps):
+    return [
+        pltpu.VMEM((CHAN, LANES, LANES), BF16),
+        pltpu.VMEM((n_maps, LANES, LANES), BF16),
+        maps(QUARTER_ROWS + 2),
+        maps(QUARTER_ROWS + 2),
+        pltpu.VMEM((LAYERS, PER_QUARTER, STEP_ROWS, TILES, SUB, LANES), F32),
+        maps(SIDE + 2),
+        maps(SIDE + 2),
+    ]
 
 
 def local(image_pool, target_index, labels, support, ridge_coef):
@@ -472,45 +511,37 @@
     s_maps, mine, gram, picked = call(
         side_body,
         [
-            jax.ShapeDtypeStruct((n_maps, 16, PIX), BF16),
+            jax.ShapeDtypeStruct((PIX, LANES), BF16),
             jax.ShapeDtypeStruct((n_sup * n_sup_dev, LANES), F32),
             jax.ShapeDtypeStruct((n_sup * n_sup_dev, n_sup * n_sup_dev), F32),
             jax.ShapeDtypeStruct((SUB, LANES), F32),
         ],
         4,
-        scratch=[pltpu.VMEM((16, PIX), F32)],
+        scratch=[pltpu.VMEM((LANES, PIX), F32)],
         flops=10**8,
         name="support_maps",
     )(by_channel, ridge_coef, label_col, rows)
     merged = call(
-        merge_body, jax.ShapeDtypeStruct((n_sup_dev, n_tgt, LANES), BF16), 1, name="merge_targets"
+        merge_body, jax.ShapeDtypeStruct((n_sup_dev, SIDE, LANES), BF16), 1, name="merge_targets"
     )(got)
     pixels = lax.all_to_all(merged, "sup", 0, 0, tiled=True)
-    tgt_nat = pltpu.VMEM((SIDE * LANES, LANES), F32)
     sent = call(
         functools.partial(forward_body, n_sup),
         jax.ShapeDtypeStruct((n_sup_dev, SUB, LANES), F32),
         3,
-        scratch=[tgt_nat, pltpu.VMEM(((CHAN + LAYERS) * PIX, LANES), F32), *[maps()] * 4, pltpu.VMEM((SUB, LANES), F32)],
+        scratch=[*map_scratch(CHAN + LAYERS), pltpu.VMEM((SUB, LANES), F32)],
         flops=10**8,
         name="forward_maps",
         vmem=12,
     )(pixels, s_maps, gram)
     arrived = lax.all_to_all(sent, "sup", 0, 0, tiled=True)
-    layer_maps = pltpu.VMEM((LAYERS - 1, PLANES, SIDE, SUB, LANES), F32)
+    layer_maps = pltpu.VMEM((LAYERS - 1, SIDE, TILES, SUB, LANES), F32)
     flat = (CHAN + 1) * PIX
     high, low = call(
         functools.partial(backward_body, n_sup),
         [jax.ShapeDtypeStruct((flat, LANES), BF16)] * 2,
         2,
-        scratch=[
-            tgt_nat,
-            pltpu.VMEM((n_maps * PIX, LANES), F32),
-            *[maps()] * 4,
-            layer_maps,
-            layer_maps,
-            pltpu.VMEM((flat, LANES), F32),
-        ],
+        scratch=[*map_scratch(n_maps), maps(SIDE + 2), maps(SIDE + 2), layer_maps, layer_maps],
         flops=10**10,
         name="backward_maps",
         vmem=20,

time: 111 us -> 103 us (0.928)
  Pallas kernels: 31.5 us -> 18.6 us
  waiting for transfers between devices: 32.6 us -> 37.1 us
    pallas_call x1, Pallas kernels: 14.2 us -> 6.49 us  [local(): call(functools.partial(backward_body, n_sup), [jax.ShapeDtypeStruct((flat...]
    pallas_call x1, Pallas kernels: 10.4 us -> 4.76 us  [local(): call(functools.partial(forward_body, n_sup), jax.ShapeDtypeStruct((n_sup_...]
    all_to_all x1, waiting for transfers between devices: 0.01 us -> 4.74 us  [local(): arrived = lax.all_to_all(sent, 'sup', 0, 0, tiled=True)]
  transfers between devices with their start and end apart: 5 -> 5, of which waited for: 4 -> 5; matrix products, arithmetic and copies ran while one was open for 0% -> 0% of each run, Pallas kernels for 15% -> 9%
where the time goes in v3:
time: 103 us; the launch traced here: 102 us
  waiting for transfers between devices  37.1 us (36%)
  starting transfers between devices  29.6 us (29%)
  Pallas kernels  18.6 us (18%)
  blocking collectives  12.9 us (13%)
  local copies, waits for them, and re-layouts  3.22 us (3%)
    all_to_all x1, waiting for transfers between devices, local(): rows = lax.all_to_all(packed, 'sup', 0, 0, tiled=True)  14.6 us
    all_to_all x1, starting transfers between devices, local(): rows = lax.all_to_all(packed, 'sup', 0, 0, tiled=True)  14.2 us
    all_to_all x1, blocking collectives, local(): got = lax.all_to_all(chosen, ('chip', 'core'), 0, 0, tiled=True)  12.9 us
    all_to_all x1, waiting for transfers between devices, local(): pixels = lax.all_to_all(merged, 'sup', 0, 0, tiled=True)  9.81 us
    all_to_all x1, waiting for transfers between devices, local(): shares = lax.all_to_all(summed, 'chip', 0, 0, tiled=True)  6.74 us
    pallas_call x1, Pallas kernels, local(): call(functools.partial(backward_body, n_sup), [jax.ShapeDtypeStruct((flat...  6.49 us
    all_to_all x1, starting transfers between devices, local(): pixels = lax.all_to_all(merged, 'sup', 0, 0, tiled=True)  5.45 us
    all_to_all x1, starting transfers between devices, local(): arrived = lax.all_to_all(sent, 'sup', 0, 0, tiled=True)  5.14 us
  transfers between devices with their start and end apart: 5, of which 5 were waited for; matrix products, arithmetic and copies ran while one was open for 0% of the time, Pallas kernels for 9%

profile of v3, /device:TPU:2, one launch (start us, length us, event | category | flops | bytes accessed | tf_op | source)
XLA Modules:
  0.0 102.1 jit_solution(11187680531275353077)
XLA Ops:
  0.6 1.0 copy-done
  1.6 0.7 copy-done.2
  2.3 1.3 %pack_pool.1 = bf16[32,64,128]{2,1,0:T(8,128)(2,1)} custom-call(bf16[64,3072]{1,0:T(8,128)(2,1)S(1)} %copy-done, f32[4,1024]{1,0:T(4,128)S(1)} %copy-done.2), custom_call_target="tpu_custom_call" | custom-call | bytes 1048576 | tf_op jit(solution)/shard_map/pack_pool/pallas_call | solution.py:496
  3.6 14.2 %all-to-all-start = ((bf16[32,64,128]{2,1,0:T(8,128)(2,1)}), bf16[32,64,128]{2,1,0:T(8,128)(2,1)S(1)}, u32[]{:S(2)}, u32[]{:S(2)}) async-start(bf16[32,64,128]{2,1,0:T(8,128)(2,1)} %pack_pool.1), calls=%async_computation | async-start | bytes 1048576 | tf_op jit(solution)/shard_map/all_to_all | solution.py:504
  17.9 0.7 copy-done.4
  18.7 14.6 %all-to-all-done.rows_ref = bf16[32,64,128]{2,1,0:T(8,128)(2,1)S(1)} async-done(((bf16[32,64,128]{2,1,0:T(8,128)(2,1)}), bf16[32,64,128]{2,1,0:T(8,128)(2,1)S(1)}, u32[]{:S(2)}, u32[]{:S(2)}) %all-to-all-start) | async-done | bytes 524320 | tf_op jit(solution)/shard_map/all_to_all | solution.py:504
  33.3 0.5 select_targets.1
  33.8 12.9 %all_to_all.25.parts_ref = bf16[8,32,128]{2,1,0:T(8,128)(2,1)S(1)} all-to-all(bf16[8,32,128]{2,1,0:T(8,128)(2,1)S(1)} %select_targets.1), channel_id=1, replica_groups=mesh['chip'=4,'core'=2,'sup'=32] {'chip','core'}, dimensions={0} | all-to-all | bytes 131072 | tf_op jit(solution)/shard_map/all_to_all | solution.py:508
  46.7 0.9 merge_targets.1
  47.5 5.4 %all-to-all-start.2 = ((bf16[32,32,128]{2,1,0:T(8,128)(2,1)}), bf16[32,32,128]{2,1,0:T(8,128)(2,1)S(1)}, u32[]{:S(2)}, u32[]{:S(2)}) async-start(bf16[32,32,128]{2,1,0:T(8,128)(2,1)} %merge_targets.1), calls=%async_computation.2 | async-start | bytes 524288 | tf_op jit(solution)/shard_map/all_to_all | solution.py:527
  53.1 0.6 copy-done.3
  53.7 1.2 %support_maps.1 = (bf16[1024,128]{1,0:T(8,128)(2,1)S(1)}, f32[128,128]{1,0:T(8,128)S(1)}, f32[128,128]{1,0:T(8,128)S(1)}, f32[8,128]{1,0:T(8,128)S(1)}) custom-call(f32[3,4,1024]{2,1,0:T(4,128)S(1)} %bitcast.6, f32[4,1024]{1,0:T(4,128)S(1)} %copy-done.3, s32[32,1]{1,0:T(8,128)S(1)} %copy.10.labels_ref, bf16[32,64,128]{2,1,0:T(8,128)(2,1)S(1)} %all-to-all-done.rows_ref), custom_call_target="tpu_custom_call" | custom-call | flops 100000000 | bytes 1048576 | tf_op jit(solution)/shard_map/support_maps/pallas_call | solution.py:511
  54.9 9.8 %all-to-all-done.2.pix_ref = bf16[32,32,128]{2,1,0:T(8,128)(2,1)S(1)} async-done(((bf16[32,32,128]{2,1,0:T(8,128)(2,1)}), bf16[32,32,128]{2,1,0:T(8,128)(2,1)S(1)}, u32[]{:S(2)}, u32[]{:S(2)}) %all-to-all-start.2) | async-done | bytes 262176 | tf_op jit(solution)/shard_map/all_to_all | solution.py:527
  64.8 4.8 %forward_maps.1 = f32[32,8,128]{2,1,0:T(8,128)} custom-call(bf16[32,32,128]{2,1,0:T(8,128)(2,1)S(1)} %all-to-all-done.2.pix_ref, bf16[1024,128]{1,0:T(8,128)(2,1)S(1)} %get-tuple-element.12.maps_ref, f32[128,128]{1,0:T(8,128)S(1)} %get-tuple-element.13.gram_ref), custom_call_target="tpu_custom_call" | custom-call | flops 100000000 | bytes 1048576 | tf_op jit(solution)/shard_map/forward_maps/pallas_call | solution.py:528
  69.5 5.1 %all-to-all-start.3 = ((f32[32,8,128]{2,1,0:T(8,128)}), f32[32,8,128]{2,1,0:T(8,128)S(1)}, u32[]{:S(2)}, u32[]{:S(2)}) async-start(f32[32,8,128]{2,1,0:T(8,128)} %forward_maps.1), calls=%async_computation.3 | async-start | bytes 262144 | tf_op jit(solution)/shard_map/all_to_all | solution.py:537
  74.7 6.5 %backward_maps.1 = (bf16[4096,128]{1,0:T(8,128)(2,1)S(1)}, bf16[4096,128]{1,0:T(8,128)(2,1)S(1)}) custom-call(bf16[32,32,128]{2,1,0:T(8,128)(2,1)S(1)} %all-to-all-done.2.pix_ref, bf16[1024,128]{1,0:T(8,128)(2,1)S(1)} %get-tuple-element.12.maps_ref), custom_call_target="tpu_custom_call" | custom-call | flops 10000000000 | bytes 1048576 | tf_op jit(solution)/shard_map/backward_maps/pallas_call | solution.py:540
  81.2 4.7 %all-to-all-done.3.got_ref = f32[32,8,128]{2,1,0:T(8,128)S(1)} async-done(((f32[32,8,128]{2,1,0:T(8,128)}), f32[32,8,128]{2,1,0:T(8,128)S(1)}, u32[]{:S(2)}, u32[]{:S(2)}) %all-to-all-start.3) | async-done | bytes 131104 | tf_op jit(solution)/shard_map/all_to_all | solution.py:537
  85.9 1.0 weigh_gradient.1.a_ref
  87.0 1.2 %collective-permute-done.b_ref = f32[96,128]{1,0:T(8,128)S(1)} collective-permute-done((f32[96,128]{1,0:T(8,128)S(1)}, f32[96,128]{1,0:T(8,128)S(1)}, u32[]{:S(2)}, u32[]{:S(2)}) %collective-permute-start) | collective-permute-done | bytes 49184 | tf_op jit(solution)/shard_map/ppermute | solution.py:558
  88.2 0.7 sum_cores.1
  88.9 4.7 %all-to-all-start.4 = ((f32[4,96,128]{2,1,0:T(8,128)}), f32[4,96,128]{2,1,0:T(8,128)S(1)}, u32[]{:S(2)}, u32[]{:S(2)}) async-start(f32[4,96,128]{2,1,0:T(8,128)} %sum_cores.1), calls=%async_computation.4 | async-start | bytes 393216 | tf_op jit(solution)/shard_map/all_to_all | solution.py:560
  93.6 1.1 %residual.1 = f32[32,32]{1,0:T(8,128)} custom-call(s32[1]{0:T(128)} %bitcast.start_ref, f32[32,8,128]{2,1,0:T(8,128)S(1)} %all-to-all-done.3.got_ref, f32[128,128]{1,0:T(8,128)S(1)} %get-tuple-element.14.mine_ref, s32[32,1]{1,0:T(8,128)S(1)} %copy.10.labels_ref), custom_call_target="tpu_custom_call" | custom-call | flops 10000000 | bytes 1048576 | tf_op jit(solution)/shard_map/residual/pallas_call | solution.py:561
  94.7 6.7 %all-to-all-done.4.parts_ref = f32[4,96,128]{2,1,0:T(8,128)S(1)} async-done(((f32[4,96,128]{2,1,0:T(8,128)}), f32[4,96,128]{2,1,0:T(8,128)S(1)}, u32[]{:S(2)}, u32[]{:S(2)}) %all-to-all-start.4) | async-done | bytes 196640 | tf_op jit(solution)/shard_map/all_to_all | solution.py:560
  101.4 0.7 sum_chips.1
  (11 shorter events, 0.3 us)
Async XLA Ops:
  0.6 1.0 copy-start
  1.6 0.7 copy-start.2
  3.6 29.7 %all-to-all-start = ((bf16[32,64,128]{2,1,0:T(8,128)(2,1)}), bf16[32,64,128]{2,1,0:T(8,128)(2,1)S(1)}, u32[]{:S(2)}, u32[]{:S(2)}) async-start(bf16[32,64,128]{2,1,0:T(8,128)(2,1)} %pack_pool.1), calls=%async_computation | async-start | bytes 1048576 | tf_op jit(solution)/shard_map/all_to_all | solution.py:504
  17.9 0.7 copy-start.4
  47.5 5.5 %copy-start.5 = (s32[32]{0:T(128)S(1)}, s32[32]{0:T(128)}, u32[]{:S(2)}) copy-start(s32[32]{0:T(128)} %param.7) | copy-start | bytes 388
  47.5 5.6 %copy-start.1 = (f32[4,3,1024]{2,0,1:T(4,128)S(1)}, f32[4,3,1024]{2,0,1:T(4,128)}, u32[]{:S(2)}) copy-start(f32[4,3,1024]{2,0,1:T(4,128)} %param.8) | copy-start | bytes 147460
  47.5 17.2 %all-to-all-start.2 = ((bf16[32,32,128]{2,1,0:T(8,128)(2,1)}), bf16[32,32,128]{2,1,0:T(8,128)(2,1)S(1)}, u32[]{:S(2)}, u32[]{:S(2)}) async-start(bf16[32,32,128]{2,1,0:T(8,128)(2,1)} %merge_targets.1), calls=%async_computation.2 | async-start | bytes 524288 | tf_op jit(solution)/shard_map/all_to_all | solution.py:527
  53.0 0.7 copy-start.3
  69.5 16.4 %all-to-all-start.3 = ((f32[32,8,128]{2,1,0:T(8,128)}), f32[32,8,128]{2,1,0:T(8,128)S(1)}, u32[]{:S(2)}, u32[]{:S(2)}) async-start(f32[32,8,128]{2,1,0:T(8,128)} %forward_maps.1), calls=%async_computation.3 | async-start | bytes 262144 | tf_op jit(solution)/shard_map/all_to_all | solution.py:537
  86.9 1.3 %collective-permute-start = (f32[96,128]{1,0:T(8,128)S(1)}, f32[96,128]{1,0:T(8,128)S(1)}, u32[]{:S(2)}, u32[]{:S(2)}) collective-permute-start(f32[96,128]{1,0:T(8,128)S(1)} %weigh_gradient.1.a_ref), channel_id=1, source_target_pairs={{0,32},{32,0},{1,33},{33,1},{2,34},{34,2},{3,35},{35,3},{4,36},{36... | collective-permute-start | bytes 147464 | tf_op jit(solution)/shard_map/ppermute | solution.py:558
  88.9 12.5 %all-to-all-start.4 = ((f32[4,96,128]{2,1,0:T(8,128)}), f32[4,96,128]{2,1,0:T(8,128)S(1)}, u32[]{:S(2)}, u32[]{:S(2)}) async-start(f32[4,96,128]{2,1,0:T(8,128)} %sum_cores.1), calls=%async_computation.4 | async-start | bytes 393216 | tf_op jit(solution)/shard_map/all_to_all | solution.py:560

commit v4 on v3

--- a/solution.py
+++ b/solution.py
@@ -75,42 +75,55 @@
 
 
 def pack_body(pool_ref, ridge_ref, out_ref, parts_ref):
-    rows = pool_ref.shape[0]
     n_sup = ridge_ref.shape[0]
+    halves = out_ref.shape[1]
     parts_ref[...] = jnp.zeros_like(parts_ref)
     for k, part in enumerate(three_parts(ridge_ref[...])):
         parts_ref[k * n_sup : (k + 1) * n_sup, :] = part.astype(F32)
     for tile in range(PIX // LANES):
         at = tile * LANES
         pieces = [pool_ref[:, c * PIX + at : c * PIX + at + LANES] for c in range(CHAN)]
-        pieces.append(parts_ref[:, at : at + LANES].astype(BF16))
         for r in range(LANES // SIDE):
             cut = [p[:, r * SIDE : (r + 1) * SIDE] for p in pieces]
-            out_ref[tile * (LANES // SIDE) + r, :, :] = jnp.concatenate(cut, axis=1)
-
-
-def select_body(base_ref, index_ref, rows_ref, out_ref):
-    n_src, rows, _ = rows_ref.shape
+            image_row = tile * (LANES // SIDE) + r
+            owner, half = image_row // halves, image_row % halves
+            first = (half * (SIDE // halves) + owner) * SIDE
+            cut.append(parts_ref[:, first : first + SIDE].astype(BF16))
+            out_ref[owner, half] = jnp.concatenate(cut, axis=1)
+
+
+def select_body(at_ref, index_ref, rows_ref, out_ref):
+    n_src, halves, rows, _ = rows_ref.shape
+    n_dst, _, n_tgt, _ = out_ref.shape
     total = n_src * rows
-    data = rows_ref[...].reshape(total, LANES)
-    wanted = index_ref[...] - base_ref[0]
+    wanted = index_ref[...] - at_ref[0]
     ids = lax.broadcasted_iota(jnp.int32, (wanted.shape[0], total), 1)
     pick = jnp.where(ids == wanted, 1.0, 0.0).astype(BF16)
-    got = dot_bf16(pick, data, ((1,), (0,)))
-    out_ref[...] = got.astype(BF16).reshape(out_ref.shape)
+    lane = lax.broadcasted_iota(jnp.int32, (n_tgt, LANES), 1)
+    share = n_src // (n_dst // halves)
+    for half in range(halves):
+        data = rows_ref[:, half].reshape(total, LANES)
+        got = dot_bf16(pick, data, ((1,), (0,)))
+        ridge = rows_ref[pl.ds(at_ref[1] * share, share), half, 0 : n_tgt // share].reshape(n_tgt, LANES).astype(F32)
+        for k in range(n_dst // halves):
+            message = jnp.where(lane < CHAN * SIDE, got[k * n_tgt : (k + 1) * n_tgt], ridge).astype(BF16)
+            for twin in range(halves):
+                out_ref[k * halves + twin, half] = message
 
 
 def merge_body(parts_ref, out_ref):
-    total = parts_ref[0].astype(F32)
-    for k in range(1, parts_ref.shape[0]):
-        total = total + parts_ref[k].astype(F32)
-    turned = total.T
-    n_tgt = turned.shape[1]
-    cut = [turned[c * SIDE : (c + 1) * SIDE, :] for c in range(CHAN)]
-    cut.append(jnp.zeros((SIDE, LANES - CHAN * n_tgt), F32))
-    message = jnp.concatenate(cut, axis=1).astype(BF16)
-    for k in range(out_ref.shape[0]):
-        out_ref[k] = message
+    n_dst, halves, _, _ = out_ref.shape
+    for half in range(halves):
+        total = parts_ref[0, half].astype(F32)
+        for k in range(1, parts_ref.shape[0]):
+            total = total + parts_ref[k, half].astype(F32)
+        turned = total.T
+        n_tgt = turned.shape[1]
+        cut = [turned[c * SIDE : (c + 1) * SIDE, :] for c in range(CHAN)]
+        cut.append(jnp.zeros((SIDE, LANES - CHAN * n_tgt), F32))
+        message = jnp.concatenate(cut, axis=1).astype(BF16)
+        for k in range(n_dst):
+            out_ref[k, half] = message
 
 
 def steps(fn):
@@ -182,15 +195,21 @@
     return x + above + below
 
 
-def side_body(sup_ref, ridge_ref, labels_ref, rows_ref, maps_ref, mine_ref, gram_ref, picked_ref, parts_ref):
+def side_body(half_ref, sup_ref, ridge_ref, labels_ref, got_ref, maps_ref, mine_ref, gram_ref, picked_ref, parts_ref):
     n_sup = sup_ref.shape[1]
     n_tgt = labels_ref.shape[0]
-    n_src = rows_ref.shape[0]
-    for j in range(n_sup):
-        total = jnp.zeros((n_src, LANES), F32)
-        for k in range(PARTS):
-            total = total + rows_ref[:, k * n_sup + j, :].astype(F32)
-        mine_ref[j * n_src : (j + 1) * n_src, :] = total
+    n_parts, halves, n_rows, _ = got_ref.shape
+    got = got_ref[:, half_ref[0]].astype(F32)
+    n_src = mine_ref.shape[0] // n_sup
+    share = n_src // n_parts
+    for k in range(n_parts):
+        for i in range(share):
+            at = i * (n_rows // share)
+            total = got[k, at : at + n_sup]
+            for p in range(1, PARTS):
+                total = total + got[k, at + p * n_sup : at + (p + 1) * n_sup]
+            source = (k % halves) * (n_src // halves) + (k // halves) * share + i
+            mine_ref[pl.ds(source, n_sup, stride=n_src), :] = total
     lane = lax.broadcasted_iota(jnp.int32, mine_ref.shape, 1)
     mine = jnp.where(lane >= CHAN * SIDE, mine_ref[...], 0.0)
     mine_ref[...] = mine
@@ -481,31 +500,35 @@
 
 
 def local(image_pool, target_index, labels, support, ridge_coef):
-    n_chip, n_core, n_sup_dev = lax.axis_size("chip"), lax.axis_size("core"), lax.axis_size("sup")
-    n_grp = n_chip * n_core
+    n_chip, n_core, n_half, n_flat = (lax.axis_size(k) for k in ("chip", "core", "zh", "xy"))
+    n_grp, n_sup_dev = n_chip * n_core, n_half * n_flat
     pool_rows = image_pool.shape[0]
     n_sup = support.shape[0]
     n_tgt = labels.shape[0]
     classes = ridge_coef.shape[1] // n_sup_dev
     group = lax.axis_index("chip") * n_core + lax.axis_index("core")
-    base = (group * (n_sup_dev * pool_rows))[None].astype(jnp.int32)
-    start = (lax.axis_index("sup") * classes)[None].astype(jnp.int32)
+    half = lax.axis_index("zh")
+    at = jnp.stack([(group * n_half + half) * (n_flat * pool_rows), group]).astype(jnp.int32)
+    start = ((half * n_flat + lax.axis_index("xy")) * classes)[None].astype(jnp.int32)
     label_col = labels[:, None]
     index_col = target_index[:, None]
 
     packed = call(
         pack_body,
-        jax.ShapeDtypeStruct((n_sup_dev, pool_rows, LANES), BF16),
+        jax.ShapeDtypeStruct((n_flat, n_half, pool_rows, LANES), BF16),
         2,
         scratch=[pltpu.VMEM((pool_rows, PIX), F32)],
         name="pack_pool",
     )(image_pool, ridge_coef)
-    packed, index_col = lax.optimization_barrier((packed, index_col))
-    rows = lax.all_to_all(packed, "sup", 0, 0, tiled=True)
+    rows = lax.all_to_all(packed, "xy", 0, 0, tiled=True)
     chosen = call(
-        select_body, jax.ShapeDtypeStruct((n_grp, n_tgt, LANES), BF16), 3, smem=(0,), name="select_targets"
-    )(base, index_col, rows)
-    got = lax.all_to_all(chosen, ("chip", "core"), 0, 0, tiled=True)
+        select_body,
+        jax.ShapeDtypeStruct((n_grp * n_half, n_half, n_tgt, LANES), BF16),
+        3,
+        smem=(0,),
+        name="select_targets",
+    )(at, index_col, rows)
+    got = lax.all_to_all(chosen, ("chip", "core", "zh"), 0, 0, tiled=True)
     by_channel = jnp.swapaxes(support, 0, 1)
     n_maps = CHAN + 2 * LAYERS - 1
     s_maps, mine, gram, picked = call(
@@ -516,15 +539,16 @@
             jax.ShapeDtypeStruct((n_sup * n_sup_dev, n_sup * n_sup_dev), F32),
             jax.ShapeDtypeStruct((SUB, LANES), F32),
         ],
-        4,
+        5,
         scratch=[pltpu.VMEM((LANES, PIX), F32)],
+        smem=(0,),
         flops=10**8,
         name="support_maps",
-    )(by_channel, ridge_coef, label_col, rows)
+    )(half[None].astype(jnp.int32), by_channel, ridge_coef, label_col, got)
     merged = call(
-        merge_body, jax.ShapeDtypeStruct((n_sup_dev, SIDE, LANES), BF16), 1, name="merge_targets"
+        merge_body, jax.ShapeDtypeStruct((n_flat, n_half, SIDE, LANES), BF16), 1, name="merge_targets"
     )(got)
-    pixels = lax.all_to_all(merged, "sup", 0, 0, tiled=True)
+    pixels = lax.all_to_all(merged, "xy", 0, 0, tiled=True).reshape(SIDE, SIDE, LANES)
     sent = call(
         functools.partial(forward_body, n_sup),
         jax.ShapeDtypeStruct((n_sup_dev, SUB, LANES), F32),
@@ -534,7 +558,7 @@
         name="forward_maps",
         vmem=12,
     )(pixels, s_maps, gram)
-    arrived = lax.all_to_all(sent, "sup", 0, 0, tiled=True)
+    arrived = lax.all_to_all(sent, ("zh", "xy"), 0, 0, tiled=True)
     layer_maps = pltpu.VMEM((LAYERS - 1, SIDE, TILES, SUB, LANES), F32)
     flat = (CHAN + 1) * PIX
     high, low = call(
@@ -572,8 +596,8 @@
 
 def solution(mesh):
     n_tgt, n_sup = mesh.devices.shape
-    parts = Mesh(mesh.devices.reshape(n_tgt // 2, 2, n_sup), ("chip", "core", "sup"))
-    tgt = ("chip", "core")
-    in_specs = (P((*tgt, "sup"), None), P(), P(tgt), P("sup", None, None), P("sup", None))
-    out_specs = (P(tgt, "sup"), P("sup", None, None))
+    parts = Mesh(mesh.devices.reshape(n_tgt // 2, 2, 2, n_sup // 2), ("chip", "core", "zh", "xy"))
+    tgt, sup = ("chip", "core"), ("zh", "xy")
+    in_specs = (P((*tgt, *sup), None), P(), P(tgt), P(sup, None, None), P(sup, None))
+    out_specs = (P(tgt, sup), P(sup, None, None))
     return jax.shard_map(local, mesh=parts, in_specs=in_specs, out_specs=out_specs, check_vma=False)

time: 103 us -> 94.1 us (0.914)
  waiting for transfers between devices: 37.1 us -> 26 us
  blocking collectives: 12.9 us -> 20.7 us
  starting transfers between devices: 29.6 us -> 23.6 us
    all_to_all x3, waiting for transfers between devices: 29.2 us -> 18.1 us  [the longest x1 8.43 us: local(): rows = lax.all_to_all(packed, 'xy', 0, 0, tiled=True)]
    all_to_all x1, blocking collectives: 12.9 us -> 20.7 us  [local(): got = lax.all_to_all(chosen, ('chip', 'core', 'zh'), 0, 0, tiled=True)]
    all_to_all x3, starting transfers between devices: 24.8 us -> 19.2 us  [the longest x1 7.48 us: local(): rows = lax.all_to_all(packed, 'xy', 0, 0, tiled=True)]
where the time goes in v4:
time: 94.1 us; the launch traced here: 93.5 us
  waiting for transfers between devices  26 us (28%)
  starting transfers between devices  23.6 us (25%)
  blocking collectives  20.7 us (22%)
  Pallas kernels  19.2 us (20%)
  local copies, waits for them, and re-layouts  3.22 us (3%)
    all_to_all x1, blocking collectives, local(): got = lax.all_to_all(chosen, ('chip', 'core', 'zh'), 0, 0, tiled=True)  20.7 us
    all_to_all x1, waiting for transfers between devices, local(): rows = lax.all_to_all(packed, 'xy', 0, 0, tiled=True)  8.43 us
    all_to_all x1, starting transfers between devices, local(): rows = lax.all_to_all(packed, 'xy', 0, 0, tiled=True)  7.48 us
    all_to_all x1, waiting for transfers between devices, local(): shares = lax.all_to_all(summed, 'chip', 0, 0, tiled=True)  6.74 us
    pallas_call x1, Pallas kernels, local(): call(functools.partial(backward_body, n_sup), [jax.ShapeDtypeStruct((flat...  6.49 us
    all_to_all x1, starting transfers between devices, local(): arrived = lax.all_to_all(sent, ('zh', 'xy'), 0, 0, tiled=True)  5.9 us
    all_to_all x1, starting transfers between devices, local(): lax.all_to_all(merged, 'xy', 0, 0, tiled=True).reshape(SIDE, SIDE, LANES)  5.8 us
    all_to_all x1, waiting for transfers between devices, local(): lax.all_to_all(merged, 'xy', 0, 0, tiled=True).reshape(SIDE, SIDE, LANES)  4.88 us
  transfers between devices with their start and end apart: 5, of which 5 were waited for; matrix products, arithmetic and copies ran while one was open for 0% of the time, Pallas kernels for 9%

profile of v4, /device:TPU:2, one launch (start us, length us, event | category | flops | bytes accessed | tf_op | source)
XLA Modules:
  0.0 93.5 jit_solution(11972050044903881902)
XLA Ops:
  0.6 1.0 %copy-done = bf16[64,3072]{1,0:T(8,128)(2,1)S(1)} copy-done((bf16[64,3072]{1,0:T(8,128)(2,1)S(1)}, bf16[64,3072]{1,0:T(8,128)(2,1)}, u32[]{:S(2)}) %copy-start) | copy-done | bytes 393240
  1.6 0.7 copy-done.2
  2.3 1.3 %pack_pool.1 = bf16[16,2,64,128]{3,2,1,0:T(8,128)(2,1)} custom-call(bf16[64,3072]{1,0:T(8,128)(2,1)S(1)} %copy-done, f32[4,1024]{1,0:T(4,128)S(1)} %copy-done.2), custom_call_target="tpu_custom_call" | custom-call | bytes 1048576 | tf_op jit(solution)/shard_map/pack_pool/pallas_call | solution.py:516
  3.6 7.5 %all-to-all-start = ((bf16[16,2,64,128]{3,2,1,0:T(8,128)(2,1)}), bf16[16,2,64,128]{3,2,1,0:T(8,128)(2,1)S(1)}, u32[]{:S(2)}, u32[]{:S(2)}) async-start(bf16[16,2,64,128]{3,2,1,0:T(8,128)(2,1)} %pack_pool.1), calls=%async_computation | async-start | bytes 1048576 | tf_op jit(solution)/shard_map/all_to_all | solution.py:523
  11.1 0.7 copy-done.4
  12.0 8.4 %all-to-all-done.rows_ref = bf16[16,2,64,128]{3,2,1,0:T(8,128)(2,1)S(1)} async-done(((bf16[16,2,64,128]{3,2,1,0:T(8,128)(2,1)}), bf16[16,2,64,128]{3,2,1,0:T(8,128)(2,1)S(1)}, u32[]{:S(2)}, u32[]{:S(2)}) %all-to-all-start) | async-done | bytes 524320 | tf_op jit(solution)/shard_map/all_to_all | solution.py:523
  20.4 1.1 %select_targets.1 = bf16[16,2,32,128]{3,2,1,0:T(8,128)(2,1)S(1)} custom-call(s32[2]{0:T(128)S(1)} %pad_add_fusion.at_ref, s32[256,1]{1,0:T(8,128)S(1)} %copy.9.index_ref, bf16[16,2,64,128]{3,2,1,0:T(8,128)(2,1)S(1)} %all-to-all-done.rows_ref), custom_call_target="tpu_custom_call" | custom-call | bytes 1048576 | tf_op jit(solution)/shard_map/select_targets/pallas_call | solution.py:524
  21.5 20.7 %all_to_all.25.parts_ref.got_ref = bf16[16,2,32,128]{3,2,1,0:T(8,128)(2,1)S(1)} all-to-all(bf16[16,2,32,128]{3,2,1,0:T(8,128)(2,1)S(1)} %select_targets.1), channel_id=1, replica_groups=mesh['chip'=4,'core'=2,'zh'=2,'xy'=16] {'chip','core','zh'}, dimensions={0} | all-to-all | bytes 524288 | tf_op jit(solution)/shard_map/all_to_all | solution.py:531
  42.2 0.9 merge_targets.1
  43.1 5.8 %all-to-all-start.2 = ((bf16[16,2,32,128]{3,2,1,0:T(8,128)(2,1)}), bf16[16,2,32,128]{3,2,1,0:T(8,128)(2,1)S(1)}, u32[]{:S(2)}, u32[]{:S(2)}) async-start(bf16[16,2,32,128]{3,2,1,0:T(8,128)(2,1)} %merge_targets.1), calls=%async_computation.2 | async-start | bytes 524288 | tf_op jit(solution)/shard_map/all_to_all | solution.py:551
  49.0 0.6 copy-done.3
  49.6 1.2 %support_maps.1 = (bf16[1024,128]{1,0:T(8,128)(2,1)S(1)}, f32[128,128]{1,0:T(8,128)S(1)}, f32[128,128]{1,0:T(8,128)S(1)}, f32[8,128]{1,0:T(8,128)S(1)}) custom-call(s32[1]{0:T(128)} %bitcast.5.half_ref, f32[3,4,1024]{2,1,0:T(4,128)S(1)} %bitcast.11, f32[4,1024]{1,0:T(4,128)S(1)} %copy-done.3, s32[32,1]{1,0:T(8,128)S(1)} %copy.10.labels_ref, ...), custom_call_target="tpu_custom_call" | custom-call | flops 100000000 | bytes 1048576 | tf_op jit(solution)/shard_map/support_maps/pallas_call | solution.py:534
  50.8 4.9 %all-to-all-done.2 = bf16[16,2,32,128]{3,2,1,0:T(8,128)(2,1)S(1)} async-done(((bf16[16,2,32,128]{3,2,1,0:T(8,128)(2,1)}), bf16[16,2,32,128]{3,2,1,0:T(8,128)(2,1)S(1)}, u32[]{:S(2)}, u32[]{:S(2)}) %all-to-all-start.2) | async-done | bytes 262176 | tf_op jit(solution)/shard_map/all_to_all | solution.py:551
  55.7 4.8 %forward_maps.1 = f32[32,8,128]{2,1,0:T(8,128)} custom-call(bf16[32,32,128]{2,1,0:T(8,128)(2,1)S(1)} %bitcast.9, bf16[1024,128]{1,0:T(8,128)(2,1)S(1)} %get-tuple-element.8.maps_ref, f32[128,128]{1,0:T(8,128)S(1)} %get-tuple-element.9.gram_ref), custom_call_target="tpu_custom_call" | custom-call | flops 100000000 | bytes 1048576 | tf_op jit(solution)/shard_map/forward_maps/pallas_call | solution.py:552
  60.5 5.9 %all-to-all-start.3 = ((f32[32,8,128]{2,1,0:T(8,128)}), f32[32,8,128]{2,1,0:T(8,128)S(1)}, u32[]{:S(2)}, u32[]{:S(2)}) async-start(f32[32,8,128]{2,1,0:T(8,128)} %forward_maps.1), calls=%async_computation.3 | async-start | bytes 262144 | tf_op jit(solution)/shard_map/all_to_all | solution.py:561
  66.4 6.5 %backward_maps.1 = (bf16[4096,128]{1,0:T(8,128)(2,1)S(1)}, bf16[4096,128]{1,0:T(8,128)(2,1)S(1)}) custom-call(bf16[32,32,128]{2,1,0:T(8,128)(2,1)S(1)} %bitcast.10, bf16[1024,128]{1,0:T(8,128)(2,1)S(1)} %get-tuple-element.8.maps_ref), custom_call_target="tpu_custom_call" | custom-call | flops 10000000000 | bytes 1048576 | tf_op jit(solution)/shard_map/backward_maps/pallas_call | solution.py:564
  72.9 4.8 %all-to-all-done.3.got_ref = f32[32,8,128]{2,1,0:T(8,128)S(1)} async-done(((f32[32,8,128]{2,1,0:T(8,128)}), f32[32,8,128]{2,1,0:T(8,128)S(1)}, u32[]{:S(2)}, u32[]{:S(2)}) %all-to-all-start.3) | async-done | bytes 131104 | tf_op jit(solution)/shard_map/all_to_all | solution.py:561
  77.6 1.0 %weigh_gradient.1.a_ref = f32[96,128]{1,0:T(8,128)S(1)} custom-call(f32[32,8,128]{2,1,0:T(8,128)S(1)} %all-to-all-done.3.got_ref, bf16[4096,128]{1,0:T(8,128)(2,1)S(1)} %get-tuple-element.11.high_ref, bf16[4096,128]{1,0:T(8,128)(2,1)S(1)} %get-tuple-element.12.low_ref, f32[8,128]{1,0:T(8,128)S(1)} %get-tuple-element.13.picked_ref, f32[3,4,1024]{2,1,0:T(4,128)S(1)} %bitcast.12), custom_call_target="tpu_custom_call" | custom-call | bytes 1048576 | tf_op jit(solution)/shard_map/weigh_gradient/pallas_call | solution.py:575
  78.8 1.2 %collective-permute-done.b_ref = f32[96,128]{1,0:T(8,128)S(1)} collective-permute-done((f32[96,128]{1,0:T(8,128)S(1)}, f32[96,128]{1,0:T(8,128)S(1)}, u32[]{:S(2)}, u32[]{:S(2)}) %collective-permute-start) | collective-permute-done | bytes 49184 | tf_op jit(solution)/shard_map/ppermute | solution.py:582
  80.0 0.7 sum_cores.1
  80.7 4.3 %all-to-all-start.4 = ((f32[4,96,128]{2,1,0:T(8,128)}), f32[4,96,128]{2,1,0:T(8,128)S(1)}, u32[]{:S(2)}, u32[]{:S(2)}) async-start(f32[4,96,128]{2,1,0:T(8,128)} %sum_cores.1), calls=%async_computation.4 | async-start | bytes 393216 | tf_op jit(solution)/shard_map/all_to_all | solution.py:584
  85.0 1.1 %residual.1 = f32[32,32]{1,0:T(8,128)} custom-call(s32[1]{0:T(128)} %bitcast.start_ref, f32[32,8,128]{2,1,0:T(8,128)S(1)} %all-to-all-done.3.got_ref, f32[128,128]{1,0:T(8,128)S(1)} %get-tuple-element.10.mine_ref, s32[32,1]{1,0:T(8,128)S(1)} %copy.10.labels_ref), custom_call_target="tpu_custom_call" | custom-call | flops 10000000 | bytes 1048576 | tf_op jit(solution)/shard_map/residual/pallas_call | solution.py:585
  86.1 6.7 %all-to-all-done.4.parts_ref = f32[4,96,128]{2,1,0:T(8,128)S(1)} async-done(((f32[4,96,128]{2,1,0:T(8,128)}), f32[4,96,128]{2,1,0:T(8,128)S(1)}, u32[]{:S(2)}, u32[]{:S(2)}) %all-to-all-start.4) | async-done | bytes 196640 | tf_op jit(solution)/shard_map/all_to_all | solution.py:584
  92.8 0.7 sum_chips.1
  (12 shorter events, 0.4 us)
Async XLA Ops:
  0.6 1.0 %copy-start = (bf16[64,3072]{1,0:T(8,128)(2,1)S(1)}, bf16[64,3072]{1,0:T(8,128)(2,1)}, u32[]{:S(2)}) copy-start(bf16[64,3072]{1,0:T(8,128)(2,1)} %pool_ref.1) | copy-start | bytes 1179652
  1.6 0.7 copy-start.2
  3.6 16.8 %all-to-all-start = ((bf16[16,2,64,128]{3,2,1,0:T(8,128)(2,1)}), bf16[16,2,64,128]{3,2,1,0:T(8,128)(2,1)S(1)}, u32[]{:S(2)}, u32[]{:S(2)}) async-start(bf16[16,2,64,128]{3,2,1,0:T(8,128)(2,1)} %pack_pool.1), calls=%async_computation | async-start | bytes 1048576 | tf_op jit(solution)/shard_map/all_to_all | solution.py:523
  11.1 0.7 copy-start.4
  43.1 5.8 %copy-start.5 = (s32[32]{0:T(128)S(1)}, s32[32]{0:T(128)}, u32[]{:S(2)}) copy-start(s32[32]{0:T(128)} %param.7) | copy-start | bytes 388
  43.1 5.9 %copy-start.1 = (f32[4,3,1024]{2,0,1:T(4,128)S(1)}, f32[4,3,1024]{2,0,1:T(4,128)}, u32[]{:S(2)}) copy-start(f32[4,3,1024]{2,0,1:T(4,128)} %param.8) | copy-start | bytes 147460
  43.1 12.6 %all-to-all-start.2 = ((bf16[16,2,32,128]{3,2,1,0:T(8,128)(2,1)}), bf16[16,2,32,128]{3,2,1,0:T(8,128)(2,1)S(1)}, u32[]{:S(2)}, u32[]{:S(2)}) async-start(bf16[16,2,32,128]{3,2,1,0:T(8,128)(2,1)} %merge_targets.1), calls=%async_computation.2 | async-start | bytes 524288 | tf_op jit(solution)/shard_map/all_to_all | solution.py:551
  48.9 0.7 copy-start.3
  60.5 17.2 %all-to-all-start.3 = ((f32[32,8,128]{2,1,0:T(8,128)}), f32[32,8,128]{2,1,0:T(8,128)S(1)}, u32[]{:S(2)}, u32[]{:S(2)}) async-start(f32[32,8,128]{2,1,0:T(8,128)} %forward_maps.1), calls=%async_computation.3 | async-start | bytes 262144 | tf_op jit(solution)/shard_map/all_to_all | solution.py:561
  78.7 1.3 %collective-permute-start = (f32[96,128]{1,0:T(8,128)S(1)}, f32[96,128]{1,0:T(8,128)S(1)}, u32[]{:S(2)}, u32[]{:S(2)}) collective-permute-start(f32[96,128]{1,0:T(8,128)S(1)} %weigh_gradient.1.a_ref), channel_id=1, source_target_pairs={{0,32},{32,0},{1,33},{33,1},{2,34},{34,2},{3,35},{35,3},{4,36},{36... | collective-permute-start | bytes 147464 | tf_op jit(solution)/shard_map/ppermute | solution.py:582
  80.7 12.1 %all-to-all-start.4 = ((f32[4,96,128]{2,1,0:T(8,128)}), f32[4,96,128]{2,1,0:T(8,128)S(1)}, u32[]{:S(2)}, u32[]{:S(2)}) async-start(f32[4,96,128]{2,1,0:T(8,128)} %sum_cores.1), calls=%async_computation.4 | async-start | bytes 393216 | tf_op jit(solution)/shard_map/all_to_all | solution.py:584

commit v5 on v4

--- a/solution.py
+++ b/solution.py
@@ -92,23 +92,41 @@
             out_ref[owner, half] = jnp.concatenate(cut, axis=1)
 
 
-def select_body(at_ref, index_ref, rows_ref, out_ref):
+def select_body(at_ref, index_ref, rows_ref, keep_ref, send_ref):
     n_src, halves, rows, _ = rows_ref.shape
-    n_dst, _, n_tgt, _ = out_ref.shape
+    n_chip, _, _, n_tgt, _ = keep_ref.shape
     total = n_src * rows
     wanted = index_ref[...] - at_ref[0]
     ids = lax.broadcasted_iota(jnp.int32, (wanted.shape[0], total), 1)
     pick = jnp.where(ids == wanted, 1.0, 0.0).astype(BF16)
     lane = lax.broadcasted_iota(jnp.int32, (n_tgt, LANES), 1)
-    share = n_src // (n_dst // halves)
+    pixel = lane < CHAN * SIDE
+    low_core = at_ref[2] == 0
+    share = n_src // n_chip // halves
+    ridge = [[None] * halves for _ in range(halves)]
     for half in range(halves):
-        data = rows_ref[:, half].reshape(total, LANES)
+        for part in range(halves):
+            first = (at_ref[1] * halves + part) * share
+            block = rows_ref[pl.ds(first, share), half, 0 : n_tgt // share]
+            ridge[half][part] = block.reshape(n_tgt, LANES).astype(F32)
+    for part in range(halves):
+        data = rows_ref[:, part].reshape(total, LANES)
         got = dot_bf16(pick, data, ((1,), (0,)))
-        ridge = rows_ref[pl.ds(at_ref[1] * share, share), half, 0 : n_tgt // share].reshape(n_tgt, LANES).astype(F32)
-        for k in range(n_dst // halves):
-            message = jnp.where(lane < CHAN * SIDE, got[k * n_tgt : (k + 1) * n_tgt], ridge).astype(BF16)
-            for twin in range(halves):
-                out_ref[k * halves + twin, half] = message
+        for chip in range(n_chip):
+            low = got[2 * chip * n_tgt : (2 * chip + 1) * n_tgt]
+            high = got[(2 * chip + 1) * n_tgt : (2 * chip + 2) * n_tgt]
+            mine = jnp.where(low_core, low, high)
+            send_ref[chip, part] = jnp.where(pixel, jnp.where(low_core, high, low), 0.0).astype(BF16)
+            for half in range(halves):
+                keep_ref[chip, half, part] = jnp.where(pixel, mine, ridge[half][part]).astype(BF16)
+
+
+def add_body(keep_ref, other_ref, out_ref):
+    n_chip, halves = keep_ref.shape[:2]
+    for chip in range(n_chip):
+        other = other_ref[chip].astype(F32)
+        for half in range(halves):
+            out_ref[chip * halves + half] = (keep_ref[chip, half].astype(F32) + other).astype(BF16)
 
 
 def merge_body(parts_ref, out_ref):
@@ -195,21 +213,22 @@
     return x + above + below
 
 
-def side_body(half_ref, sup_ref, ridge_ref, labels_ref, got_ref, maps_ref, mine_ref, gram_ref, picked_ref, parts_ref):
+def side_body(sup_ref, ridge_ref, labels_ref, got_ref, maps_ref, mine_ref, gram_ref, picked_ref, parts_ref):
     n_sup = sup_ref.shape[1]
     n_tgt = labels_ref.shape[0]
     n_parts, halves, n_rows, _ = got_ref.shape
-    got = got_ref[:, half_ref[0]].astype(F32)
     n_src = mine_ref.shape[0] // n_sup
-    share = n_src // n_parts
+    share = n_src // n_parts // halves
     for k in range(n_parts):
-        for i in range(share):
-            at = i * (n_rows // share)
-            total = got[k, at : at + n_sup]
-            for p in range(1, PARTS):
-                total = total + got[k, at + p * n_sup : at + (p + 1) * n_sup]
-            source = (k % halves) * (n_src // halves) + (k // halves) * share + i
-            mine_ref[pl.ds(source, n_sup, stride=n_src), :] = total
+        for part in range(halves):
+            got = got_ref[k, part].astype(F32)
+            for i in range(share):
+                at = i * (n_rows // share)
+                total = got[at : at + n_sup]
+                for p in range(1, PARTS):
+                    total = total + got[at + p * n_sup : at + (p + 1) * n_sup]
+                source = (k % halves) * (n_src // halves) + ((k // halves) * halves + part) * share + i
+                mine_ref[pl.ds(source, n_sup, stride=n_src), :] = total
     lane = lax.broadcasted_iota(jnp.int32, mine_ref.shape, 1)
     mine = jnp.where(lane >= CHAN * SIDE, mine_ref[...], 0.0)
     mine_ref[...] = mine
@@ -501,14 +520,14 @@
 
 def local(image_pool, target_index, labels, support, ridge_coef):
     n_chip, n_core, n_half, n_flat = (lax.axis_size(k) for k in ("chip", "core", "zh", "xy"))
-    n_grp, n_sup_dev = n_chip * n_core, n_half * n_flat
+    n_sup_dev = n_half * n_flat
     pool_rows = image_pool.shape[0]
     n_sup = support.shape[0]
     n_tgt = labels.shape[0]
     classes = ridge_coef.shape[1] // n_sup_dev
-    group = lax.axis_index("chip") * n_core + lax.axis_index("core")
-    half = lax.axis_index("zh")
-    at = jnp.stack([(group * n_half + half) * (n_flat * pool_rows), group]).astype(jnp.int32)
+    chip, core, half = (lax.axis_index(k) for k in ("chip", "core", "zh"))
+    first_row = ((chip * n_core + core) * n_half + half) * (n_flat * pool_rows)
+    at = jnp.stack([first_row, chip, core]).astype(jnp.int32)
     start = ((half * n_flat + lax.axis_index("xy")) * classes)[None].astype(jnp.int32)
     label_col = labels[:, None]
     index_col = target_index[:, None]
@@ -521,14 +540,25 @@
         name="pack_pool",
     )(image_pool, ridge_coef)
     rows = lax.all_to_all(packed, "xy", 0, 0, tiled=True)
-    chosen = call(
+    keep, send = call(
         select_body,
-        jax.ShapeDtypeStruct((n_grp * n_half, n_half, n_tgt, LANES), BF16),
+        [
+            jax.ShapeDtypeStruct((n_chip, n_half, n_half, n_tgt, LANES), BF16),
+            jax.ShapeDtypeStruct((n_chip, n_half, n_tgt, LANES), BF16),
+        ],
         3,
         smem=(0,),
         name="select_targets",
     )(at, index_col, rows)
-    got = lax.all_to_all(chosen, ("chip", "core", "zh"), 0, 0, tiled=True)
+    swap = [(k, (k + 1) % n_core) for k in range(n_core)]
+    other = lax.ppermute(send, "core", swap)
+    chosen = call(
+        add_body,
+        jax.ShapeDtypeStruct((n_chip * n_half, n_half, n_tgt, LANES), BF16),
+        2,
+        name="add_core_targets",
+    )(keep, other)
+    got = lax.all_to_all(chosen, ("chip", "zh"), 0, 0, tiled=True)
     by_channel = jnp.swapaxes(support, 0, 1)
     n_maps = CHAN + 2 * LAYERS - 1
     s_maps, mine, gram, picked = call(
@@ -539,12 +569,11 @@
             jax.ShapeDtypeStruct((n_sup * n_sup_dev, n_sup * n_sup_dev), F32),
             jax.ShapeDtypeStruct((SUB, LANES), F32),
         ],
-        5,
+        4,
         scratch=[pltpu.VMEM((LANES, PIX), F32)],
-        smem=(0,),
         flops=10**8,
         name="support_maps",
-    )(half[None].astype(jnp.int32), by_channel, ridge_coef, label_col, got)
+    )(by_channel, ridge_coef, label_col, got)
     merged = call(
         merge_body, jax.ShapeDtypeStruct((n_flat, n_half, SIDE, LANES), BF16), 1, name="merge_targets"
     )(got)
@@ -579,7 +608,7 @@
         name="weigh_gradient",
         vmem=8,
     )(arrived, high, low, picked, by_channel)
-    other = lax.ppermute(grad, "core", [(k, (k + 1) % n_core) for k in range(n_core)])
+    other = lax.ppermute(grad, "core", swap)
     summed = call(pair_sum_body, jax.ShapeDtypeStruct((n_chip, wide, LANES), F32), 2, name="sum_cores")(grad, other)
     shares = lax.all_to_all(summed, "chip", 0, 0, tiled=True)
     residual = call(

time: 94.1 us -> 92 us (0.978)
  blocking collectives: 20.7 us -> 16.3 us
  waiting for transfers between devices: 26 us -> 27.3 us
    all_to_all x1, blocking collectives: 20.7 us -> 16.3 us  [local(): got = lax.all_to_all(chosen, ('chip', 'zh'), 0, 0, tiled=True)]
    ppermute x1 -> x2, waiting for transfers between devices: 1.22 us -> 2.46 us  [the longest x1 1.24 us: local(): other = lax.ppermute(send, 'core', swap)]
  transfers between devices with their start and end apart: 5 -> 6, of which waited for: 5 -> 6; matrix products, arithmetic and copies ran while one was open for 0% -> 0% of each run, Pallas kernels for 9% -> 10%
where the time goes in v5:
time: 92 us; the launch traced here: 91.3 us
  waiting for transfers between devices  27.3 us (30%)
  starting transfers between devices  24.4 us (27%)
  Pallas kernels  19.2 us (21%)
  blocking collectives  16.3 us (18%)
  local copies, waits for them, and re-layouts  3.22 us (4%)
    all_to_all x1, blocking collectives, local(): got = lax.all_to_all(chosen, ('chip', 'zh'), 0, 0, tiled=True)  16.3 us
    all_to_all x1, waiting for transfers between devices, local(): rows = lax.all_to_all(packed, 'xy', 0, 0, tiled=True)  8.43 us
    all_to_all x1, starting transfers between devices, local(): rows = lax.all_to_all(packed, 'xy', 0, 0, tiled=True)  7.48 us
    all_to_all x1, waiting for transfers between devices, local(): shares = lax.all_to_all(summed, 'chip', 0, 0, tiled=True)  6.74 us
    all_to_all x1, starting transfers between devices, local(): arrived = lax.all_to_all(sent, ('zh', 'xy'), 0, 0, tiled=True)  6.7 us
    pallas_call x1, Pallas kernels, local(): call(functools.partial(backward_body, n_sup), [jax.ShapeDtypeStruct((flat...  6.49 us
    all_to_all x1, starting transfers between devices, local(): lax.all_to_all(merged, 'xy', 0, 0, tiled=True).reshape(SIDE, SIDE, LANES)  5.8 us
    all_to_all x1, waiting for transfers between devices, local(): lax.all_to_all(merged, 'xy', 0, 0, tiled=True).reshape(SIDE, SIDE, LANES)  4.88 us
  transfers between devices with their start and end apart: 6, of which 6 were waited for; matrix products, arithmetic and copies ran while one was open for 0% of the time, Pallas kernels for 10%

profile of v5, /device:TPU:2, one launch (start us, length us, event | category | flops | bytes accessed | tf_op | source)
XLA Modules:
  0.0 91.3 jit_solution(12437244249967669441)
XLA Ops:
  0.6 1.0 %copy-done = bf16[64,3072]{1,0:T(8,128)(2,1)S(1)} copy-done((bf16[64,3072]{1,0:T(8,128)(2,1)S(1)}, bf16[64,3072]{1,0:T(8,128)(2,1)}, u32[]{:S(2)}) %copy-start) | copy-done | bytes 393240
  1.6 0.7 copy-done.2
  2.3 1.3 %pack_pool.1 = bf16[16,2,64,128]{3,2,1,0:T(8,128)(2,1)} custom-call(bf16[64,3072]{1,0:T(8,128)(2,1)S(1)} %copy-done, f32[4,1024]{1,0:T(4,128)S(1)} %copy-done.2), custom_call_target="tpu_custom_call" | custom-call | bytes 1048576 | tf_op jit(solution)/shard_map/pack_pool/pallas_call | solution.py:535
  3.6 7.5 %all-to-all-start = ((bf16[16,2,64,128]{3,2,1,0:T(8,128)(2,1)}), bf16[16,2,64,128]{3,2,1,0:T(8,128)(2,1)S(1)}, u32[]{:S(2)}, u32[]{:S(2)}) async-start(bf16[16,2,64,128]{3,2,1,0:T(8,128)(2,1)} %pack_pool.1), calls=%async_computation | async-start | bytes 1048576 | tf_op jit(solution)/shard_map/all_to_all | solution.py:542
  11.1 0.7 copy-done.4
  12.0 8.4 %all-to-all-done.rows_ref = bf16[16,2,64,128]{3,2,1,0:T(8,128)(2,1)S(1)} async-done(((bf16[16,2,64,128]{3,2,1,0:T(8,128)(2,1)}), bf16[16,2,64,128]{3,2,1,0:T(8,128)(2,1)S(1)}, u32[]{:S(2)}, u32[]{:S(2)}) %all-to-all-start) | async-done | bytes 524320 | tf_op jit(solution)/shard_map/all_to_all | solution.py:542
  20.4 1.1 %select_targets.1 = (bf16[4,2,2,32,128]{4,3,2,1,0:T(8,128)(2,1)S(1)}, bf16[4,2,32,128]{3,2,1,0:T(8,128)(2,1)S(1)}) custom-call(s32[3]{0:T(128)S(1)} %pad_add_fusion.at_ref, s32[256,1]{1,0:T(8,128)S(1)} %copy.9.index_ref, bf16[16,2,64,128]{3,2,1,0:T(8,128)(2,1)S(1)} %all-to-all-done.rows_ref), custom_call_target="tpu_custom_call" | custom-call | bytes 1048576 | tf_op jit(solution)/shard_map/select_targets/pallas_call | solution.py:543
  21.6 1.2 %collective-permute-done.other_ref = bf16[4,2,32,128]{3,2,1,0:T(8,128)(2,1)S(1)} collective-permute-done((bf16[4,2,32,128]{3,2,1,0:T(8,128)(2,1)S(1)}, bf16[4,2,32,128]{3,2,1,0:T(8,128)(2,1)S(1)}, u32[]{:S(2)}, u32[]{:S(2)}) %collective-permute-start) | collective-permute-done | bytes 65568 | tf_op jit(solution)/shard_map/ppermute | solution.py:554
  22.9 16.3 %all_to_all.25.parts_ref.got_ref = bf16[8,2,32,128]{3,2,1,0:T(8,128)(2,1)S(1)} all-to-all(bf16[8,2,32,128]{3,2,1,0:T(8,128)(2,1)S(1)} %add_core_targets.1), channel_id=1, replica_groups=mesh['chip'=4,'core'=2,'zh'=2,'xy'=16] {'chip','zh'}, dimensions={0} | all-to-all | bytes 262144 | tf_op jit(solution)/shard_map/all_to_all | solution.py:561
  39.2 0.9 merge_targets.1
  40.1 5.8 %all-to-all-start.2 = ((bf16[16,2,32,128]{3,2,1,0:T(8,128)(2,1)}), bf16[16,2,32,128]{3,2,1,0:T(8,128)(2,1)S(1)}, u32[]{:S(2)}, u32[]{:S(2)}) async-start(bf16[16,2,32,128]{3,2,1,0:T(8,128)(2,1)} %merge_targets.1), calls=%async_computation.2 | async-start | bytes 524288 | tf_op jit(solution)/shard_map/all_to_all | solution.py:580
  46.6 1.2 %support_maps.1 = (bf16[1024,128]{1,0:T(8,128)(2,1)S(1)}, f32[128,128]{1,0:T(8,128)S(1)}, f32[128,128]{1,0:T(8,128)S(1)}, f32[8,128]{1,0:T(8,128)S(1)}) custom-call(f32[3,4,1024]{2,1,0:T(4,128)S(1)} %bitcast.11, f32[4,1024]{1,0:T(4,128)S(1)} %copy-done.3, s32[32,1]{1,0:T(8,128)S(1)} %copy.10.labels_ref, bf16[8,2,32,128]{3,2,1,0:T(8,128)(2,1)S(1)} %all_to_all.25.parts_ref.got_ref), custom_call_target="tpu_custom_call" | custom-call | flops 100000000 | bytes 1048576 | tf_op jit(solution)/shard_map/support_maps/pallas_call | solution.py:564
  47.8 4.9 %all-to-all-done.2 = bf16[16,2,32,128]{3,2,1,0:T(8,128)(2,1)S(1)} async-done(((bf16[16,2,32,128]{3,2,1,0:T(8,128)(2,1)}), bf16[16,2,32,128]{3,2,1,0:T(8,128)(2,1)S(1)}, u32[]{:S(2)}, u32[]{:S(2)}) %all-to-all-start.2) | async-done | bytes 262176 | tf_op jit(solution)/shard_map/all_to_all | solution.py:580
  52.7 4.8 %forward_maps.1 = f32[32,8,128]{2,1,0:T(8,128)} custom-call(bf16[32,32,128]{2,1,0:T(8,128)(2,1)S(1)} %bitcast.9, bf16[1024,128]{1,0:T(8,128)(2,1)S(1)} %get-tuple-element.12.maps_ref, f32[128,128]{1,0:T(8,128)S(1)} %get-tuple-element.13.gram_ref), custom_call_target="tpu_custom_call" | custom-call | flops 100000000 | bytes 1048576 | tf_op jit(solution)/shard_map/forward_maps/pallas_call | solution.py:581
  57.5 6.7 %all-to-all-start.3 = ((f32[32,8,128]{2,1,0:T(8,128)}), f32[32,8,128]{2,1,0:T(8,128)S(1)}, u32[]{:S(2)}, u32[]{:S(2)}) async-start(f32[32,8,128]{2,1,0:T(8,128)} %forward_maps.1), calls=%async_computation.3 | async-start | bytes 262144 | tf_op jit(solution)/shard_map/all_to_all | solution.py:590
  64.2 6.5 %backward_maps.1 = (bf16[4096,128]{1,0:T(8,128)(2,1)S(1)}, bf16[4096,128]{1,0:T(8,128)(2,1)S(1)}) custom-call(bf16[32,32,128]{2,1,0:T(8,128)(2,1)S(1)} %bitcast.10, bf16[1024,128]{1,0:T(8,128)(2,1)S(1)} %get-tuple-element.12.maps_ref), custom_call_target="tpu_custom_call" | custom-call | flops 10000000000 | bytes 1048576 | tf_op jit(solution)/shard_map/backward_maps/pallas_call | solution.py:593
  70.7 4.8 %all-to-all-done.3.got_ref = f32[32,8,128]{2,1,0:T(8,128)S(1)} async-done(((f32[32,8,128]{2,1,0:T(8,128)}), f32[32,8,128]{2,1,0:T(8,128)S(1)}, u32[]{:S(2)}, u32[]{:S(2)}) %all-to-all-start.3) | async-done | bytes 131104 | tf_op jit(solution)/shard_map/all_to_all | solution.py:590
  75.5 1.0 %weigh_gradient.1.a_ref = f32[96,128]{1,0:T(8,128)S(1)} custom-call(f32[32,8,128]{2,1,0:T(8,128)S(1)} %all-to-all-done.3.got_ref, bf16[4096,128]{1,0:T(8,128)(2,1)S(1)} %get-tuple-element.15.high_ref, bf16[4096,128]{1,0:T(8,128)(2,1)S(1)} %get-tuple-element.16.low_ref, f32[8,128]{1,0:T(8,128)S(1)} %get-tuple-element.17.picked_ref, f32[3,4,1024]{2,1,0:T(4,128)S(1)} %bitcast.12), custom_call_target="tpu_custom_call" | custom-call | bytes 1048576 | tf_op jit(solution)/shard_map/weigh_gradient/pallas_call | solution.py:604
  76.6 1.2 %collective-permute-done.1.b_ref = f32[96,128]{1,0:T(8,128)S(1)} collective-permute-done((f32[96,128]{1,0:T(8,128)S(1)}, f32[96,128]{1,0:T(8,128)S(1)}, u32[]{:S(2)}, u32[]{:S(2)}) %collective-permute-start.1) | collective-permute-done | bytes 49184 | tf_op jit(solution)/shard_map/ppermute | solution.py:611
  77.8 0.7 sum_cores.1
  78.5 4.3 %all-to-all-start.4 = ((f32[4,96,128]{2,1,0:T(8,128)}), f32[4,96,128]{2,1,0:T(8,128)S(1)}, u32[]{:S(2)}, u32[]{:S(2)}) async-start(f32[4,96,128]{2,1,0:T(8,128)} %sum_cores.1), calls=%async_computation.4 | async-start | bytes 393216 | tf_op jit(solution)/shard_map/all_to_all | solution.py:613
  82.8 1.1 %residual.1 = f32[32,32]{1,0:T(8,128)} custom-call(s32[1]{0:T(128)} %bitcast.start_ref, f32[32,8,128]{2,1,0:T(8,128)S(1)} %all-to-all-done.3.got_ref, f32[128,128]{1,0:T(8,128)S(1)} %get-tuple-element.14.mine_ref, s32[32,1]{1,0:T(8,128)S(1)} %copy.10.labels_ref), custom_call_target="tpu_custom_call" | custom-call | flops 10000000 | bytes 1048576 | tf_op jit(solution)/shard_map/residual/pallas_call | solution.py:614
  83.9 6.7 %all-to-all-done.4.parts_ref = f32[4,96,128]{2,1,0:T(8,128)S(1)} async-done(((f32[4,96,128]{2,1,0:T(8,128)}), f32[4,96,128]{2,1,0:T(8,128)S(1)}, u32[]{:S(2)}, u32[]{:S(2)}) %all-to-all-start.4) | async-done | bytes 196640 | tf_op jit(solution)/shard_map/all_to_all | solution.py:613
  90.6 0.7 sum_chips.1
  (15 shorter events, 1.1 us)
Async XLA Ops:
  0.6 1.0 %copy-start = (bf16[64,3072]{1,0:T(8,128)(2,1)S(1)}, bf16[64,3072]{1,0:T(8,128)(2,1)}, u32[]{:S(2)}) copy-start(bf16[64,3072]{1,0:T(8,128)(2,1)} %pool_ref.1) | copy-start | bytes 1179652
  1.6 0.7 copy-start.2
  3.6 16.8 %all-to-all-start = ((bf16[16,2,64,128]{3,2,1,0:T(8,128)(2,1)}), bf16[16,2,64,128]{3,2,1,0:T(8,128)(2,1)S(1)}, u32[]{:S(2)}, u32[]{:S(2)}) async-start(bf16[16,2,64,128]{3,2,1,0:T(8,128)(2,1)} %pack_pool.1), calls=%async_computation | async-start | bytes 1048576 | tf_op jit(solution)/shard_map/all_to_all | solution.py:542
  11.1 0.7 copy-start.4
  21.5 1.3 %collective-permute-start = (bf16[4,2,32,128]{3,2,1,0:T(8,128)(2,1)S(1)}, bf16[4,2,32,128]{3,2,1,0:T(8,128)(2,1)S(1)}, u32[]{:S(2)}, u32[]{:S(2)}) collective-permute-start(bf16[4,2,32,128]{3,2,1,0:T(8,128)(2,1)S(1)} %get-tuple-element.11), channel_id=1, source_target_pairs={{0,32},{32,0},{1,33},{33,1},{2,34},{34,2},{3,35},{35,3},{4,36},{36... | collective-permute-start | bytes 196616 | tf_op jit(solution)/shard_map/ppermute | solution.py:554
  40.1 5.8 %copy-start.5 = (s32[32]{0:T(128)S(1)}, s32[32]{0:T(128)}, u32[]{:S(2)}) copy-start(s32[32]{0:T(128)} %param.7) | copy-start | bytes 388
  40.1 5.9 %copy-start.1 = (f32[4,3,1024]{2,0,1:T(4,128)S(1)}, f32[4,3,1024]{2,0,1:T(4,128)}, u32[]{:S(2)}) copy-start(f32[4,3,1024]{2,0,1:T(4,128)} %param.8) | copy-start | bytes 147460
  40.1 12.6 %all-to-all-start.2 = ((bf16[16,2,32,128]{3,2,1,0:T(8,128)(2,1)}), bf16[16,2,32,128]{3,2,1,0:T(8,128)(2,1)S(1)}, u32[]{:S(2)}, u32[]{:S(2)}) async-start(bf16[16,2,32,128]{3,2,1,0:T(8,128)(2,1)} %merge_targets.1), calls=%async_computation.2 | async-start | bytes 524288 | tf_op jit(solution)/shard_map/all_to_all | solution.py:580
  45.9 0.7 copy-start.3
  57.5 18.0 %all-to-all-start.3 = ((f32[32,8,128]{2,1,0:T(8,128)}), f32[32,8,128]{2,1,0:T(8,128)S(1)}, u32[]{:S(2)}, u32[]{:S(2)}) async-start(f32[32,8,128]{2,1,0:T(8,128)} %forward_maps.1), calls=%async_computation.3 | async-start | bytes 262144 | tf_op jit(solution)/shard_map/all_to_all | solution.py:590
  76.5 1.3 %collective-permute-start.1 = (f32[96,128]{1,0:T(8,128)S(1)}, f32[96,128]{1,0:T(8,128)S(1)}, u32[]{:S(2)}, u32[]{:S(2)}) collective-permute-start(f32[96,128]{1,0:T(8,128)S(1)} %weigh_gradient.1.a_ref), channel_id=1, source_target_pairs={{0,32},{32,0},{1,33},{33,1},{2,34},{34,2},{3,35},{35,3},{4,36},{36... | collective-permute-start | bytes 147464 | tf_op jit(solution)/shard_map/ppermute | solution.py:611
  78.5 12.1 %all-to-all-start.4 = ((f32[4,96,128]{2,1,0:T(8,128)}), f32[4,96,128]{2,1,0:T(8,128)S(1)}, u32[]{:S(2)}, u32[]{:S(2)}) async-start(f32[4,96,128]{2,1,0:T(8,128)} %sum_cores.1), calls=%async_computation.4 | async-start | bytes 393216 | tf_op jit(solution)/shard_map/all_to_all | solution.py:613

commit v6 on v5

--- a/solution.py
+++ b/solution.py
@@ -18,6 +18,7 @@
 STEP_ROWS = 8
 STEP_PIX = STEP_ROWS * SIDE
 PARTS = 3
+PACK_CUTS = 1
 
 WEIGHT_VAR = 2.0
 BIAS_VAR = 0.1
@@ -28,19 +29,15 @@
 VMEM = pl.BlockSpec(memory_space=pltpu.VMEM)
 SMEM = pl.BlockSpec(memory_space=pltpu.SMEM)
 
-ASIN_Q = [
-    c * 2.0 / math.pi
-    for c in (
-        1.5707963050,
-        -0.2145988016,
-        0.0889789874,
-        -0.0501743046,
-        0.0308918810,
-        -0.0170881256,
-        0.0066700901,
-        -0.0012624911,
-    )
-]
+ASIN_Q = (
+    0.9999999439523269,
+    -0.13661292782489154,
+    0.05655466043182583,
+    -0.03131997834776645,
+    0.01767426424200143,
+    -0.007641460751180656,
+    0.0016626264836763138,
+)
 
 
 def call(body, outs, n_in, scratch=(), smem=(), flops=0, name=None, vmem=4):
@@ -74,15 +71,36 @@
     return lax.dot_general(a, b, (dims, ((), ())), preferred_element_type=F32)
 
 
-def pack_body(pool_ref, ridge_ref, out_ref, parts_ref):
+def pack_body(pool_ref, ridge_ref, out_ref, pool_here, ridge_here, parts_ref, pool_sems, ridge_sem):
     n_sup = ridge_ref.shape[0]
     halves = out_ref.shape[1]
+    width = PIX // PACK_CUTS
+    copies = [
+        [
+            pltpu.make_async_copy(
+                pool_ref.at[:, pl.ds(c * PIX + k * width, width)],
+                pool_here.at[:, pl.ds(c * PIX + k * width, width)],
+                pool_sems.at[k, c],
+            )
+            for c in range(CHAN)
+        ]
+        for k in range(PACK_CUTS)
+    ]
+    ridge_copy = pltpu.make_async_copy(ridge_ref, ridge_here, ridge_sem)
+    ridge_copy.start()
+    for group in copies:
+        for copy in group:
+            copy.start()
     parts_ref[...] = jnp.zeros_like(parts_ref)
-    for k, part in enumerate(three_parts(ridge_ref[...])):
+    ridge_copy.wait()
+    for k, part in enumerate(three_parts(ridge_here[...])):
         parts_ref[k * n_sup : (k + 1) * n_sup, :] = part.astype(F32)
     for tile in range(PIX // LANES):
         at = tile * LANES
-        pieces = [pool_ref[:, c * PIX + at : c * PIX + at + LANES] for c in range(CHAN)]
+        if at % width == 0:
+            for copy in copies[at // width]:
+                copy.wait()
+        pieces = [pool_here[:, c * PIX + at : c * PIX + at + LANES] for c in range(CHAN)]
         for r in range(LANES // SIDE):
             cut = [p[:, r * SIDE : (r + 1) * SIDE] for p in pieces]
             image_row = tile * (LANES // SIDE) + r
@@ -181,25 +199,25 @@
     ref[pl.ds(b * STEP_ROWS + 1, STEP_ROWS)] = x
 
 
-def q_poly(a):
-    acc = ASIN_Q[-1] * a + ASIN_Q[-2]
+def q_poly(a, scale=1.0):
+    acc = (scale * ASIN_Q[-1]) * a + scale * ASIN_Q[-2]
     for c in ASIN_Q[-3::-1]:
-        acc = acc * a + c
+        acc = acc * a + scale * c
     return acc
 
 
-def act_of(x):
+def act_of(x, scale):
     a = jnp.abs(x)
     left = 1.0 - a
     inv = lax.rsqrt(left)
-    value = 1.0 - left * inv * q_poly(a)
+    value = scale - left * inv * q_poly(a, scale)
     return jnp.where(x < 0.0, -value, value), a, inv
 
 
-def self_act(var, inv):
+def self_act(var, inv, scale=1.0):
     x = 2.0 * var * inv * inv
     left = 1.0 - x
-    return 1.0 - left * lax.rsqrt(left) * q_poly(x)
+    return scale - left * lax.rsqrt(left) * q_poly(x, scale)
 
 
 def flat_box(x):
@@ -307,20 +325,20 @@
             t = target_map(pix_ref, tgt_ref, c, b)
             own = own + t * t
             pair = pair + t * support_map(maps_ref, sup_ref, c, b)
-        put(pair_ref, b, pair * (1.0 / CHAN))
+        put(pair_ref, b, pair * (2.0 * BOX_SCALE / CHAN))
         at = pl.ds((b % PER_QUARTER) * STEP_ROWS + 1, STEP_ROWS)
-        self_a[at] = jnp.where(lane_block(own.shape) == b // PER_QUARTER, own * (1.0 / CHAN), self_a[at])
+        self_a[at] = jnp.where(lane_block(own.shape) == b // PER_QUARTER, own * (BOX_SCALE / CHAN), self_a[at])
 
     steps(one)
     put_edges(self_a, self_a[1], self_a[QUARTER_ROWS])
     for depth in range(LAYERS):
         now, later = (self_a, self_b) if depth % 2 == 0 else (self_b, self_a)
         for part in range(PER_QUARTER):
-            var = BOX_SCALE * box(now, part * STEP_ROWS, STEP_ROWS) + BIAS_VAR
+            var = box(now, part * STEP_ROWS, STEP_ROWS) + BIAS_VAR
             inv = lax.rsqrt(1.0 + 2.0 * var)
             inv_ref[depth, part] = inv
             if depth < LAYERS - 1:
-                value = self_act(var, inv)
+                value = self_act(var, inv, BOX_SCALE)
                 later[part * STEP_ROWS + 1 : (part + 1) * STEP_ROWS + 1] = value
         if depth < LAYERS - 1:
             put_edges(later, later[1], later[QUARTER_ROWS])
@@ -346,9 +364,9 @@
         now, later = (pair_a, pair_b) if depth % 2 == 0 else (pair_b, pair_a)
 
         def one(b, depth=depth, now=now, later=later):
-            twice = (2.0 * BOX_SCALE) * step_box(now, b) + 2.0 * BIAS_VAR
+            twice = step_box(now, b) + 2.0 * BIAS_VAR
             both = target_inv(inv_ref, depth, b) * support_map(maps_ref, sup_ref, CHAN + depth, b)
-            value = act_of(twice * both)[0]
+            value = act_of(twice * both, 2.0 * BOX_SCALE if depth < LAYERS - 1 else 1.0)[0]
             if depth < LAYERS - 1:
                 put(later, b, value)
             else:
@@ -391,12 +409,12 @@
         now, later = (pair_a, pair_b) if depth % 2 == 0 else (pair_b, pair_a)
 
         def one(b, depth=depth, now=now, later=later):
-            twice = (2.0 * BOX_SCALE) * step_box(now, b) + 2.0 * BIAS_VAR
+            twice = step_box(now, b) + 2.0 * BIAS_VAR
             s_inv = support_map(maps_ref, sup_ref, CHAN + depth, b)
             both = target_inv(inv_ref, depth, b) * s_inv
             x = twice * both
             if depth < last:
-                value, a, left = act_of(x)
+                value, a, left = act_of(x, 2.0 * BOX_SCALE)
                 put(later, b, value)
             else:
                 a = jnp.abs(x)
@@ -532,11 +550,20 @@
     label_col = labels[:, None]
     index_col = target_index[:, None]
 
-    packed = call(
+    hbm = pl.BlockSpec(memory_space=pltpu.HBM)
+    packed = pl.pallas_call(
         pack_body,
-        jax.ShapeDtypeStruct((n_flat, n_half, pool_rows, LANES), BF16),
-        2,
-        scratch=[pltpu.VMEM((pool_rows, PIX), F32)],
+        out_shape=jax.ShapeDtypeStruct((n_flat, n_half, pool_rows, LANES), BF16),
+        in_specs=[hbm, hbm],
+        out_specs=VMEM,
+        scratch_shapes=[
+            pltpu.VMEM(image_pool.shape, BF16),
+            pltpu.VMEM(ridge_coef.shape, F32),
+            pltpu.VMEM((pool_rows, PIX), F32),
+            pltpu.SemaphoreType.DMA((PACK_CUTS, CHAN)),
+            pltpu.SemaphoreType.DMA,
+        ],
+        compiler_params=pltpu.CompilerParams(vmem_limit_bytes=56 * 2**20),
         name="pack_pool",
     )(image_pool, ridge_coef)
     rows = lax.all_to_all(packed, "xy", 0, 0, tiled=True)

time: 92 us -> 91 us (0.989)
  local copies, waits for them, and re-layouts: 3.22 us -> 1.51 us
    unnamed x12 -> x8, local copies, waits for them, and re-layouts: 3 us -> 1.29 us
    pallas_call x1, Pallas kernels: 1.29 us -> 2.35 us  [local(): pl.pallas_call(pack_body, out_shape=jax.ShapeDtypeStruct((n_flat, n_half,...]
where the time goes in v6:
time: 91 us; the launch traced here: 90.4 us
  waiting for transfers between devices  27.4 us (30%)
  starting transfers between devices  24.5 us (27%)
  Pallas kernels  19.9 us (22%)
  blocking collectives  16.3 us (18%)
  local copies, waits for them, and re-layouts  1.51 us (2%)
    all_to_all x1, blocking collectives, local(): got = lax.all_to_all(chosen, ('chip', 'zh'), 0, 0, tiled=True)  16.3 us
    all_to_all x1, waiting for transfers between devices, local(): rows = lax.all_to_all(packed, 'xy', 0, 0, tiled=True)  8.43 us
    all_to_all x1, starting transfers between devices, local(): rows = lax.all_to_all(packed, 'xy', 0, 0, tiled=True)  7.49 us
    all_to_all x1, waiting for transfers between devices, local(): shares = lax.all_to_all(summed, 'chip', 0, 0, tiled=True)  6.74 us
    all_to_all x1, starting transfers between devices, local(): arrived = lax.all_to_all(sent, ('zh', 'xy'), 0, 0, tiled=True)  6.69 us
    pallas_call x1, Pallas kernels, local(): call(functools.partial(backward_body, n_sup), [jax.ShapeDtypeStruct((flat...  6.34 us
    all_to_all x1, starting transfers between devices, local(): lax.all_to_all(merged, 'xy', 0, 0, tiled=True).reshape(SIDE, SIDE, LANES)  5.8 us
    all_to_all x1, waiting for transfers between devices, local(): arrived = lax.all_to_all(sent, ('zh', 'xy'), 0, 0, tiled=True)  4.93 us
  transfers between devices with their start and end apart: 6, of which 6 were waited for; matrix products, arithmetic and copies ran while one was open for 0% of the time, Pallas kernels for 10%

profile of v6, /device:TPU:2, one launch (start us, length us, event | category | flops | bytes accessed | tf_op | source)
XLA Modules:
  0.0 90.4 jit_solution(458520345995089351)
XLA Ops:
  0.6 2.4 %pack_pool.1 = bf16[16,2,64,128]{3,2,1,0:T(8,128)(2,1)} custom-call(bf16[64,3072]{1,0:T(8,128)(2,1)} %pool_ref.1, f32[4,1024]{1,0:T(4,128)} %ridge_ref.3), custom_call_target="tpu_custom_call" | custom-call | tf_op jit(solution)/shard_map/pack_pool/pallas_call | solution.py:554
  3.0 7.5 %all-to-all-start = ((bf16[16,2,64,128]{3,2,1,0:T(8,128)(2,1)}), bf16[16,2,64,128]{3,2,1,0:T(8,128)(2,1)S(1)}, u32[]{:S(2)}, u32[]{:S(2)}) async-start(bf16[16,2,64,128]{3,2,1,0:T(8,128)(2,1)} %pack_pool.1), calls=%async_computation | async-start | bytes 1048576 | tf_op jit(solution)/shard_map/all_to_all | solution.py:569
  10.5 0.7 copy-done.2
  11.2 0.1 copy.9.index_ref
  11.4 8.4 %all-to-all-done.rows_ref = bf16[16,2,64,128]{3,2,1,0:T(8,128)(2,1)S(1)} async-done(((bf16[16,2,64,128]{3,2,1,0:T(8,128)(2,1)}), bf16[16,2,64,128]{3,2,1,0:T(8,128)(2,1)S(1)}, u32[]{:S(2)}, u32[]{:S(2)}) %all-to-all-start) | async-done | bytes 524320 | tf_op jit(solution)/shard_map/all_to_all | solution.py:569
  19.8 1.1 %select_targets.1 = (bf16[4,2,2,32,128]{4,3,2,1,0:T(8,128)(2,1)S(1)}, bf16[4,2,32,128]{3,2,1,0:T(8,128)(2,1)S(1)}) custom-call(s32[3]{0:T(128)S(1)} %pad_add_fusion.at_ref, s32[256,1]{1,0:T(8,128)S(1)} %copy.9.index_ref, bf16[16,2,64,128]{3,2,1,0:T(8,128)(2,1)S(1)} %all-to-all-done.rows_ref), custom_call_target="tpu_custom_call" | custom-call | bytes 1048576 | tf_op jit(solution)/shard_map/select_targets/pallas_call | solution.py:570
  21.0 1.2 %collective-permute-done.other_ref = bf16[4,2,32,128]{3,2,1,0:T(8,128)(2,1)S(1)} collective-permute-done((bf16[4,2,32,128]{3,2,1,0:T(8,128)(2,1)S(1)}, bf16[4,2,32,128]{3,2,1,0:T(8,128)(2,1)S(1)}, u32[]{:S(2)}, u32[]{:S(2)}) %collective-permute-start) | collective-permute-done | bytes 65568 | tf_op jit(solution)/shard_map/ppermute | solution.py:581
  22.3 16.3 %all_to_all.25.parts_ref.got_ref = bf16[8,2,32,128]{3,2,1,0:T(8,128)(2,1)S(1)} all-to-all(bf16[8,2,32,128]{3,2,1,0:T(8,128)(2,1)S(1)} %add_core_targets.1), channel_id=1, replica_groups=mesh['chip'=4,'core'=2,'zh'=2,'xy'=16] {'chip','zh'}, dimensions={0} | all-to-all | bytes 262144 | tf_op jit(solution)/shard_map/all_to_all | solution.py:588
  38.6 0.9 merge_targets.1
  39.5 5.8 %all-to-all-start.2 = ((bf16[16,2,32,128]{3,2,1,0:T(8,128)(2,1)}), bf16[16,2,32,128]{3,2,1,0:T(8,128)(2,1)S(1)}, u32[]{:S(2)}, u32[]{:S(2)}) async-start(bf16[16,2,32,128]{3,2,1,0:T(8,128)(2,1)} %merge_targets.1), calls=%async_computation.2 | async-start | bytes 524288 | tf_op jit(solution)/shard_map/all_to_all | solution.py:607
  45.4 0.6 copy-done.1
  46.0 1.2 %support_maps.1 = (bf16[1024,128]{1,0:T(8,128)(2,1)S(1)}, f32[128,128]{1,0:T(8,128)S(1)}, f32[128,128]{1,0:T(8,128)S(1)}, f32[8,128]{1,0:T(8,128)S(1)}) custom-call(f32[3,4,1024]{2,1,0:T(4,128)S(1)} %bitcast.11, f32[4,1024]{1,0:T(4,128)S(1)} %copy-done.1, s32[32,1]{1,0:T(8,128)S(1)} %copy.10.labels_ref, bf16[8,2,32,128]{3,2,1,0:T(8,128)(2,1)S(1)} %all_to_all.25.parts_ref.got_ref), custom_call_target="tpu_custom_call" | custom-call | flops 100000000 | bytes 1048576 | tf_op jit(solution)/shard_map/support_maps/pallas_call | solution.py:591
  47.2 4.9 %all-to-all-done.2 = bf16[16,2,32,128]{3,2,1,0:T(8,128)(2,1)S(1)} async-done(((bf16[16,2,32,128]{3,2,1,0:T(8,128)(2,1)}), bf16[16,2,32,128]{3,2,1,0:T(8,128)(2,1)S(1)}, u32[]{:S(2)}, u32[]{:S(2)}) %all-to-all-start.2) | async-done | bytes 262176 | tf_op jit(solution)/shard_map/all_to_all | solution.py:607
  52.1 4.6 %forward_maps.1 = f32[32,8,128]{2,1,0:T(8,128)} custom-call(bf16[32,32,128]{2,1,0:T(8,128)(2,1)S(1)} %bitcast.9, bf16[1024,128]{1,0:T(8,128)(2,1)S(1)} %get-tuple-element.12.maps_ref, f32[128,128]{1,0:T(8,128)S(1)} %get-tuple-element.13.gram_ref), custom_call_target="tpu_custom_call" | custom-call | flops 100000000 | bytes 1048576 | tf_op jit(solution)/shard_map/forward_maps/pallas_call | solution.py:608
  56.6 6.7 %all-to-all-start.3 = ((f32[32,8,128]{2,1,0:T(8,128)}), f32[32,8,128]{2,1,0:T(8,128)S(1)}, u32[]{:S(2)}, u32[]{:S(2)}) async-start(f32[32,8,128]{2,1,0:T(8,128)} %forward_maps.1), calls=%async_computation.3 | async-start | bytes 262144 | tf_op jit(solution)/shard_map/all_to_all | solution.py:617
  63.3 6.3 %backward_maps.1 = (bf16[4096,128]{1,0:T(8,128)(2,1)S(1)}, bf16[4096,128]{1,0:T(8,128)(2,1)S(1)}) custom-call(bf16[32,32,128]{2,1,0:T(8,128)(2,1)S(1)} %bitcast.10, bf16[1024,128]{1,0:T(8,128)(2,1)S(1)} %get-tuple-element.12.maps_ref), custom_call_target="tpu_custom_call" | custom-call | flops 10000000000 | bytes 1048576 | tf_op jit(solution)/shard_map/backward_maps/pallas_call | solution.py:620
  69.7 4.9 %all-to-all-done.3.got_ref = f32[32,8,128]{2,1,0:T(8,128)S(1)} async-done(((f32[32,8,128]{2,1,0:T(8,128)}), f32[32,8,128]{2,1,0:T(8,128)S(1)}, u32[]{:S(2)}, u32[]{:S(2)}) %all-to-all-start.3) | async-done | bytes 131104 | tf_op jit(solution)/shard_map/all_to_all | solution.py:617
  74.6 1.0 %weigh_gradient.1.a_ref = f32[96,128]{1,0:T(8,128)S(1)} custom-call(f32[32,8,128]{2,1,0:T(8,128)S(1)} %all-to-all-done.3.got_ref, bf16[4096,128]{1,0:T(8,128)(2,1)S(1)} %get-tuple-element.15.high_ref, bf16[4096,128]{1,0:T(8,128)(2,1)S(1)} %get-tuple-element.16.low_ref, f32[8,128]{1,0:T(8,128)S(1)} %get-tuple-element.17.picked_ref, f32[3,4,1024]{2,1,0:T(4,128)S(1)} %bitcast.12), custom_call_target="tpu_custom_call" | custom-call | bytes 1048576 | tf_op jit(solution)/shard_map/weigh_gradient/pallas_call | solution.py:631
  75.7 1.2 %collective-permute-done.1.b_ref = f32[96,128]{1,0:T(8,128)S(1)} collective-permute-done((f32[96,128]{1,0:T(8,128)S(1)}, f32[96,128]{1,0:T(8,128)S(1)}, u32[]{:S(2)}, u32[]{:S(2)}) %collective-permute-start.1) | collective-permute-done | bytes 49184 | tf_op jit(solution)/shard_map/ppermute | solution.py:638
  76.9 0.7 sum_cores.1
  77.6 4.3 %all-to-all-start.4 = ((f32[4,96,128]{2,1,0:T(8,128)}), f32[4,96,128]{2,1,0:T(8,128)S(1)}, u32[]{:S(2)}, u32[]{:S(2)}) async-start(f32[4,96,128]{2,1,0:T(8,128)} %sum_cores.1), calls=%async_computation.4 | async-start | bytes 393216 | tf_op jit(solution)/shard_map/all_to_all | solution.py:640
  81.9 1.1 %residual.1 = f32[32,32]{1,0:T(8,128)} custom-call(s32[1]{0:T(128)} %bitcast.start_ref, f32[32,8,128]{2,1,0:T(8,128)S(1)} %all-to-all-done.3.got_ref, f32[128,128]{1,0:T(8,128)S(1)} %get-tuple-element.14.mine_ref, s32[32,1]{1,0:T(8,128)S(1)} %copy.10.labels_ref), custom_call_target="tpu_custom_call" | custom-call | flops 10000000 | bytes 1048576 | tf_op jit(solution)/shard_map/residual/pallas_call | solution.py:641
  83.0 6.7 %all-to-all-done.4.parts_ref = f32[4,96,128]{2,1,0:T(8,128)S(1)} async-done(((f32[4,96,128]{2,1,0:T(8,128)}), f32[4,96,128]{2,1,0:T(8,128)S(1)}, u32[]{:S(2)}, u32[]{:S(2)}) %all-to-all-start.4) | async-done | bytes 196640 | tf_op jit(solution)/shard_map/all_to_all | solution.py:640
  89.8 0.7 sum_chips.1
  (11 shorter events, 0.4 us)
Async XLA Ops:
  3.0 16.8 %all-to-all-start = ((bf16[16,2,64,128]{3,2,1,0:T(8,128)(2,1)}), bf16[16,2,64,128]{3,2,1,0:T(8,128)(2,1)S(1)}, u32[]{:S(2)}, u32[]{:S(2)}) async-start(bf16[16,2,64,128]{3,2,1,0:T(8,128)(2,1)} %pack_pool.1), calls=%async_computation | async-start | bytes 1048576 | tf_op jit(solution)/shard_map/all_to_all | solution.py:569
  10.5 0.7 copy-start.2
  20.9 1.3 %collective-permute-start = (bf16[4,2,32,128]{3,2,1,0:T(8,128)(2,1)S(1)}, bf16[4,2,32,128]{3,2,1,0:T(8,128)(2,1)S(1)}, u32[]{:S(2)}, u32[]{:S(2)}) collective-permute-start(bf16[4,2,32,128]{3,2,1,0:T(8,128)(2,1)S(1)} %get-tuple-element.11), channel_id=1, source_target_pairs={{0,32},{32,0},{1,33},{33,1},{2,34},{34,2},{3,35},{35,3},{4,36},{36... | collective-permute-start | bytes 196616 | tf_op jit(solution)/shard_map/ppermute | solution.py:581
  39.5 5.8 %copy-start.3 = (s32[32]{0:T(128)S(1)}, s32[32]{0:T(128)}, u32[]{:S(2)}) copy-start(s32[32]{0:T(128)} %param.7) | copy-start | bytes 388
  39.5 5.9 %copy-start = (f32[4,3,1024]{2,0,1:T(4,128)S(1)}, f32[4,3,1024]{2,0,1:T(4,128)}, u32[]{:S(2)}) copy-start(f32[4,3,1024]{2,0,1:T(4,128)} %param.8) | copy-start | bytes 147460
  39.5 12.6 %all-to-all-start.2 = ((bf16[16,2,32,128]{3,2,1,0:T(8,128)(2,1)}), bf16[16,2,32,128]{3,2,1,0:T(8,128)(2,1)S(1)}, u32[]{:S(2)}, u32[]{:S(2)}) async-start(bf16[16,2,32,128]{3,2,1,0:T(8,128)(2,1)} %merge_targets.1), calls=%async_computation.2 | async-start | bytes 524288 | tf_op jit(solution)/shard_map/all_to_all | solution.py:607
  45.3 0.7 copy-start.1
  56.6 18.0 %all-to-all-start.3 = ((f32[32,8,128]{2,1,0:T(8,128)}), f32[32,8,128]{2,1,0:T(8,128)S(1)}, u32[]{:S(2)}, u32[]{:S(2)}) async-start(f32[32,8,128]{2,1,0:T(8,128)} %forward_maps.1), calls=%async_computation.3 | async-start | bytes 262144 | tf_op jit(solution)/shard_map/all_to_all | solution.py:617
  75.6 1.3 %collective-permute-start.1 = (f32[96,128]{1,0:T(8,128)S(1)}, f32[96,128]{1,0:T(8,128)S(1)}, u32[]{:S(2)}, u32[]{:S(2)}) collective-permute-start(f32[96,128]{1,0:T(8,128)S(1)} %weigh_gradient.1.a_ref), channel_id=1, source_target_pairs={{0,32},{32,0},{1,33},{33,1},{2,34},{34,2},{3,35},{35,3},{4,36},{36... | collective-permute-start | bytes 147464 | tf_op jit(solution)/shard_map/ppermute | solution.py:638
  77.6 12.1 %all-to-all-start.4 = ((f32[4,96,128]{2,1,0:T(8,128)}), f32[4,96,128]{2,1,0:T(8,128)S(1)}, u32[]{:S(2)}, u32[]{:S(2)}) async-start(f32[4,96,128]{2,1,0:T(8,128)} %sum_cores.1), calls=%async_computation.4 | async-start | bytes 393216 | tf_op jit(solution)/shard_map/all_to_all | solution.py:640

commit v7 on v6

--- a/solution.py
+++ b/solution.py
@@ -71,7 +71,7 @@
     return lax.dot_general(a, b, (dims, ((), ())), preferred_element_type=F32)
 
 
-def pack_body(pool_ref, ridge_ref, out_ref, pool_here, ridge_here, parts_ref, pool_sems, ridge_sem):
+def pack_body(pool_ref, ridge_ref, out_ref, pool_here, ridge_here, parts_ref, out_here, pool_sems, ridge_sem, out_sems):
     n_sup = ridge_ref.shape[0]
     halves = out_ref.shape[1]
     width = PIX // PACK_CUTS
@@ -95,6 +95,7 @@
     ridge_copy.wait()
     for k, part in enumerate(three_parts(ridge_here[...])):
         parts_ref[k * n_sup : (k + 1) * n_sup, :] = part.astype(F32)
+    writes = []
     for tile in range(PIX // LANES):
         at = tile * LANES
         if at % width == 0:
@@ -107,16 +108,26 @@
             owner, half = image_row // halves, image_row % halves
             first = (half * (SIDE // halves) + owner) * SIDE
             cut.append(parts_ref[:, first : first + SIDE].astype(BF16))
-            out_ref[owner, half] = jnp.concatenate(cut, axis=1)
-
-
-def select_body(at_ref, index_ref, rows_ref, keep_ref, send_ref):
+            out_here[owner, half] = jnp.concatenate(cut, axis=1)
+        owners = LANES // SIDE // halves
+        done = pl.ds(tile * owners, owners)
+        writes.append(pltpu.make_async_copy(out_here.at[done], out_ref.at[done], out_sems.at[tile]))
+        writes[-1].start()
+    for write in writes:
+        write.wait()
+
+
+def pick_body(at_ref, index_ref, out_ref):
+    wanted = index_ref[...] - at_ref[0]
+    ids = lax.broadcasted_iota(jnp.int32, out_ref.shape, 1)
+    out_ref[...] = jnp.where(ids == wanted, 1.0, 0.0).astype(BF16)
+
+
+def select_body(at_ref, pick_ref, rows_ref, keep_ref, send_ref):
     n_src, halves, rows, _ = rows_ref.shape
     n_chip, _, _, n_tgt, _ = keep_ref.shape
     total = n_src * rows
-    wanted = index_ref[...] - at_ref[0]
-    ids = lax.broadcasted_iota(jnp.int32, (wanted.shape[0], total), 1)
-    pick = jnp.where(ids == wanted, 1.0, 0.0).astype(BF16)
+    pick = pick_ref[...]
     lane = lax.broadcasted_iota(jnp.int32, (n_tgt, LANES), 1)
     pixel = lane < CHAN * SIDE
     low_core = at_ref[2] == 0
@@ -197,6 +208,12 @@
 
 def put(ref, b, x):
     ref[pl.ds(b * STEP_ROWS + 1, STEP_ROWS)] = x
+
+
+def clear_halo(*refs):
+    for ref in refs:
+        for row in (0, SIDE + 1):
+            ref[row] = jnp.zeros((TILES, SUB, LANES), F32)
 
 
 def q_poly(a, scale=1.0):
@@ -355,8 +372,7 @@
     n_sup, pix_ref, maps_ref, gram_ref, out_ref, tgt_ref, sup_ref, self_a, self_b, inv_ref, pair_a, pair_b, acc_ref
 ):
     n_tgt = LANES // n_sup
-    for ref in (self_a, self_b, pair_a, pair_b):
-        ref[...] = jnp.zeros_like(ref)
+    clear_halo(pair_a, pair_b)
     fill_spreads(n_sup, n_tgt, tgt_ref, sup_ref)
     first_maps(pix_ref, maps_ref, tgt_ref, sup_ref, self_a, self_b, inv_ref, pair_a)
     acc_ref[...] = jnp.zeros_like(acc_ref)
@@ -400,8 +416,7 @@
     dvar_ref,
 ):
     n_tgt = LANES // n_sup
-    for ref in (self_a, self_b, pair_a, pair_b, grad_a, grad_b):
-        ref[...] = jnp.zeros_like(ref)
+    clear_halo(pair_a, pair_b, grad_a, grad_b)
     fill_spreads(n_sup, n_tgt, tgt_ref, sup_ref)
     first_maps(pix_ref, maps_ref, tgt_ref, sup_ref, self_a, self_b, inv_ref, pair_a)
     last = LAYERS - 1
@@ -555,18 +570,28 @@
         pack_body,
         out_shape=jax.ShapeDtypeStruct((n_flat, n_half, pool_rows, LANES), BF16),
         in_specs=[hbm, hbm],
-        out_specs=VMEM,
+        out_specs=hbm,
         scratch_shapes=[
             pltpu.VMEM(image_pool.shape, BF16),
             pltpu.VMEM(ridge_coef.shape, F32),
             pltpu.VMEM((pool_rows, PIX), F32),
+            pltpu.VMEM((n_flat, n_half, pool_rows, LANES), BF16),
             pltpu.SemaphoreType.DMA((PACK_CUTS, CHAN)),
             pltpu.SemaphoreType.DMA,
+            pltpu.SemaphoreType.DMA((PIX // LANES,)),
         ],
         compiler_params=pltpu.CompilerParams(vmem_limit_bytes=56 * 2**20),
         name="pack_pool",
     )(image_pool, ridge_coef)
     rows = lax.all_to_all(packed, "xy", 0, 0, tiled=True)
+    pick = call(
+        pick_body,
+        jax.ShapeDtypeStruct((target_index.shape[0], n_flat * pool_rows), BF16),
+        2,
+        smem=(0,),
+        flops=10**8,
+        name="pick_rows",
+    )(at, index_col)
     keep, send = call(
         select_body,
         [
@@ -576,7 +601,7 @@
         3,
         smem=(0,),
         name="select_targets",
-    )(at, index_col, rows)
+    )(at, pick, rows)
     swap = [(k, (k + 1) % n_core) for k in range(n_core)]
     other = lax.ppermute(send, "core", swap)
     chosen = call(

time: 91 us -> 90.8 us (level)
  no operation moved by 1% of the time
where the time goes in v7:
time: 90.8 us; the launch traced here: 90.2 us
  waiting for transfers between devices  26.7 us (29%)
  starting transfers between devices  24.5 us (27%)
  Pallas kernels  20.4 us (22%)
  blocking collectives  16.3 us (18%)
  local copies, waits for them, and re-layouts  1.51 us (2%)
    all_to_all x1, blocking collectives, local(): got = lax.all_to_all(chosen, ('chip', 'zh'), 0, 0, tiled=True)  16.3 us
    all_to_all x1, waiting for transfers between devices, local(): rows = lax.all_to_all(packed, 'xy', 0, 0, tiled=True)  7.72 us
    all_to_all x1, starting transfers between devices, local(): rows = lax.all_to_all(packed, 'xy', 0, 0, tiled=True)  7.49 us
    all_to_all x1, waiting for transfers between devices, local(): shares = lax.all_to_all(summed, 'chip', 0, 0, tiled=True)  6.74 us
    all_to_all x1, starting transfers between devices, local(): arrived = lax.all_to_all(sent, ('zh', 'xy'), 0, 0, tiled=True)  6.7 us
    pallas_call x1, Pallas kernels, local(): call(functools.partial(backward_body, n_sup), [jax.ShapeDtypeStruct((flat...  6.33 us
    all_to_all x1, starting transfers between devices, local(): lax.all_to_all(merged, 'xy', 0, 0, tiled=True).reshape(SIDE, SIDE, LANES)  5.8 us
    all_to_all x1, waiting for transfers between devices, local(): arrived = lax.all_to_all(sent, ('zh', 'xy'), 0, 0, tiled=True)  4.94 us
  transfers between devices with their start and end apart: 6, of which 6 were waited for; matrix products, arithmetic and copies ran while one was open for 0% of the time, Pallas kernels for 10%

profile of v7, /device:TPU:2, one launch (start us, length us, event | category | flops | bytes accessed | tf_op | source)
XLA Modules:
  0.0 90.2 jit_solution(17281488169651676068)
XLA Ops:
  0.6 2.3 %pack_pool.1 = bf16[16,2,64,128]{3,2,1,0:T(8,128)(2,1)} custom-call(bf16[64,3072]{1,0:T(8,128)(2,1)} %pool_ref.1, f32[4,1024]{1,0:T(4,128)} %ridge_ref.3), custom_call_target="tpu_custom_call" | custom-call | tf_op jit(solution)/shard_map/pack_pool/pallas_call | solution.py:569
  2.9 7.5 %all-to-all-start = ((bf16[16,2,64,128]{3,2,1,0:T(8,128)(2,1)}), bf16[16,2,64,128]{3,2,1,0:T(8,128)(2,1)S(1)}, u32[]{:S(2)}, u32[]{:S(2)}) async-start(bf16[16,2,64,128]{3,2,1,0:T(8,128)(2,1)} %pack_pool.1), calls=%async_computation | async-start | bytes 1048576 | tf_op jit(solution)/shard_map/all_to_all | solution.py:586
  10.4 0.7 copy-done.2
  11.3 0.7 pick_rows.1.pick_ref
  12.0 7.7 %all-to-all-done.rows_ref = bf16[16,2,64,128]{3,2,1,0:T(8,128)(2,1)S(1)} async-done(((bf16[16,2,64,128]{3,2,1,0:T(8,128)(2,1)}), bf16[16,2,64,128]{3,2,1,0:T(8,128)(2,1)S(1)}, u32[]{:S(2)}, u32[]{:S(2)}) %all-to-all-start) | async-done | bytes 524320 | tf_op jit(solution)/shard_map/all_to_all | solution.py:586
  19.7 1.0 %select_targets.1 = (bf16[4,2,2,32,128]{4,3,2,1,0:T(8,128)(2,1)S(1)}, bf16[4,2,32,128]{3,2,1,0:T(8,128)(2,1)S(1)}) custom-call(s32[3]{0:T(128)S(1)} %pad_add_fusion.at_ref, bf16[256,1024]{1,0:T(8,128)(2,1)S(1)} %pick_rows.1.pick_ref, bf16[16,2,64,128]{3,2,1,0:T(8,128)(2,1)S(1)} %all-to-all-done.rows_ref), custom_call_target="tpu_custom_call" | custom-call | bytes 1048576 | tf_op jit(solution)/shard_map/select_targets/pallas_call | solution.py:595
  20.8 1.2 %collective-permute-done.other_ref = bf16[4,2,32,128]{3,2,1,0:T(8,128)(2,1)S(1)} collective-permute-done((bf16[4,2,32,128]{3,2,1,0:T(8,128)(2,1)S(1)}, bf16[4,2,32,128]{3,2,1,0:T(8,128)(2,1)S(1)}, u32[]{:S(2)}, u32[]{:S(2)}) %collective-permute-start) | collective-permute-done | bytes 65568 | tf_op jit(solution)/shard_map/ppermute | solution.py:606
  22.1 16.3 %all_to_all.25.parts_ref.got_ref = bf16[8,2,32,128]{3,2,1,0:T(8,128)(2,1)S(1)} all-to-all(bf16[8,2,32,128]{3,2,1,0:T(8,128)(2,1)S(1)} %add_core_targets.1), channel_id=1, replica_groups=mesh['chip'=4,'core'=2,'zh'=2,'xy'=16] {'chip','zh'}, dimensions={0} | all-to-all | bytes 262144 | tf_op jit(solution)/shard_map/all_to_all | solution.py:613
  38.3 0.9 merge_targets.1
  39.2 5.8 %all-to-all-start.2 = ((bf16[16,2,32,128]{3,2,1,0:T(8,128)(2,1)}), bf16[16,2,32,128]{3,2,1,0:T(8,128)(2,1)S(1)}, u32[]{:S(2)}, u32[]{:S(2)}) async-start(bf16[16,2,32,128]{3,2,1,0:T(8,128)(2,1)} %merge_targets.1), calls=%async_computation.2 | async-start | bytes 524288 | tf_op jit(solution)/shard_map/all_to_all | solution.py:632
  45.1 0.6 copy-done.1
  45.8 1.2 %support_maps.1 = (bf16[1024,128]{1,0:T(8,128)(2,1)S(1)}, f32[128,128]{1,0:T(8,128)S(1)}, f32[128,128]{1,0:T(8,128)S(1)}, f32[8,128]{1,0:T(8,128)S(1)}) custom-call(f32[3,4,1024]{2,1,0:T(4,128)S(1)} %bitcast.11, f32[4,1024]{1,0:T(4,128)S(1)} %copy-done.1, s32[32,1]{1,0:T(8,128)S(1)} %copy.10.labels_ref, bf16[8,2,32,128]{3,2,1,0:T(8,128)(2,1)S(1)} %all_to_all.25.parts_ref.got_ref), custom_call_target="tpu_custom_call" | custom-call | flops 100000000 | bytes 1048576 | tf_op jit(solution)/shard_map/support_maps/pallas_call | solution.py:616
  47.0 4.9 %all-to-all-done.2 = bf16[16,2,32,128]{3,2,1,0:T(8,128)(2,1)S(1)} async-done(((bf16[16,2,32,128]{3,2,1,0:T(8,128)(2,1)}), bf16[16,2,32,128]{3,2,1,0:T(8,128)(2,1)S(1)}, u32[]{:S(2)}, u32[]{:S(2)}) %all-to-all-start.2) | async-done | bytes 262176 | tf_op jit(solution)/shard_map/all_to_all | solution.py:632
  51.8 4.5 %forward_maps.1 = f32[32,8,128]{2,1,0:T(8,128)} custom-call(bf16[32,32,128]{2,1,0:T(8,128)(2,1)S(1)} %bitcast.9, bf16[1024,128]{1,0:T(8,128)(2,1)S(1)} %get-tuple-element.12.maps_ref, f32[128,128]{1,0:T(8,128)S(1)} %get-tuple-element.13.gram_ref), custom_call_target="tpu_custom_call" | custom-call | flops 100000000 | bytes 1048576 | tf_op jit(solution)/shard_map/forward_maps/pallas_call | solution.py:633
  56.4 6.7 %all-to-all-start.3 = ((f32[32,8,128]{2,1,0:T(8,128)}), f32[32,8,128]{2,1,0:T(8,128)S(1)}, u32[]{:S(2)}, u32[]{:S(2)}) async-start(f32[32,8,128]{2,1,0:T(8,128)} %forward_maps.1), calls=%async_computation.3 | async-start | bytes 262144 | tf_op jit(solution)/shard_map/all_to_all | solution.py:642
  63.1 6.3 %backward_maps.1 = (bf16[4096,128]{1,0:T(8,128)(2,1)S(1)}, bf16[4096,128]{1,0:T(8,128)(2,1)S(1)}) custom-call(bf16[32,32,128]{2,1,0:T(8,128)(2,1)S(1)} %bitcast.10, bf16[1024,128]{1,0:T(8,128)(2,1)S(1)} %get-tuple-element.12.maps_ref), custom_call_target="tpu_custom_call" | custom-call | flops 10000000000 | bytes 1048576 | tf_op jit(solution)/shard_map/backward_maps/pallas_call | solution.py:645
  69.4 4.9 %all-to-all-done.3.got_ref = f32[32,8,128]{2,1,0:T(8,128)S(1)} async-done(((f32[32,8,128]{2,1,0:T(8,128)}), f32[32,8,128]{2,1,0:T(8,128)S(1)}, u32[]{:S(2)}, u32[]{:S(2)}) %all-to-all-start.3) | async-done | bytes 131104 | tf_op jit(solution)/shard_map/all_to_all | solution.py:642
  74.4 1.0 %weigh_gradient.1.a_ref = f32[96,128]{1,0:T(8,128)S(1)} custom-call(f32[32,8,128]{2,1,0:T(8,128)S(1)} %all-to-all-done.3.got_ref, bf16[4096,128]{1,0:T(8,128)(2,1)S(1)} %get-tuple-element.15.high_ref, bf16[4096,128]{1,0:T(8,128)(2,1)S(1)} %get-tuple-element.16.low_ref, f32[8,128]{1,0:T(8,128)S(1)} %get-tuple-element.17.picked_ref, f32[3,4,1024]{2,1,0:T(4,128)S(1)} %bitcast.12), custom_call_target="tpu_custom_call" | custom-call | bytes 1048576 | tf_op jit(solution)/shard_map/weigh_gradient/pallas_call | solution.py:656
  75.5 1.2 %collective-permute-done.1.b_ref = f32[96,128]{1,0:T(8,128)S(1)} collective-permute-done((f32[96,128]{1,0:T(8,128)S(1)}, f32[96,128]{1,0:T(8,128)S(1)}, u32[]{:S(2)}, u32[]{:S(2)}) %collective-permute-start.1) | collective-permute-done | bytes 49184 | tf_op jit(solution)/shard_map/ppermute | solution.py:663
  76.7 0.7 sum_cores.1
  77.4 4.3 %all-to-all-start.4 = ((f32[4,96,128]{2,1,0:T(8,128)}), f32[4,96,128]{2,1,0:T(8,128)S(1)}, u32[]{:S(2)}, u32[]{:S(2)}) async-start(f32[4,96,128]{2,1,0:T(8,128)} %sum_cores.1), calls=%async_computation.4 | async-start | bytes 393216 | tf_op jit(solution)/shard_map/all_to_all | solution.py:665
  81.7 1.1 %residual.1 = f32[32,32]{1,0:T(8,128)} custom-call(s32[1]{0:T(128)} %bitcast.start_ref, f32[32,8,128]{2,1,0:T(8,128)S(1)} %all-to-all-done.3.got_ref, f32[128,128]{1,0:T(8,128)S(1)} %get-tuple-element.14.mine_ref, s32[32,1]{1,0:T(8,128)S(1)} %copy.10.labels_ref), custom_call_target="tpu_custom_call" | custom-call | flops 10000000 | bytes 1048576 | tf_op jit(solution)/shard_map/residual/pallas_call | solution.py:666
  82.8 6.7 %all-to-all-done.4.parts_ref = f32[4,96,128]{2,1,0:T(8,128)S(1)} async-done(((f32[4,96,128]{2,1,0:T(8,128)}), f32[4,96,128]{2,1,0:T(8,128)S(1)}, u32[]{:S(2)}, u32[]{:S(2)}) %all-to-all-start.4) | async-done | bytes 196640 | tf_op jit(solution)/shard_map/all_to_all | solution.py:665
  89.5 0.7 sum_chips.1
  (12 shorter events, 0.5 us)
Async XLA Ops:
  2.9 16.8 %all-to-all-start = ((bf16[16,2,64,128]{3,2,1,0:T(8,128)(2,1)}), bf16[16,2,64,128]{3,2,1,0:T(8,128)(2,1)S(1)}, u32[]{:S(2)}, u32[]{:S(2)}) async-start(bf16[16,2,64,128]{3,2,1,0:T(8,128)(2,1)} %pack_pool.1), calls=%async_computation | async-start | bytes 1048576 | tf_op jit(solution)/shard_map/all_to_all | solution.py:586
  10.4 0.7 copy-start.2
  20.7 1.3 %collective-permute-start = (bf16[4,2,32,128]{3,2,1,0:T(8,128)(2,1)S(1)}, bf16[4,2,32,128]{3,2,1,0:T(8,128)(2,1)S(1)}, u32[]{:S(2)}, u32[]{:S(2)}) collective-permute-start(bf16[4,2,32,128]{3,2,1,0:T(8,128)(2,1)S(1)} %get-tuple-element.11), channel_id=1, source_target_pairs={{0,32},{32,0},{1,33},{33,1},{2,34},{34,2},{3,35},{35,3},{4,36},{36... | collective-permute-start | bytes 196616 | tf_op jit(solution)/shard_map/ppermute | solution.py:606
  39.2 5.8 %copy-start.3 = (s32[32]{0:T(128)S(1)}, s32[32]{0:T(128)}, u32[]{:S(2)}) copy-start(s32[32]{0:T(128)} %param.7) | copy-start | bytes 388
  39.2 5.9 %copy-start = (f32[4,3,1024]{2,0,1:T(4,128)S(1)}, f32[4,3,1024]{2,0,1:T(4,128)}, u32[]{:S(2)}) copy-start(f32[4,3,1024]{2,0,1:T(4,128)} %param.8) | copy-start | bytes 147460
  39.2 12.6 %all-to-all-start.2 = ((bf16[16,2,32,128]{3,2,1,0:T(8,128)(2,1)}), bf16[16,2,32,128]{3,2,1,0:T(8,128)(2,1)S(1)}, u32[]{:S(2)}, u32[]{:S(2)}) async-start(bf16[16,2,32,128]{3,2,1,0:T(8,128)(2,1)} %merge_targets.1), calls=%async_computation.2 | async-start | bytes 524288 | tf_op jit(solution)/shard_map/all_to_all | solution.py:632
  45.0 0.7 copy-start.1
  56.4 18.0 %all-to-all-start.3 = ((f32[32,8,128]{2,1,0:T(8,128)}), f32[32,8,128]{2,1,0:T(8,128)S(1)}, u32[]{:S(2)}, u32[]{:S(2)}) async-start(f32[32,8,128]{2,1,0:T(8,128)} %forward_maps.1), calls=%async_computation.3 | async-start | bytes 262144 | tf_op jit(solution)/shard_map/all_to_all | solution.py:642
  75.4 1.3 %collective-permute-start.1 = (f32[96,128]{1,0:T(8,128)S(1)}, f32[96,128]{1,0:T(8,128)S(1)}, u32[]{:S(2)}, u32[]{:S(2)}) collective-permute-start(f32[96,128]{1,0:T(8,128)S(1)} %weigh_gradient.1.a_ref), channel_id=1, source_target_pairs={{0,32},{32,0},{1,33},{33,1},{2,34},{34,2},{3,35},{35,3},{4,36},{36... | collective-permute-start | bytes 147464 | tf_op jit(solution)/shard_map/ppermute | solution.py:663
  77.4 12.1 %all-to-all-start.4 = ((f32[4,96,128]{2,1,0:T(8,128)}), f32[4,96,128]{2,1,0:T(8,128)S(1)}, u32[]{:S(2)}, u32[]{:S(2)}) async-start(f32[4,96,128]{2,1,0:T(8,128)} %sum_cores.1), calls=%async_computation.4 | async-start | bytes 393216 | tf_op jit(solution)/shard_map/all_to_all | solution.py:665

commit v8 on v7

--- a/solution.py
+++ b/solution.py
@@ -138,9 +138,10 @@
             first = (at_ref[1] * halves + part) * share
             block = rows_ref[pl.ds(first, share), half, 0 : n_tgt // share]
             ridge[half][part] = block.reshape(n_tgt, LANES).astype(F32)
+    both = jnp.concatenate([rows_ref[:, part].reshape(total, LANES) for part in range(halves)], axis=1)
+    both = dot_bf16(pick, both, ((1,), (0,)))
     for part in range(halves):
-        data = rows_ref[:, part].reshape(total, LANES)
-        got = dot_bf16(pick, data, ((1,), (0,)))
+        got = both[:, part * LANES : (part + 1) * LANES]
         for chip in range(n_chip):
             low = got[2 * chip * n_tgt : (2 * chip + 1) * n_tgt]
             high = got[(2 * chip + 1) * n_tgt : (2 * chip + 2) * n_tgt]
@@ -338,10 +339,15 @@
 def first_maps(pix_ref, maps_ref, tgt_ref, sup_ref, self_a, self_b, inv_ref, pair_ref):
     def one(b):
         own = pair = 0.0
+        pix = pix_ref[rows_of(b)].reshape(STEP_PIX, LANES)
+        spread_t = jnp.concatenate([tgt_ref[c] for c in range(CHAN)], axis=1)
+        spread_s = jnp.concatenate([sup_ref[c] for c in range(CHAN)], axis=1)
+        all_t = dot_bf16(pix, spread_t, ((1,), (0,)))
+        all_s = dot_bf16(maps_ref[pixels_of(b), :], spread_s, ((1,), (0,)))
         for c in range(CHAN):
-            t = target_map(pix_ref, tgt_ref, c, b)
+            t = as_map(all_t[:, c * LANES : (c + 1) * LANES])
             own = own + t * t
-            pair = pair + t * support_map(maps_ref, sup_ref, c, b)
+            pair = pair + t * as_map(all_s[:, c * LANES : (c + 1) * LANES])
         put(pair_ref, b, pair * (2.0 * BOX_SCALE / CHAN))
         at = pl.ds((b % PER_QUARTER) * STEP_ROWS + 1, STEP_ROWS)
         self_a[at] = jnp.where(lane_block(own.shape) == b // PER_QUARTER, own * (BOX_SCALE / CHAN), self_a[at])

time: 90.8 us -> 90.6 us (level)
  no operation moved by 1% of the time
where the time goes in v8:
time: 90.6 us; the launch traced here: 90 us
  waiting for transfers between devices  26.8 us (30%)
  starting transfers between devices  24.5 us (27%)
  Pallas kernels  20.1 us (22%)
  blocking collectives  16.3 us (18%)
  local copies, waits for them, and re-layouts  1.51 us (2%)
    all_to_all x1, blocking collectives, local(): got = lax.all_to_all(chosen, ('chip', 'zh'), 0, 0, tiled=True)  16.3 us
    all_to_all x1, waiting for transfers between devices, local(): rows = lax.all_to_all(packed, 'xy', 0, 0, tiled=True)  7.72 us
    all_to_all x1, starting transfers between devices, local(): rows = lax.all_to_all(packed, 'xy', 0, 0, tiled=True)  7.49 us
    all_to_all x1, waiting for transfers between devices, local(): shares = lax.all_to_all(summed, 'chip', 0, 0, tiled=True)  6.74 us
    all_to_all x1, starting transfers between devices, local(): arrived = lax.all_to_all(sent, ('zh', 'xy'), 0, 0, tiled=True)  6.7 us
    pallas_call x1, Pallas kernels, local(): call(functools.partial(backward_body, n_sup), [jax.ShapeDtypeStruct((flat...  6.25 us
    all_to_all x1, starting transfers between devices, local(): lax.all_to_all(merged, 'xy', 0, 0, tiled=True).reshape(SIDE, SIDE, LANES)  5.79 us
    all_to_all x1, waiting for transfers between devices, local(): arrived = lax.all_to_all(sent, ('zh', 'xy'), 0, 0, tiled=True)  5.01 us
  transfers between devices with their start and end apart: 6, of which 6 were waited for; matrix products, arithmetic and copies ran while one was open for 0% of the time, Pallas kernels for 10%

profile of v8, /device:TPU:2, one launch (start us, length us, event | category | flops | bytes accessed | tf_op | source)
XLA Modules:
  0.0 90.0 jit_solution(13265897906031170464)
XLA Ops:
  0.6 2.3 %pack_pool.1 = bf16[16,2,64,128]{3,2,1,0:T(8,128)(2,1)} custom-call(bf16[64,3072]{1,0:T(8,128)(2,1)} %pool_ref.1, f32[4,1024]{1,0:T(4,128)} %ridge_ref.3), custom_call_target="tpu_custom_call" | custom-call | tf_op jit(solution)/shard_map/pack_pool/pallas_call | solution.py:575
  2.9 7.5 %all-to-all-start = ((bf16[16,2,64,128]{3,2,1,0:T(8,128)(2,1)}), bf16[16,2,64,128]{3,2,1,0:T(8,128)(2,1)S(1)}, u32[]{:S(2)}, u32[]{:S(2)}) async-start(bf16[16,2,64,128]{3,2,1,0:T(8,128)(2,1)} %pack_pool.1), calls=%async_computation | async-start | bytes 1048576 | tf_op jit(solution)/shard_map/all_to_all | solution.py:592
  10.4 0.7 copy-done.2
  11.3 0.7 pick_rows.1.pick_ref
  12.0 7.7 %all-to-all-done.rows_ref = bf16[16,2,64,128]{3,2,1,0:T(8,128)(2,1)S(1)} async-done(((bf16[16,2,64,128]{3,2,1,0:T(8,128)(2,1)}), bf16[16,2,64,128]{3,2,1,0:T(8,128)(2,1)S(1)}, u32[]{:S(2)}, u32[]{:S(2)}) %all-to-all-start) | async-done | bytes 524320 | tf_op jit(solution)/shard_map/all_to_all | solution.py:592
  19.7 0.9 select_targets.1
  20.7 1.2 %collective-permute-done.other_ref = bf16[4,2,32,128]{3,2,1,0:T(8,128)(2,1)S(1)} collective-permute-done((bf16[4,2,32,128]{3,2,1,0:T(8,128)(2,1)S(1)}, bf16[4,2,32,128]{3,2,1,0:T(8,128)(2,1)S(1)}, u32[]{:S(2)}, u32[]{:S(2)}) %collective-permute-start) | collective-permute-done | bytes 65568 | tf_op jit(solution)/shard_map/ppermute | solution.py:612
  21.9 16.3 %all_to_all.25.parts_ref.got_ref = bf16[8,2,32,128]{3,2,1,0:T(8,128)(2,1)S(1)} all-to-all(bf16[8,2,32,128]{3,2,1,0:T(8,128)(2,1)S(1)} %add_core_targets.1), channel_id=1, replica_groups=mesh['chip'=4,'core'=2,'zh'=2,'xy'=16] {'chip','zh'}, dimensions={0} | all-to-all | bytes 262144 | tf_op jit(solution)/shard_map/all_to_all | solution.py:619
  38.2 0.9 merge_targets.1
  39.1 5.8 %all-to-all-start.2 = ((bf16[16,2,32,128]{3,2,1,0:T(8,128)(2,1)}), bf16[16,2,32,128]{3,2,1,0:T(8,128)(2,1)S(1)}, u32[]{:S(2)}, u32[]{:S(2)}) async-start(bf16[16,2,32,128]{3,2,1,0:T(8,128)(2,1)} %merge_targets.1), calls=%async_computation.2 | async-start | bytes 524288 | tf_op jit(solution)/shard_map/all_to_all | solution.py:638
  45.0 0.6 copy-done.1
  45.6 1.2 %support_maps.1 = (bf16[1024,128]{1,0:T(8,128)(2,1)S(1)}, f32[128,128]{1,0:T(8,128)S(1)}, f32[128,128]{1,0:T(8,128)S(1)}, f32[8,128]{1,0:T(8,128)S(1)}) custom-call(f32[3,4,1024]{2,1,0:T(4,128)S(1)} %bitcast.11, f32[4,1024]{1,0:T(4,128)S(1)} %copy-done.1, s32[32,1]{1,0:T(8,128)S(1)} %copy.10.labels_ref, bf16[8,2,32,128]{3,2,1,0:T(8,128)(2,1)S(1)} %all_to_all.25.parts_ref.got_ref), custom_call_target="tpu_custom_call" | custom-call | flops 100000000 | bytes 1048576 | tf_op jit(solution)/shard_map/support_maps/pallas_call | solution.py:622
  46.8 4.9 %all-to-all-done.2 = bf16[16,2,32,128]{3,2,1,0:T(8,128)(2,1)S(1)} async-done(((bf16[16,2,32,128]{3,2,1,0:T(8,128)(2,1)}), bf16[16,2,32,128]{3,2,1,0:T(8,128)(2,1)S(1)}, u32[]{:S(2)}, u32[]{:S(2)}) %all-to-all-start.2) | async-done | bytes 262176 | tf_op jit(solution)/shard_map/all_to_all | solution.py:638
  51.7 4.5 %forward_maps.1 = f32[32,8,128]{2,1,0:T(8,128)} custom-call(bf16[32,32,128]{2,1,0:T(8,128)(2,1)S(1)} %bitcast.9, bf16[1024,128]{1,0:T(8,128)(2,1)S(1)} %get-tuple-element.12.maps_ref, f32[128,128]{1,0:T(8,128)S(1)} %get-tuple-element.13.gram_ref), custom_call_target="tpu_custom_call" | custom-call | flops 100000000 | bytes 1048576 | tf_op jit(solution)/shard_map/forward_maps/pallas_call | solution.py:639
  56.2 6.7 %all-to-all-start.3 = ((f32[32,8,128]{2,1,0:T(8,128)}), f32[32,8,128]{2,1,0:T(8,128)S(1)}, u32[]{:S(2)}, u32[]{:S(2)}) async-start(f32[32,8,128]{2,1,0:T(8,128)} %forward_maps.1), calls=%async_computation.3 | async-start | bytes 262144 | tf_op jit(solution)/shard_map/all_to_all | solution.py:648
  62.9 6.3 %backward_maps.1 = (bf16[4096,128]{1,0:T(8,128)(2,1)S(1)}, bf16[4096,128]{1,0:T(8,128)(2,1)S(1)}) custom-call(bf16[32,32,128]{2,1,0:T(8,128)(2,1)S(1)} %bitcast.10, bf16[1024,128]{1,0:T(8,128)(2,1)S(1)} %get-tuple-element.12.maps_ref), custom_call_target="tpu_custom_call" | custom-call | flops 10000000000 | bytes 1048576 | tf_op jit(solution)/shard_map/backward_maps/pallas_call | solution.py:651
  69.2 5.0 %all-to-all-done.3.got_ref = f32[32,8,128]{2,1,0:T(8,128)S(1)} async-done(((f32[32,8,128]{2,1,0:T(8,128)}), f32[32,8,128]{2,1,0:T(8,128)S(1)}, u32[]{:S(2)}, u32[]{:S(2)}) %all-to-all-start.3) | async-done | bytes 131104 | tf_op jit(solution)/shard_map/all_to_all | solution.py:648
  74.2 1.0 %weigh_gradient.1.a_ref = f32[96,128]{1,0:T(8,128)S(1)} custom-call(f32[32,8,128]{2,1,0:T(8,128)S(1)} %all-to-all-done.3.got_ref, bf16[4096,128]{1,0:T(8,128)(2,1)S(1)} %get-tuple-element.15.high_ref, bf16[4096,128]{1,0:T(8,128)(2,1)S(1)} %get-tuple-element.16.low_ref, f32[8,128]{1,0:T(8,128)S(1)} %get-tuple-element.17.picked_ref, f32[3,4,1024]{2,1,0:T(4,128)S(1)} %bitcast.12), custom_call_target="tpu_custom_call" | custom-call | bytes 1048576 | tf_op jit(solution)/shard_map/weigh_gradient/pallas_call | solution.py:662
  75.3 1.2 %collective-permute-done.1.b_ref = f32[96,128]{1,0:T(8,128)S(1)} collective-permute-done((f32[96,128]{1,0:T(8,128)S(1)}, f32[96,128]{1,0:T(8,128)S(1)}, u32[]{:S(2)}, u32[]{:S(2)}) %collective-permute-start.1) | collective-permute-done | bytes 49184 | tf_op jit(solution)/shard_map/ppermute | solution.py:669
  76.6 0.7 sum_cores.1
  77.2 4.3 %all-to-all-start.4 = ((f32[4,96,128]{2,1,0:T(8,128)}), f32[4,96,128]{2,1,0:T(8,128)S(1)}, u32[]{:S(2)}, u32[]{:S(2)}) async-start(f32[4,96,128]{2,1,0:T(8,128)} %sum_cores.1), calls=%async_computation.4 | async-start | bytes 393216 | tf_op jit(solution)/shard_map/all_to_all | solution.py:671
  81.5 1.1 %residual.1 = f32[32,32]{1,0:T(8,128)} custom-call(s32[1]{0:T(128)} %bitcast.start_ref, f32[32,8,128]{2,1,0:T(8,128)S(1)} %all-to-all-done.3.got_ref, f32[128,128]{1,0:T(8,128)S(1)} %get-tuple-element.14.mine_ref, s32[32,1]{1,0:T(8,128)S(1)} %copy.10.labels_ref), custom_call_target="tpu_custom_call" | custom-call | flops 10000000 | bytes 1048576 | tf_op jit(solution)/shard_map/residual/pallas_call | solution.py:672
  82.6 6.7 %all-to-all-done.4.parts_ref = f32[4,96,128]{2,1,0:T(8,128)S(1)} async-done(((f32[4,96,128]{2,1,0:T(8,128)}), f32[4,96,128]{2,1,0:T(8,128)S(1)}, u32[]{:S(2)}, u32[]{:S(2)}) %all-to-all-start.4) | async-done | bytes 196640 | tf_op jit(solution)/shard_map/all_to_all | solution.py:671
  89.4 0.7 sum_chips.1
  (12 shorter events, 0.5 us)
Async XLA Ops:
  2.9 16.8 %all-to-all-start = ((bf16[16,2,64,128]{3,2,1,0:T(8,128)(2,1)}), bf16[16,2,64,128]{3,2,1,0:T(8,128)(2,1)S(1)}, u32[]{:S(2)}, u32[]{:S(2)}) async-start(bf16[16,2,64,128]{3,2,1,0:T(8,128)(2,1)} %pack_pool.1), calls=%async_computation | async-start | bytes 1048576 | tf_op jit(solution)/shard_map/all_to_all | solution.py:592
  10.4 0.7 copy-start.2
  20.6 1.3 %collective-permute-start = (bf16[4,2,32,128]{3,2,1,0:T(8,128)(2,1)S(1)}, bf16[4,2,32,128]{3,2,1,0:T(8,128)(2,1)S(1)}, u32[]{:S(2)}, u32[]{:S(2)}) collective-permute-start(bf16[4,2,32,128]{3,2,1,0:T(8,128)(2,1)S(1)} %get-tuple-element.11), channel_id=1, source_target_pairs={{0,32},{32,0},{1,33},{33,1},{2,34},{34,2},{3,35},{35,3},{4,36},{36... | collective-permute-start | bytes 196616 | tf_op jit(solution)/shard_map/ppermute | solution.py:612
  39.1 5.8 %copy-start.3 = (s32[32]{0:T(128)S(1)}, s32[32]{0:T(128)}, u32[]{:S(2)}) copy-start(s32[32]{0:T(128)} %param.7) | copy-start | bytes 388
  39.1 5.9 %copy-start = (f32[4,3,1024]{2,0,1:T(4,128)S(1)}, f32[4,3,1024]{2,0,1:T(4,128)}, u32[]{:S(2)}) copy-start(f32[4,3,1024]{2,0,1:T(4,128)} %param.8) | copy-start | bytes 147460
  39.1 12.6 %all-to-all-start.2 = ((bf16[16,2,32,128]{3,2,1,0:T(8,128)(2,1)}), bf16[16,2,32,128]{3,2,1,0:T(8,128)(2,1)S(1)}, u32[]{:S(2)}, u32[]{:S(2)}) async-start(bf16[16,2,32,128]{3,2,1,0:T(8,128)(2,1)} %merge_targets.1), calls=%async_computation.2 | async-start | bytes 524288 | tf_op jit(solution)/shard_map/all_to_all | solution.py:638
  44.9 0.7 copy-start.1
  56.2 18.0 %all-to-all-start.3 = ((f32[32,8,128]{2,1,0:T(8,128)}), f32[32,8,128]{2,1,0:T(8,128)S(1)}, u32[]{:S(2)}, u32[]{:S(2)}) async-start(f32[32,8,128]{2,1,0:T(8,128)} %forward_maps.1), calls=%async_computation.3 | async-start | bytes 262144 | tf_op jit(solution)/shard_map/all_to_all | solution.py:648
  75.2 1.3 %collective-permute-start.1 = (f32[96,128]{1,0:T(8,128)S(1)}, f32[96,128]{1,0:T(8,128)S(1)}, u32[]{:S(2)}, u32[]{:S(2)}) collective-permute-start(f32[96,128]{1,0:T(8,128)S(1)} %weigh_gradient.1.a_ref), channel_id=1, source_target_pairs={{0,32},{32,0},{1,33},{33,1},{2,34},{34,2},{3,35},{35,3},{4,36},{36... | collective-permute-start | bytes 147464 | tf_op jit(solution)/shard_map/ppermute | solution.py:669
  77.2 12.1 %all-to-all-start.4 = ((f32[4,96,128]{2,1,0:T(8,128)}), f32[4,96,128]{2,1,0:T(8,128)S(1)}, u32[]{:S(2)}, u32[]{:S(2)}) async-start(f32[4,96,128]{2,1,0:T(8,128)} %sum_cores.1), calls=%async_computation.4 | async-start | bytes 393216 | tf_op jit(solution)/shard_map/all_to_all | solution.py:671

commit v9 on v8

--- a/solution.py
+++ b/solution.py
@@ -249,7 +249,7 @@
     return x + above + below
 
 
-def side_body(sup_ref, ridge_ref, labels_ref, got_ref, maps_ref, mine_ref, gram_ref, picked_ref, parts_ref):
+def side_body(sup_ref, ridge_ref, labels_ref, got_ref, maps_ref, mine_ref, gram_ref, picked_ref, tgt_ref, spread_ref, parts_ref):
     n_sup = sup_ref.shape[1]
     n_tgt = labels_ref.shape[0]
     n_parts, halves, n_rows, _ = got_ref.shape
@@ -298,6 +298,7 @@
     lane = lax.broadcasted_iota(jnp.int32, (LANES, LANES), 1)
     same = jnp.where(row == lane, 1.0, 0.0).astype(BF16)
     maps_ref[...] = dot_bf16(parts_ref[...].astype(BF16), same, ((0,), (0,))).astype(BF16)
+    fill_spreads(n_sup, n_tgt, tgt_ref, spread_ref)
 
 
 def fill_spreads(n_sup, n_tgt, tgt_ref, sup_ref):
@@ -375,11 +376,9 @@
 
 
 def forward_body(
-    n_sup, pix_ref, maps_ref, gram_ref, out_ref, tgt_ref, sup_ref, self_a, self_b, inv_ref, pair_a, pair_b, acc_ref
+    n_sup, pix_ref, maps_ref, tgt_ref, sup_ref, gram_ref, out_ref, self_a, self_b, inv_ref, pair_a, pair_b, acc_ref
 ):
-    n_tgt = LANES // n_sup
     clear_halo(pair_a, pair_b)
-    fill_spreads(n_sup, n_tgt, tgt_ref, sup_ref)
     first_maps(pix_ref, maps_ref, tgt_ref, sup_ref, self_a, self_b, inv_ref, pair_a)
     acc_ref[...] = jnp.zeros_like(acc_ref)
     for depth in range(LAYERS):
@@ -404,13 +403,12 @@
 
 
 def backward_body(
-    n_sup,
     pix_ref,
     maps_ref,
+    tgt_ref,
+    sup_ref,
     high_ref,
     low_ref,
-    tgt_ref,
-    sup_ref,
     self_a,
     self_b,
     inv_ref,
@@ -421,9 +419,7 @@
     dcov_ref,
     dvar_ref,
 ):
-    n_tgt = LANES // n_sup
     clear_halo(pair_a, pair_b, grad_a, grad_b)
-    fill_spreads(n_sup, n_tgt, tgt_ref, sup_ref)
     first_maps(pix_ref, maps_ref, tgt_ref, sup_ref, self_a, self_b, inv_ref, pair_a)
     last = LAYERS - 1
     for depth in range(LAYERS):
@@ -545,10 +541,8 @@
     return pltpu.VMEM((rows, TILES, SUB, LANES), F32)
 
 
-def map_scratch(n_maps):
+def map_scratch():
     return [
-        pltpu.VMEM((CHAN, LANES, LANES), BF16),
-        pltpu.VMEM((n_maps, LANES, LANES), BF16),
         maps(QUARTER_ROWS + 2),
         maps(QUARTER_ROWS + 2),
         pltpu.VMEM((LAYERS, PER_QUARTER, STEP_ROWS, TILES, SUB, LANES), F32),
@@ -619,13 +613,15 @@
     got = lax.all_to_all(chosen, ("chip", "zh"), 0, 0, tiled=True)
     by_channel = jnp.swapaxes(support, 0, 1)
     n_maps = CHAN + 2 * LAYERS - 1
-    s_maps, mine, gram, picked = call(
+    s_maps, mine, gram, picked, spread_t, spread_s = call(
         side_body,
         [
             jax.ShapeDtypeStruct((PIX, LANES), BF16),
             jax.ShapeDtypeStruct((n_sup * n_sup_dev, LANES), F32),
             jax.ShapeDtypeStruct((n_sup * n_sup_dev, n_sup * n_sup_dev), F32),
             jax.ShapeDtypeStruct((SUB, LANES), F32),
+            jax.ShapeDtypeStruct((CHAN, LANES, LANES), BF16),
+            jax.ShapeDtypeStruct((n_maps, LANES, LANES), BF16),
         ],
         4,
         scratch=[pltpu.VMEM((LANES, PIX), F32)],
@@ -639,24 +635,24 @@
     sent = call(
         functools.partial(forward_body, n_sup),
         jax.ShapeDtypeStruct((n_sup_dev, SUB, LANES), F32),
-        3,
-        scratch=[*map_scratch(CHAN + LAYERS), pltpu.VMEM((SUB, LANES), F32)],
+        5,
+        scratch=[*map_scratch(), pltpu.VMEM((SUB, LANES), F32)],
         flops=10**8,
         name="forward_maps",
         vmem=12,
-    )(pixels, s_maps, gram)
+    )(pixels, s_maps, spread_t, spread_s, gram)
     arrived = lax.all_to_all(sent, ("zh", "xy"), 0, 0, tiled=True)
     layer_maps = pltpu.VMEM((LAYERS - 1, SIDE, TILES, SUB, LANES), F32)
     flat = (CHAN + 1) * PIX
     high, low = call(
-        functools.partial(backward_body, n_sup),
+        backward_body,
         [jax.ShapeDtypeStruct((flat, LANES), BF16)] * 2,
-        2,
-        scratch=[*map_scratch(n_maps), maps(SIDE + 2), maps(SIDE + 2), layer_maps, layer_maps],
+        4,
+        scratch=[*map_scratch(), maps(SIDE + 2), maps(SIDE + 2), layer_maps, layer_maps],
         flops=10**10,
         name="backward_maps",
         vmem=20,
-    )(pixels, s_maps)
+    )(pixels, s_maps, spread_t, spread_s)
     loss_scale = float(PIX) / n_tgt
     wide = n_sup * CHAN * PIX // LANES
     grad = call(

time: 90.6 us -> 90.6 us (level)
  no operation moved by 1% of the time
where the time goes in v9:
time: 90.6 us; the launch traced here: 90 us
  waiting for transfers between devices  27 us (30%)
  starting transfers between devices  24.5 us (27%)
  Pallas kernels  19.9 us (22%)
  blocking collectives  16.3 us (18%)
  local copies, waits for them, and re-layouts  1.51 us (2%)
    all_to_all x1, blocking collectives, local(): got = lax.all_to_all(chosen, ('chip', 'zh'), 0, 0, tiled=True)  16.3 us
    all_to_all x1, waiting for transfers between devices, local(): rows = lax.all_to_all(packed, 'xy', 0, 0, tiled=True)  7.72 us
    all_to_all x1, starting transfers between devices, local(): rows = lax.all_to_all(packed, 'xy', 0, 0, tiled=True)  7.49 us
    all_to_all x1, waiting for transfers between devices, local(): shares = lax.all_to_all(summed, 'chip', 0, 0, tiled=True)  6.74 us
    all_to_all x1, starting transfers between devices, local(): arrived = lax.all_to_all(sent, ('zh', 'xy'), 0, 0, tiled=True)  6.69 us
    pallas_call x1, Pallas kernels, local(): call(backward_body, [jax.ShapeDtypeStruct((flat, LANES), BF16)] * 2, 4, s...  6.09 us
    all_to_all x1, starting transfers between devices, local(): lax.all_to_all(merged, 'xy', 0, 0, tiled=True).reshape(SIDE, SIDE, LANES)  5.79 us
    all_to_all x1, waiting for transfers between devices, local(): arrived = lax.all_to_all(sent, ('zh', 'xy'), 0, 0, tiled=True)  5.17 us
  transfers between devices with their start and end apart: 6, of which 6 were waited for; matrix products, arithmetic and copies ran while one was open for 0% of the time, Pallas kernels for 10%

profile of v9, /device:TPU:2, one launch (start us, length us, event | category | flops | bytes accessed | tf_op | source)
XLA Modules:
  0.0 90.0 jit_solution(15253119092403137021)
XLA Ops:
  0.6 2.3 %pack_pool.1 = bf16[16,2,64,128]{3,2,1,0:T(8,128)(2,1)} custom-call(bf16[64,3072]{1,0:T(8,128)(2,1)} %pool_ref.1, f32[4,1024]{1,0:T(4,128)} %ridge_ref.3), custom_call_target="tpu_custom_call" | custom-call | tf_op jit(solution)/shard_map/pack_pool/pallas_call | solution.py:569
  2.9 7.5 %all-to-all-start = ((bf16[16,2,64,128]{3,2,1,0:T(8,128)(2,1)}), bf16[16,2,64,128]{3,2,1,0:T(8,128)(2,1)S(1)}, u32[]{:S(2)}, u32[]{:S(2)}) async-start(bf16[16,2,64,128]{3,2,1,0:T(8,128)(2,1)} %pack_pool.1), calls=%async_computation | async-start | bytes 1048576 | tf_op jit(solution)/shard_map/all_to_all | solution.py:586
  10.4 0.7 copy-done.2
  11.3 0.7 pick_rows.1.pick_ref
  12.0 7.7 %all-to-all-done.rows_ref = bf16[16,2,64,128]{3,2,1,0:T(8,128)(2,1)S(1)} async-done(((bf16[16,2,64,128]{3,2,1,0:T(8,128)(2,1)}), bf16[16,2,64,128]{3,2,1,0:T(8,128)(2,1)S(1)}, u32[]{:S(2)}, u32[]{:S(2)}) %all-to-all-start) | async-done | bytes 524320 | tf_op jit(solution)/shard_map/all_to_all | solution.py:586
  19.7 0.9 select_targets.1
  20.7 1.2 %collective-permute-done.other_ref = bf16[4,2,32,128]{3,2,1,0:T(8,128)(2,1)S(1)} collective-permute-done((bf16[4,2,32,128]{3,2,1,0:T(8,128)(2,1)S(1)}, bf16[4,2,32,128]{3,2,1,0:T(8,128)(2,1)S(1)}, u32[]{:S(2)}, u32[]{:S(2)}) %collective-permute-start) | collective-permute-done | bytes 65568 | tf_op jit(solution)/shard_map/ppermute | solution.py:606
  21.9 16.3 %all_to_all.25.parts_ref.got_ref = bf16[8,2,32,128]{3,2,1,0:T(8,128)(2,1)S(1)} all-to-all(bf16[8,2,32,128]{3,2,1,0:T(8,128)(2,1)S(1)} %add_core_targets.1), channel_id=1, replica_groups=mesh['chip'=4,'core'=2,'zh'=2,'xy'=16] {'chip','zh'}, dimensions={0} | all-to-all | bytes 262144 | tf_op jit(solution)/shard_map/all_to_all | solution.py:613
  38.2 0.9 merge_targets.1
  39.1 5.8 %all-to-all-start.2 = ((bf16[16,2,32,128]{3,2,1,0:T(8,128)(2,1)}), bf16[16,2,32,128]{3,2,1,0:T(8,128)(2,1)S(1)}, u32[]{:S(2)}, u32[]{:S(2)}) async-start(bf16[16,2,32,128]{3,2,1,0:T(8,128)(2,1)} %merge_targets.1), calls=%async_computation.2 | async-start | bytes 524288 | tf_op jit(solution)/shard_map/all_to_all | solution.py:634
  45.0 0.6 copy-done.1
  45.6 1.2 %support_maps.1 = (bf16[1024,128]{1,0:T(8,128)(2,1)S(1)}, f32[128,128]{1,0:T(8,128)S(1)}, f32[128,128]{1,0:T(8,128)S(1)}, f32[8,128]{1,0:T(8,128)S(1)}, bf16[3,1...) custom-call(f32[3,4,1024]{2,1,0:T(4,128)S(1)} %bitcast.11, f32[4,1024]{1,0:T(4,128)S(1)} %copy-done.1, ...), custom_call_target="tpu_custom_call" | custom-call | flops 100000000 | bytes 1048576 | tf_op jit(solution)/shard_map/support_maps/pallas_call | solution.py:616
  46.8 4.9 %all-to-all-done.2 = bf16[16,2,32,128]{3,2,1,0:T(8,128)(2,1)S(1)} async-done(((bf16[16,2,32,128]{3,2,1,0:T(8,128)(2,1)}), bf16[16,2,32,128]{3,2,1,0:T(8,128)(2,1)S(1)}, u32[]{:S(2)}, u32[]{:S(2)}) %all-to-all-start.2) | async-done | bytes 262176 | tf_op jit(solution)/shard_map/all_to_all | solution.py:634
  51.7 4.4 %forward_maps.1 = f32[32,8,128]{2,1,0:T(8,128)} custom-call(bf16[32,32,128]{2,1,0:T(8,128)(2,1)S(1)} %bitcast.9, bf16[1024,128]{1,0:T(8,128)(2,1)S(1)} %get-tuple-element.14.maps_ref, bf16[3,128,128]{2,1,0:T(8,128)(2,1)S(1)} %get-tuple-element.15.tgt_ref, bf16[10,128,128]{2,1,0:T(8,128)(2,1)S(1)} %get-tuple-element.16.sup_ref, ...), custom_call_target="tpu_custom_call" | custom-call | flops 100000000 | bytes 1048576 | tf_op jit(solution)/shard_map/forward_maps/pallas_call | solution.py:635
  56.2 6.7 %all-to-all-start.3 = ((f32[32,8,128]{2,1,0:T(8,128)}), f32[32,8,128]{2,1,0:T(8,128)S(1)}, u32[]{:S(2)}, u32[]{:S(2)}) async-start(f32[32,8,128]{2,1,0:T(8,128)} %forward_maps.1), calls=%async_computation.3 | async-start | bytes 262144 | tf_op jit(solution)/shard_map/all_to_all | solution.py:644
  62.9 6.1 %backward_maps.1 = (bf16[4096,128]{1,0:T(8,128)(2,1)S(1)}, bf16[4096,128]{1,0:T(8,128)(2,1)S(1)}) custom-call(bf16[32,32,128]{2,1,0:T(8,128)(2,1)S(1)} %bitcast.10, bf16[1024,128]{1,0:T(8,128)(2,1)S(1)} %get-tuple-element.14.maps_ref, bf16[3,128,128]{2,1,0:T(8,128)(2,1)S(1)} %get-tuple-element.15.tgt_ref, bf16[10,128,128]{2,1,0:T(8,128)(2,1)S(1)} %get-tuple-element.16.sup_ref), custom_call_target="tpu_custom_call" | custom-call | flops 10000000000 | bytes 1048576 | tf_op jit(solution)/shard_map/backward_maps/pallas_call | solution.py:647
  69.0 5.2 %all-to-all-done.3.got_ref = f32[32,8,128]{2,1,0:T(8,128)S(1)} async-done(((f32[32,8,128]{2,1,0:T(8,128)}), f32[32,8,128]{2,1,0:T(8,128)S(1)}, u32[]{:S(2)}, u32[]{:S(2)}) %all-to-all-start.3) | async-done | bytes 131104 | tf_op jit(solution)/shard_map/all_to_all | solution.py:644
  74.1 1.0 %weigh_gradient.1.a_ref = f32[96,128]{1,0:T(8,128)S(1)} custom-call(f32[32,8,128]{2,1,0:T(8,128)S(1)} %all-to-all-done.3.got_ref, bf16[4096,128]{1,0:T(8,128)(2,1)S(1)} %get-tuple-element.19.high_ref, bf16[4096,128]{1,0:T(8,128)(2,1)S(1)} %get-tuple-element.20.low_ref, f32[8,128]{1,0:T(8,128)S(1)} %get-tuple-element.21.picked_ref, f32[3,4,1024]{2,1,0:T(4,128)S(1)} %bitcast.12), custom_call_target="tpu_custom_call" | custom-call | bytes 1048576 | tf_op jit(solution)/shard_map/weigh_gradient/pallas_call | solution.py:658
  75.3 1.2 %collective-permute-done.1.b_ref = f32[96,128]{1,0:T(8,128)S(1)} collective-permute-done((f32[96,128]{1,0:T(8,128)S(1)}, f32[96,128]{1,0:T(8,128)S(1)}, u32[]{:S(2)}, u32[]{:S(2)}) %collective-permute-start.1) | collective-permute-done | bytes 49184 | tf_op jit(solution)/shard_map/ppermute | solution.py:665
  76.5 0.7 sum_cores.1
  77.2 4.3 %all-to-all-start.4 = ((f32[4,96,128]{2,1,0:T(8,128)}), f32[4,96,128]{2,1,0:T(8,128)S(1)}, u32[]{:S(2)}, u32[]{:S(2)}) async-start(f32[4,96,128]{2,1,0:T(8,128)} %sum_cores.1), calls=%async_computation.4 | async-start | bytes 393216 | tf_op jit(solution)/shard_map/all_to_all | solution.py:667
  81.5 1.1 %residual.1 = f32[32,32]{1,0:T(8,128)} custom-call(s32[1]{0:T(128)} %bitcast.start_ref, f32[32,8,128]{2,1,0:T(8,128)S(1)} %all-to-all-done.3.got_ref, f32[128,128]{1,0:T(8,128)S(1)} %get-tuple-element.18.mine_ref, s32[32,1]{1,0:T(8,128)S(1)} %copy.10.labels_ref), custom_call_target="tpu_custom_call" | custom-call | flops 10000000 | bytes 1048576 | tf_op jit(solution)/shard_map/residual/pallas_call | solution.py:668
  82.6 6.7 %all-to-all-done.4.parts_ref = f32[4,96,128]{2,1,0:T(8,128)S(1)} async-done(((f32[4,96,128]{2,1,0:T(8,128)}), f32[4,96,128]{2,1,0:T(8,128)S(1)}, u32[]{:S(2)}, u32[]{:S(2)}) %all-to-all-start.4) | async-done | bytes 196640 | tf_op jit(solution)/shard_map/all_to_all | solution.py:667
  89.3 0.7 sum_chips.1
  (12 shorter events, 0.5 us)
Async XLA Ops:
  2.9 16.8 %all-to-all-start = ((bf16[16,2,64,128]{3,2,1,0:T(8,128)(2,1)}), bf16[16,2,64,128]{3,2,1,0:T(8,128)(2,1)S(1)}, u32[]{:S(2)}, u32[]{:S(2)}) async-start(bf16[16,2,64,128]{3,2,1,0:T(8,128)(2,1)} %pack_pool.1), calls=%async_computation | async-start | bytes 1048576 | tf_op jit(solution)/shard_map/all_to_all | solution.py:586
  10.4 0.7 copy-start.2
  20.6 1.3 %collective-permute-start = (bf16[4,2,32,128]{3,2,1,0:T(8,128)(2,1)S(1)}, bf16[4,2,32,128]{3,2,1,0:T(8,128)(2,1)S(1)}, u32[]{:S(2)}, u32[]{:S(2)}) collective-permute-start(bf16[4,2,32,128]{3,2,1,0:T(8,128)(2,1)S(1)} %get-tuple-element.13), channel_id=1, source_target_pairs={{0,32},{32,0},{1,33},{33,1},{2,34},{34,2},{3,35},{35,3},{4,36},{36... | collective-permute-start | bytes 196616 | tf_op jit(solution)/shard_map/ppermute | solution.py:606
  39.1 5.8 %copy-start.3 = (s32[32]{0:T(128)S(1)}, s32[32]{0:T(128)}, u32[]{:S(2)}) copy-start(s32[32]{0:T(128)} %param.7) | copy-start | bytes 388
  39.1 5.9 %copy-start = (f32[4,3,1024]{2,0,1:T(4,128)S(1)}, f32[4,3,1024]{2,0,1:T(4,128)}, u32[]{:S(2)}) copy-start(f32[4,3,1024]{2,0,1:T(4,128)} %param.8) | copy-start | bytes 147460
  39.1 12.6 %all-to-all-start.2 = ((bf16[16,2,32,128]{3,2,1,0:T(8,128)(2,1)}), bf16[16,2,32,128]{3,2,1,0:T(8,128)(2,1)S(1)}, u32[]{:S(2)}, u32[]{:S(2)}) async-start(bf16[16,2,32,128]{3,2,1,0:T(8,128)(2,1)} %merge_targets.1), calls=%async_computation.2 | async-start | bytes 524288 | tf_op jit(solution)/shard_map/all_to_all | solution.py:634
  44.9 0.7 copy-start.1
  56.2 18.0 %all-to-all-start.3 = ((f32[32,8,128]{2,1,0:T(8,128)}), f32[32,8,128]{2,1,0:T(8,128)S(1)}, u32[]{:S(2)}, u32[]{:S(2)}) async-start(f32[32,8,128]{2,1,0:T(8,128)} %forward_maps.1), calls=%async_computation.3 | async-start | bytes 262144 | tf_op jit(solution)/shard_map/all_to_all | solution.py:644
  75.2 1.3 %collective-permute-start.1 = (f32[96,128]{1,0:T(8,128)S(1)}, f32[96,128]{1,0:T(8,128)S(1)}, u32[]{:S(2)}, u32[]{:S(2)}) collective-permute-start(f32[96,128]{1,0:T(8,128)S(1)} %weigh_gradient.1.a_ref), channel_id=1, source_target_pairs={{0,32},{32,0},{1,33},{33,1},{2,34},{34,2},{3,35},{35,3},{4,36},{36... | collective-permute-start | bytes 147464 | tf_op jit(solution)/shard_map/ppermute | solution.py:665
  77.2 12.1 %all-to-all-start.4 = ((f32[4,96,128]{2,1,0:T(8,128)}), f32[4,96,128]{2,1,0:T(8,128)S(1)}, u32[]{:S(2)}, u32[]{:S(2)}) async-start(f32[4,96,128]{2,1,0:T(8,128)} %sum_cores.1), calls=%async_computation.4 | async-start | bytes 393216 | tf_op jit(solution)/shard_map/all_to_all | solution.py:667
